TPU v7x, 256 devices: a whole 4x4x8 slice. The times are simulated.
256 devices in a mesh: rows: 32 (over x, z_lo, core), marg: 8 (over y, z_hi).
Axes of the slice: x: 4, y: 4, z: 8 (z_hi: 2, z_lo: 4; z = z_hi * 4 + z_lo), core: 2. Of those that a mesh axis runs over, the one named last changes fastest.
Arguments:
- logits: float32 [4096, 2048], P('rows', 'marg'), may hold values from -12 to 320
- first_moment: float32 [4096, 2048], P('rows', 'marg'), may hold values from -3 to 3
- second_moment: float32 [4096, 2048], P('rows', 'marg'), may hold values from 0.002 to 0.016
- targets: float32 [128, 32768], P('marg'), may hold values from 0 to 2
- triples: int32 [128, 3], P('marg'), may hold values from 0 to 63, as said below
Outputs:
- new_logits: float32 [4096, 2048], P('rows', 'marg')
- new_first: float32 [4096, 2048], P('rows', 'marg')
- new_second: float32 [4096, 2048], P('rows', 'marg')
Inputs may be any that keep to these rules, and one draw needn't show every extreme that they name: `triples`: the three attributes of a marginal are different.
All inputs are finite; a program needn't handle non-finite values.
Results may differ from a plain program's by a relative error of at most 0.0099.
Values may be sent and summed in bfloat16 or wider, within the bound.
No kernel may reach another device: no remote copies, remote signals or barrier semaphores. Data moves between devices by JAX's collectives and lax.ppermute only.
A program may use at most 64 MiB of HBM per device.

v0:
```python
import jax
import jax.numpy as jnp
from jax import lax
from jax.sharding import PartitionSpec as P

V = 32
BLOCK = 4
ADAM_STEP = 4


def relax(logits):
    shaped = logits.reshape(logits.shape[0], -1, V)
    top = jnp.max(shaped, axis=2, keepdims=True)
    expo = jnp.exp(shaped - top)
    return (expo / jnp.sum(expo, axis=2, keepdims=True)).reshape(logits.shape)


def pick(full, index):
    return lax.dynamic_slice_in_dim(full, index * V, V, 1)


def pairing(left, right):
    both = left.astype(jnp.float32)[:, :, None] * right.astype(jnp.float32)[:, None, :]
    return both.reshape(left.shape[0], V * V).astype(jnp.bfloat16)


def add_cols(total, index, term):
    start = index * V
    current = lax.dynamic_slice_in_dim(total, start, V, 1)
    return lax.dynamic_update_slice_in_dim(total, current + term, start, 1)


def answer_one(full, triple):
    pairs = pairing(pick(full, triple[0]), pick(full, triple[1]))
    total = lax.dot_general(
        pairs, pick(full, triple[2]), (((0,), (0,)), ((), ())), preferred_element_type=jnp.float32
    )
    return total.reshape(V * V * V)


def backward_one(full, triple, resid_row):
    first_cols = pick(full, triple[0])
    second_cols = pick(full, triple[1])
    third_cols = pick(full, triple[2])
    pairs = pairing(first_cols, second_cols)
    table = resid_row.reshape(V * V, V)
    third_grad = jnp.dot(pairs, table, preferred_element_type=jnp.float32)
    cross = lax.dot_general(
        third_cols, table, (((1,), (1,)), ((), ())), preferred_element_type=jnp.float32
    )
    cross = cross.reshape(-1, V, V)
    first_grad = jnp.einsum("rij,rj->ri", cross, second_cols.astype(jnp.float32))
    second_grad = jnp.einsum("rij,ri->rj", cross, first_cols.astype(jnp.float32))
    return (first_grad, second_grad, third_grad)


def shards(logits, first_moment, second_moment, targets, triples):
    row_count, local_cols = logits.shape
    marg_local, cell_count = targets.shape
    block_count = marg_local // BLOCK
    probs = relax(logits)
    probs_low = probs.astype(jnp.bfloat16)
    full = lax.all_gather(probs_low, "marg", axis=1, tiled=True)
    scale = cell_count / (row_count * lax.axis_size("rows"))
    grouped = triples.reshape(block_count, BLOCK, 3)

    def answer_block(carry, group):
        return (carry, jax.vmap(lambda triple: answer_one(full, triple))(group))

    unused, partial_value = lax.scan(answer_block, 0.0, grouped)
    partial_value = partial_value.reshape(marg_local, cell_count)
    totals = lax.psum(partial_value, "rows")
    resid = (scale * totals - targets).astype(jnp.bfloat16)
    resid_groups = resid.reshape(block_count, BLOCK, cell_count)

    def backward_block(total, inputs):
        group, resid_group = inputs
        grads = jax.vmap(lambda triple, resid_row: backward_one(full, triple, resid_row))(
            group, resid_group
        )
        for member in range(BLOCK):
            for which in range(3):
                total = add_cols(total, group[member, which], grads[which][member])
        return (total, 0.0)

    start_grad = jnp.zeros(full.shape, jnp.float32)
    row_grad, unused2 = lax.scan(backward_block, start_grad, (grouped, resid_groups))
    own_grad = lax.psum_scatter(row_grad, "marg", scatter_dimension=1, tiled=True)
    shaped_p = probs.reshape(row_count, -1, V)
    shaped_h = own_grad.reshape(row_count, -1, V)
    inner = jnp.sum(shaped_p * shaped_h, axis=2, keepdims=True)
    grad = (512.0 * shaped_p * (shaped_h - inner)).reshape(row_count, local_cols)
    new_first = 0.9 * first_moment + 0.1 * grad
    new_second = 0.999 * second_moment + 0.001 * grad * grad
    first_hat = new_first / (1.0 - 0.9**ADAM_STEP)
    second_hat = new_second / (1.0 - 0.999**ADAM_STEP)
    new_logits = logits - 0.5 * first_hat / (jnp.sqrt(second_hat) + 1e-08)
    return (new_logits, new_first, new_second)


def solution(mesh):
    in_specs = (
        P("rows", "marg"),
        P("rows", "marg"),
        P("rows", "marg"),
        P("marg", None),
        P("marg", None),
    )
    out_specs = (P("rows", "marg"), P("rows", "marg"), P("rows", "marg"))
    return jax.shard_map(shards, mesh=mesh, in_specs=in_specs, out_specs=out_specs, check_vma=False)
```

profile of v0, /device:TPU:32, one launch (start us, length us, event | category | flops | bytes accessed | tf_op | source)
XLA Modules:
  0.0 779.0 jit_solution(12299196235790781599)
XLA Ops:
  8.4 48.3 %all_gather.3 = bf16[128,2048]{0,1:T(8,128)(2,1)S(1)} all-gather(bf16[128,256]{0,1:T(8,128)(2,1)S(1)} %fusion.34), channel_id=1, replica_groups=mesh['rows'=32,'marg'=8] {'marg'}, dimensions={1}, use_global_device_ids=true | all-gather | bytes 589824 | tf_op jit(solution)/shard_map/all_gather | solution.py:63
  57.8 112.7 %while.35 = (s32[]{:T(128)}, f32[4,4,32768]{2,1,0:T(4,128)}, s32[4,4,3]{2,1,0:T(4,128)S(1)}, bf16[128,2048]{1,0:T(8,128)(2,1)}, s32[]{:T(128)}, /*index=5*/s32[]...) while((s32[]{:T(128)}, f32[4,4,32768]{2,1,0:T(4,128)}, s32[4,4,3]{2,1,0:T(4,128)S(1)}, ...), condition=%wide.region_3.4_spmd, body=%wide.region_2.3_spmd.sunk | while | flops 34603064 | bytes 5301630 | solution.py:70
  58.0 8.4 %while.40 = (s32[]{:T(128)}, bf16[128,2048]{1,0:T(8,128)(2,1)}, s32[4,2]{1,0:T(4,128)S(1)}, bf16[4,128,32]{2,1,0:T(8,128)(2,1)S(1)}, s32[]{:T(128)}) while((s32[]{:T(128)}, bf16[128,2048]{1,0:T(8,128)(2,1)}, s32[4,2]{1,0:T(4,128)S(1)}, bf16[4,128,32]{2,1,0:T(8,128)(2,1)S(1)}, s32[]{:T(128)}) %tuple.180), condition=%wide.while_cond.1, body=%wide.while_body.1.sunk | while | flops 2 | bytes 41057 | solution.py:19
  66.6 8.4 %while.41 = (s32[]{:T(128)}, bf16[128,2048]{1,0:T(8,128)(2,1)}, s32[4,2]{1,0:T(4,128)S(1)}, bf16[4,128,32]{2,1,0:T(8,128)(2,1)S(1)}, s32[]{:T(128)}) while((s32[]{:T(128)}, bf16[128,2048]{1,0:T(8,128)(2,1)}, s32[4,2]{1,0:T(4,128)S(1)}, bf16[4,128,32]{2,1,0:T(8,128)(2,1)S(1)}, s32[]{:T(128)}) %tuple.183), condition=%wide.while_cond, body=%wide.while_body.sunk | while | flops 2 | bytes 41057 | solution.py:19
  75.4 8.3 %while.42 = (s32[]{:T(128)}, bf16[128,2048]{1,0:T(8,128)(2,1)}, s32[4,2]{1,0:T(4,128)S(1)}, bf16[4,128,32]{2,1,0:T(8,128)(2,1)S(1)}, s32[]{:T(128)}) while((s32[]{:T(128)}, bf16[128,2048]{1,0:T(8,128)(2,1)}, s32[4,2]{1,0:T(4,128)S(1)}, bf16[4,128,32]{2,1,0:T(8,128)(2,1)S(1)}, s32[]{:T(128)}) %tuple.186), condition=%wide.while_cond.2, body=%wide.while_body.2.sunk | while | flops 2 | bytes 41057 | solution.py:19
  86.2 8.3 %while.40 = (s32[]{:T(128)}, bf16[128,2048]{1,0:T(8,128)(2,1)}, s32[4,2]{1,0:T(4,128)S(1)}, bf16[4,128,32]{2,1,0:T(8,128)(2,1)S(1)}, s32[]{:T(128)}) while((s32[]{:T(128)}, bf16[128,2048]{1,0:T(8,128)(2,1)}, s32[4,2]{1,0:T(4,128)S(1)}, bf16[4,128,32]{2,1,0:T(8,128)(2,1)S(1)}, s32[]{:T(128)}) %tuple.180), condition=%wide.while_cond.1, body=%wide.while_body.1.sunk | while | flops 2 | bytes 41057 | solution.py:19
  94.7 8.4 %while.41 = (s32[]{:T(128)}, bf16[128,2048]{1,0:T(8,128)(2,1)}, s32[4,2]{1,0:T(4,128)S(1)}, bf16[4,128,32]{2,1,0:T(8,128)(2,1)S(1)}, s32[]{:T(128)}) while((s32[]{:T(128)}, bf16[128,2048]{1,0:T(8,128)(2,1)}, s32[4,2]{1,0:T(4,128)S(1)}, bf16[4,128,32]{2,1,0:T(8,128)(2,1)S(1)}, s32[]{:T(128)}) %tuple.183), condition=%wide.while_cond, body=%wide.while_body.sunk | while | flops 2 | bytes 41057 | solution.py:19
  103.5 8.3 %while.42 = (s32[]{:T(128)}, bf16[128,2048]{1,0:T(8,128)(2,1)}, s32[4,2]{1,0:T(4,128)S(1)}, bf16[4,128,32]{2,1,0:T(8,128)(2,1)S(1)}, s32[]{:T(128)}) while((s32[]{:T(128)}, bf16[128,2048]{1,0:T(8,128)(2,1)}, s32[4,2]{1,0:T(4,128)S(1)}, bf16[4,128,32]{2,1,0:T(8,128)(2,1)S(1)}, s32[]{:T(128)}) %tuple.186), condition=%wide.while_cond.2, body=%wide.while_body.2.sunk | while | flops 2 | bytes 41057 | solution.py:19
  114.2 8.4 %while.40 = (s32[]{:T(128)}, bf16[128,2048]{1,0:T(8,128)(2,1)}, s32[4,2]{1,0:T(4,128)S(1)}, bf16[4,128,32]{2,1,0:T(8,128)(2,1)S(1)}, s32[]{:T(128)}) while((s32[]{:T(128)}, bf16[128,2048]{1,0:T(8,128)(2,1)}, s32[4,2]{1,0:T(4,128)S(1)}, bf16[4,128,32]{2,1,0:T(8,128)(2,1)S(1)}, s32[]{:T(128)}) %tuple.180), condition=%wide.while_cond.1, body=%wide.while_body.1.sunk | while | flops 2 | bytes 41057 | solution.py:19
  122.9 8.4 %while.41 = (s32[]{:T(128)}, bf16[128,2048]{1,0:T(8,128)(2,1)}, s32[4,2]{1,0:T(4,128)S(1)}, bf16[4,128,32]{2,1,0:T(8,128)(2,1)S(1)}, s32[]{:T(128)}) while((s32[]{:T(128)}, bf16[128,2048]{1,0:T(8,128)(2,1)}, s32[4,2]{1,0:T(4,128)S(1)}, bf16[4,128,32]{2,1,0:T(8,128)(2,1)S(1)}, s32[]{:T(128)}) %tuple.183), condition=%wide.while_cond, body=%wide.while_body.sunk | while | flops 2 | bytes 41057 | solution.py:19
  131.7 8.3 %while.42 = (s32[]{:T(128)}, bf16[128,2048]{1,0:T(8,128)(2,1)}, s32[4,2]{1,0:T(4,128)S(1)}, bf16[4,128,32]{2,1,0:T(8,128)(2,1)S(1)}, s32[]{:T(128)}) while((s32[]{:T(128)}, bf16[128,2048]{1,0:T(8,128)(2,1)}, s32[4,2]{1,0:T(4,128)S(1)}, bf16[4,128,32]{2,1,0:T(8,128)(2,1)S(1)}, s32[]{:T(128)}) %tuple.186), condition=%wide.while_cond.2, body=%wide.while_body.2.sunk | while | flops 2 | bytes 41057 | solution.py:19
  142.4 8.4 %while.40 = (s32[]{:T(128)}, bf16[128,2048]{1,0:T(8,128)(2,1)}, s32[4,2]{1,0:T(4,128)S(1)}, bf16[4,128,32]{2,1,0:T(8,128)(2,1)S(1)}, s32[]{:T(128)}) while((s32[]{:T(128)}, bf16[128,2048]{1,0:T(8,128)(2,1)}, s32[4,2]{1,0:T(4,128)S(1)}, bf16[4,128,32]{2,1,0:T(8,128)(2,1)S(1)}, s32[]{:T(128)}) %tuple.180), condition=%wide.while_cond.1, body=%wide.while_body.1.sunk | while | flops 2 | bytes 41057 | solution.py:19
  151.0 8.4 %while.41 = (s32[]{:T(128)}, bf16[128,2048]{1,0:T(8,128)(2,1)}, s32[4,2]{1,0:T(4,128)S(1)}, bf16[4,128,32]{2,1,0:T(8,128)(2,1)S(1)}, s32[]{:T(128)}) while((s32[]{:T(128)}, bf16[128,2048]{1,0:T(8,128)(2,1)}, s32[4,2]{1,0:T(4,128)S(1)}, bf16[4,128,32]{2,1,0:T(8,128)(2,1)S(1)}, s32[]{:T(128)}) %tuple.183), condition=%wide.while_cond, body=%wide.while_body.sunk | while | flops 2 | bytes 41057 | solution.py:19
  159.9 8.4 %while.42 = (s32[]{:T(128)}, bf16[128,2048]{1,0:T(8,128)(2,1)}, s32[4,2]{1,0:T(4,128)S(1)}, bf16[4,128,32]{2,1,0:T(8,128)(2,1)S(1)}, s32[]{:T(128)}) while((s32[]{:T(128)}, bf16[128,2048]{1,0:T(8,128)(2,1)}, s32[4,2]{1,0:T(4,128)S(1)}, bf16[4,128,32]{2,1,0:T(8,128)(2,1)S(1)}, s32[]{:T(128)}) %tuple.186), condition=%wide.while_cond.2, body=%wide.while_body.2.sunk | while | flops 2 | bytes 41057 | solution.py:19
  170.5 2.9 reshape.88
  173.5 283.3 %all-reduce.8.cloned.1.call-done = f32[16,32768]{1,0:T(8,128)} async-done(((f32[16,32768]{1,0:T(8,128)}), f32[16,32768]{1,0:T(8,128)}) %all-reduce.8.cloned.1.call-update) | async-done | bytes 2097168 | tf_op jit(solution)/shard_map/psum | solution.py:72
  456.8 1.8 subtract_convert_fusion
  460.0 218.5 %while.39 = (s32[]{:T(128)}, f32[128,2048]{0,1:T(8,128)}, s32[4,4,3]{2,1,0:T(4,128)S(1)}, bf16[128,2048]{1,0:T(8,128)(2,1)}, bf16[4,4,32768]{2,1,0:T(4,128)(2,1)...) while((s32[]{:T(128)}, f32[128,2048]{0,1:T(8,128)}, ...), condition=%wide.region_6.7_spmd, body=%wide.region_5.6_spmd.sunk | while | flops 70271032 | bytes 17688200 | solution.py:87
  461.6 8.4 %while.43 = (s32[]{:T(128)}, bf16[128,2048]{1,0:T(8,128)(2,1)}, s32[4,2]{1,0:T(4,128)S(1)}, bf16[4,128,32]{2,1,0:T(8,128)(2,1)S(1)}, s32[]{:T(128)}) while((s32[]{:T(128)}, bf16[128,2048]{1,0:T(8,128)(2,1)}, s32[4,2]{1,0:T(4,128)S(1)}, bf16[4,128,32]{2,1,0:T(8,128)(2,1)S(1)}, s32[]{:T(128)}) %tuple.171), condition=%wide.while_cond.4, body=%wide.while_body.4.sunk | while | flops 2 | bytes 41057 | solution.py:19
  470.2 8.3 %while.44 = (s32[]{:T(128)}, bf16[128,2048]{1,0:T(8,128)(2,1)}, s32[4,2]{1,0:T(4,128)S(1)}, bf16[4,128,32]{2,1,0:T(8,128)(2,1)S(1)}, s32[]{:T(128)}) while((s32[]{:T(128)}, bf16[128,2048]{1,0:T(8,128)(2,1)}, s32[4,2]{1,0:T(4,128)S(1)}, bf16[4,128,32]{2,1,0:T(8,128)(2,1)S(1)}, s32[]{:T(128)}) %tuple.174), condition=%wide.while_cond.3, body=%wide.while_body.3.sunk | while | flops 2 | bytes 41057 | solution.py:19
  481.8 8.9 %while.45 = (s32[]{:T(128)}, bf16[128,2048]{1,0:T(8,128)(2,1)}, s32[4,2]{1,0:T(4,128)S(1)}, bf16[4,128,32]{2,1,0:T(8,128)(2,1)S(1)}, s32[]{:T(128)}) while((s32[]{:T(128)}, bf16[128,2048]{1,0:T(8,128)(2,1)}, s32[4,2]{1,0:T(4,128)S(1)}, bf16[4,128,32]{2,1,0:T(8,128)(2,1)S(1)}, s32[]{:T(128)}) %tuple.177), condition=%wide.while_cond.5, body=%wide.while_body.5.sunk | while | flops 2 | bytes 41057 | solution.py:19
  516.2 8.3 %while.43 = (s32[]{:T(128)}, bf16[128,2048]{1,0:T(8,128)(2,1)}, s32[4,2]{1,0:T(4,128)S(1)}, bf16[4,128,32]{2,1,0:T(8,128)(2,1)S(1)}, s32[]{:T(128)}) while((s32[]{:T(128)}, bf16[128,2048]{1,0:T(8,128)(2,1)}, s32[4,2]{1,0:T(4,128)S(1)}, bf16[4,128,32]{2,1,0:T(8,128)(2,1)S(1)}, s32[]{:T(128)}) %tuple.171), condition=%wide.while_cond.4, body=%wide.while_body.4.sunk | while | flops 2 | bytes 41057 | solution.py:19
  524.7 8.3 %while.44 = (s32[]{:T(128)}, bf16[128,2048]{1,0:T(8,128)(2,1)}, s32[4,2]{1,0:T(4,128)S(1)}, bf16[4,128,32]{2,1,0:T(8,128)(2,1)S(1)}, s32[]{:T(128)}) while((s32[]{:T(128)}, bf16[128,2048]{1,0:T(8,128)(2,1)}, s32[4,2]{1,0:T(4,128)S(1)}, bf16[4,128,32]{2,1,0:T(8,128)(2,1)S(1)}, s32[]{:T(128)}) %tuple.174), condition=%wide.while_cond.3, body=%wide.while_body.3.sunk | while | flops 2 | bytes 41057 | solution.py:19
  536.3 8.9 %while.45 = (s32[]{:T(128)}, bf16[128,2048]{1,0:T(8,128)(2,1)}, s32[4,2]{1,0:T(4,128)S(1)}, bf16[4,128,32]{2,1,0:T(8,128)(2,1)S(1)}, s32[]{:T(128)}) while((s32[]{:T(128)}, bf16[128,2048]{1,0:T(8,128)(2,1)}, s32[4,2]{1,0:T(4,128)S(1)}, bf16[4,128,32]{2,1,0:T(8,128)(2,1)S(1)}, s32[]{:T(128)}) %tuple.177), condition=%wide.while_cond.5, body=%wide.while_body.5.sunk | while | flops 2 | bytes 41057 | solution.py:19
  548.6 1.7 fusion.78
  570.7 8.4 %while.43 = (s32[]{:T(128)}, bf16[128,2048]{1,0:T(8,128)(2,1)}, s32[4,2]{1,0:T(4,128)S(1)}, bf16[4,128,32]{2,1,0:T(8,128)(2,1)S(1)}, s32[]{:T(128)}) while((s32[]{:T(128)}, bf16[128,2048]{1,0:T(8,128)(2,1)}, s32[4,2]{1,0:T(4,128)S(1)}, bf16[4,128,32]{2,1,0:T(8,128)(2,1)S(1)}, s32[]{:T(128)}) %tuple.171), condition=%wide.while_cond.4, body=%wide.while_body.4.sunk | while | flops 2 | bytes 41057 | solution.py:19
  579.3 8.3 %while.44 = (s32[]{:T(128)}, bf16[128,2048]{1,0:T(8,128)(2,1)}, s32[4,2]{1,0:T(4,128)S(1)}, bf16[4,128,32]{2,1,0:T(8,128)(2,1)S(1)}, s32[]{:T(128)}) while((s32[]{:T(128)}, bf16[128,2048]{1,0:T(8,128)(2,1)}, s32[4,2]{1,0:T(4,128)S(1)}, bf16[4,128,32]{2,1,0:T(8,128)(2,1)S(1)}, s32[]{:T(128)}) %tuple.174), condition=%wide.while_cond.3, body=%wide.while_body.3.sunk | while | flops 2 | bytes 41057 | solution.py:19
  590.9 8.9 %while.45 = (s32[]{:T(128)}, bf16[128,2048]{1,0:T(8,128)(2,1)}, s32[4,2]{1,0:T(4,128)S(1)}, bf16[4,128,32]{2,1,0:T(8,128)(2,1)S(1)}, s32[]{:T(128)}) while((s32[]{:T(128)}, bf16[128,2048]{1,0:T(8,128)(2,1)}, s32[4,2]{1,0:T(4,128)S(1)}, bf16[4,128,32]{2,1,0:T(8,128)(2,1)S(1)}, s32[]{:T(128)}) %tuple.177), condition=%wide.while_cond.5, body=%wide.while_body.5.sunk | while | flops 2 | bytes 41057 | solution.py:19
  625.4 8.4 %while.43 = (s32[]{:T(128)}, bf16[128,2048]{1,0:T(8,128)(2,1)}, s32[4,2]{1,0:T(4,128)S(1)}, bf16[4,128,32]{2,1,0:T(8,128)(2,1)S(1)}, s32[]{:T(128)}) while((s32[]{:T(128)}, bf16[128,2048]{1,0:T(8,128)(2,1)}, s32[4,2]{1,0:T(4,128)S(1)}, bf16[4,128,32]{2,1,0:T(8,128)(2,1)S(1)}, s32[]{:T(128)}) %tuple.171), condition=%wide.while_cond.4, body=%wide.while_body.4.sunk | while | flops 2 | bytes 41057 | solution.py:19
  634.0 8.4 %while.44 = (s32[]{:T(128)}, bf16[128,2048]{1,0:T(8,128)(2,1)}, s32[4,2]{1,0:T(4,128)S(1)}, bf16[4,128,32]{2,1,0:T(8,128)(2,1)S(1)}, s32[]{:T(128)}) while((s32[]{:T(128)}, bf16[128,2048]{1,0:T(8,128)(2,1)}, s32[4,2]{1,0:T(4,128)S(1)}, bf16[4,128,32]{2,1,0:T(8,128)(2,1)S(1)}, s32[]{:T(128)}) %tuple.174), condition=%wide.while_cond.3, body=%wide.while_body.3.sunk | while | flops 2 | bytes 41057 | solution.py:19
  645.6 8.9 %while.45 = (s32[]{:T(128)}, bf16[128,2048]{1,0:T(8,128)(2,1)}, s32[4,2]{1,0:T(4,128)S(1)}, bf16[4,128,32]{2,1,0:T(8,128)(2,1)S(1)}, s32[]{:T(128)}) while((s32[]{:T(128)}, bf16[128,2048]{1,0:T(8,128)(2,1)}, s32[4,2]{1,0:T(4,128)S(1)}, bf16[4,128,32]{2,1,0:T(8,128)(2,1)S(1)}, s32[]{:T(128)}) %tuple.177), condition=%wide.while_cond.5, body=%wide.while_body.5.sunk | while | flops 2 | bytes 41057 | solution.py:19
  680.6 87.2 %reduce-scatter.2.cloned.1.call-done = f32[128,256]{0,1:T(8,128)} async-done(((f32[128,2048]{0,1:T(8,128)}), f32[128,256]{0,1:T(8,128)}) %reduce-scatter.2.cloned.1.call-update) | async-done | bytes 131088 | tf_op jit(solution)/shard_map/reduce_scatter | solution.py:88
  (499 shorter events, 307.1 us)
Async XLA Ops:
  7.2 50.6 %copy-start.5 = (s32[16,3]{0,1:T(4,128)S(1)}, s32[16,3]{0,1:T(4,128)}, u32[]{:S(2)}) copy-start(s32[16,3]{0,1:T(4,128)} %param.13) | copy-start | bytes 580
  7.2 449.6 %all-reduce.8.cloned.1.call-start = ((), (), s32[]{:S(2)}) async-start(), calls=%async_computation.1 | async-start | bytes 4194304 | tf_op jit(solution)/shard_map/psum | solution.py:72
  8.2 49.6 %copy-start.2 = (f32[128,256]{0,1:T(8,128)}, f32[128,256]{0,1:T(8,128)S(1)}, u32[]{:S(2)}) copy-start(f32[128,256]{0,1:T(8,128)S(1)} %copy.45) | copy-start | bytes 393220
  173.4 283.4 %copy-start.4 = (f32[16,32768]{1,0:T(8,128)S(1)}, f32[16,32768]{1,0:T(8,128)}, u32[]{:S(2)}) copy-start(f32[16,32768]{1,0:T(8,128)} %param.12) | copy-start | bytes 6291460
  173.4 594.4 %reduce-scatter.2.cloned.1.call-start = ((), (), s32[]{:S(2)}) async-start(), calls=%async_computation.2 | async-start | bytes 1179648 | tf_op jit(solution)/shard_map/reduce_scatter | solution.py:88
  460.0 18.6 %copy-start = (bf16[4,4,32768]{2,1,0:T(4,128)(2,1)}, bf16[4,4,32768]{2,1,0:T(4,128)(2,1)S(1)}, u32[]{:S(2)}) copy-start(bf16[4,4,32768]{2,1,0:T(4,128)(2,1)S(1)} %get-tuple-element.724) | copy-start | bytes 3145732 | tf_op jit(solution)/shard_map/while
  492.1 22.6 %copy-start.1 = (bf16[4,4,32768]{2,1,0:T(4,128)(2,1)S(1)}, bf16[4,4,32768]{2,1,0:T(4,128)(2,1)}, u32[]{:S(2)}) copy-start(bf16[4,4,32768]{2,1,0:T(4,128)(2,1)} %copy-done) | copy-start | bytes 3145732 | tf_op jit(solution)/shard_map/while
  514.6 18.5 %copy-start = (bf16[4,4,32768]{2,1,0:T(4,128)(2,1)}, bf16[4,4,32768]{2,1,0:T(4,128)(2,1)S(1)}, u32[]{:S(2)}) copy-start(bf16[4,4,32768]{2,1,0:T(4,128)(2,1)S(1)} %get-tuple-element.724) | copy-start | bytes 3145732 | tf_op jit(solution)/shard_map/while
  546.6 22.6 %copy-start.1 = (bf16[4,4,32768]{2,1,0:T(4,128)(2,1)S(1)}, bf16[4,4,32768]{2,1,0:T(4,128)(2,1)}, u32[]{:S(2)}) copy-start(bf16[4,4,32768]{2,1,0:T(4,128)(2,1)} %copy-done) | copy-start | bytes 3145732 | tf_op jit(solution)/shard_map/while
  569.2 18.6 %copy-start = (bf16[4,4,32768]{2,1,0:T(4,128)(2,1)}, bf16[4,4,32768]{2,1,0:T(4,128)(2,1)S(1)}, u32[]{:S(2)}) copy-start(bf16[4,4,32768]{2,1,0:T(4,128)(2,1)S(1)} %get-tuple-element.724) | copy-start | bytes 3145732 | tf_op jit(solution)/shard_map/while
  601.2 22.6 %copy-start.1 = (bf16[4,4,32768]{2,1,0:T(4,128)(2,1)S(1)}, bf16[4,4,32768]{2,1,0:T(4,128)(2,1)}, u32[]{:S(2)}) copy-start(bf16[4,4,32768]{2,1,0:T(4,128)(2,1)} %copy-done) | copy-start | bytes 3145732 | tf_op jit(solution)/shard_map/while
  623.8 18.7 %copy-start = (bf16[4,4,32768]{2,1,0:T(4,128)(2,1)}, bf16[4,4,32768]{2,1,0:T(4,128)(2,1)S(1)}, u32[]{:S(2)}) copy-start(bf16[4,4,32768]{2,1,0:T(4,128)(2,1)S(1)} %get-tuple-element.724) | copy-start | bytes 3145732 | tf_op jit(solution)/shard_map/while
  655.9 22.6 %copy-start.1 = (bf16[4,4,32768]{2,1,0:T(4,128)(2,1)S(1)}, bf16[4,4,32768]{2,1,0:T(4,128)(2,1)}, u32[]{:S(2)}) copy-start(bf16[4,4,32768]{2,1,0:T(4,128)(2,1)} %copy-done) | copy-start | bytes 3145732 | tf_op jit(solution)/shard_map/while
  678.5 90.3 %copy-start.3 = (f32[128,256]{0,1:T(8,128)S(1)}, f32[128,256]{0,1:T(8,128)}, u32[]{:S(2)}) copy-start(f32[128,256]{0,1:T(8,128)} %copy-done.2) | copy-start | bytes 393220
Sparse Core Ops, SparseCore 0:
  173.6 283.1 all-reduce.7
  678.6 89.1 reduce-scatter.1
where the time goes:
time: 790 us; the launch traced here: 779 us
  waiting for transfers between devices  371 us (47%)
  local copies, waits for them, and re-layouts  228 us (29%)
  other arithmetic  74.7 us (9%)
  blocking collectives  48.3 us (6%)
  loops' own time  32.6 us (4%)
  between operations  14.1 us (2%)
  matrix products  10.1 us (1%)
    psum x1, waiting for transfers between devices, shards(): totals = lax.psum(partial_value, 'rows')  283 us
    gather x288, local copies, waits for them, and re-layouts  201 us
    reduce_scatter x1, waiting for transfers between devices, shards(): lax.psum_scatter(row_grad, 'marg', scatter_dimension=1, tiled=True)  87.2 us
    dynamic_update_slice x48, other arithmetic, add_cols(): return lax.dynamic_update_slice_in_dim(total, current + term, start, 1)  63.9 us
    all_gather x1, blocking collectives, shards(): full = lax.all_gather(probs_low, 'marg', axis=1, tiled=True)  48.3 us
    another operation x1, loops' own time, shards(): lax.scan(backward_block, start_grad, (grouped, resid_groups))  30.1 us
  transfers between devices with their start and end apart: 2, of which 2 were waited for; matrix products, arithmetic and copies ran while one was open for 0% of the time, Pallas kernels for 0%

commit v1 on v0

v1 whole, which is shorter than its diff:
```python
import jax
import jax.numpy as jnp
from jax import lax
from jax.experimental import pallas as pl
from jax.experimental.pallas import tpu as pltpu
from jax.sharding import Mesh, PartitionSpec as P

V = 32
ADAM_STEP = 4
PARTS = (4, 2, 2, 2, 4, 2)
NAMES = ("x", "u", "w", "c", "y", "h")
ROW_AXES = ("x", "u", "w", "c")
MARG_AXES = ("y", "h")
SHARE_AXES = ("x", "w", "c")
MODS = 4
VMEM = pl.BlockSpec(memory_space=pltpu.VMEM)
SMEM = pl.BlockSpec(memory_space=pltpu.SMEM)
LIMIT = 48 * 1024 * 1024


def call(body, out_shape, operands, specs, scratch=()):
    return pl.pallas_call(
        body,
        out_shape=out_shape,
        in_specs=specs,
        out_specs=jax.tree.map(lambda unused: VMEM, out_shape),
        scratch_shapes=scratch,
        compiler_params=pltpu.CompilerParams(vmem_limit_bytes=LIMIT),
    )(*operands)


def relax_kernel(logits_ref, probs_ref, send_ref):
    flipped = logits_ref[...].T
    copies = send_ref.shape[0]
    for attr in range(probs_ref.shape[0]):
        block = flipped[attr * V : (attr + 1) * V, :]
        top = jnp.max(block, axis=0, keepdims=True)
        expo = jnp.exp(block - top)
        probs = expo / jnp.sum(expo, axis=0, keepdims=True)
        probs_ref[attr] = probs
        low = probs.astype(jnp.bfloat16)
        for copy in range(copies):
            send_ref[copy, attr] = low


def select_kernel(triples_ref, full_ref, send_ref):
    for marg in range(send_ref.shape[0]):
        for which in range(3):
            send_ref[marg, which] = full_ref[triples_ref[marg, which]]


def fill_pairs(src_ref, source, lanes, pairs_ref, first_ref, second_ref):
    first_ref[...] = src_ref[source, 0].astype(jnp.float32)
    second_ref[...] = src_ref[source, 1].astype(jnp.float32)
    first = first_ref[...]
    for mod in range(MODS):
        second = second_ref[pl.ds(mod, V // MODS, stride=MODS), :]
        both = first[:, None, :] * second[None, :, :]
        pairs_ref[mod, :, lanes] = both.reshape(V * V // MODS, both.shape[2]).astype(jnp.bfloat16)


def answer_kernel(src_ref, own_ref, send_ref, pairs_ref, third_ref, first_ref, second_ref):
    sources, unused, unused2, rows = src_ref.shape

    def fill(source, carry):
        lanes = pl.ds(pl.multiple_of(source * rows, rows), rows)
        fill_pairs(src_ref, source, lanes, pairs_ref, first_ref, second_ref)
        third_ref[:, lanes] = src_ref[source, 2]
        return carry

    lax.fori_loop(0, sources, fill, 0)
    for mod in range(MODS):
        part = lax.dot_general(
            third_ref[...], pairs_ref[mod], (((1,), (1,)), ((), ())), preferred_element_type=jnp.float32
        )
        own_ref[mod * V : (mod + 1) * V, :] = part
        send_ref[mod * V : (mod + 1) * V, :] = part.astype(jnp.bfloat16)


def backward_kernel(
    scale, src_ref, own_ref, other_ref, target_ref, out_ref, low_ref, mask_ref, pairs_ref, first_ref, second_ref, cross_ref, grad_ref
):
    sources, unused, unused2, rows = src_ref.shape
    total = own_ref[...] + other_ref[...].astype(jnp.float32)
    resid = scale * total - target_ref[...].T
    low_ref[...] = resid.astype(jnp.bfloat16)
    flipped = resid.T
    lane_mod = lax.broadcasted_iota(jnp.int32, flipped.shape, 1) // V
    for mod in range(MODS):
        mask_ref[mod] = jnp.where(lane_mod == mod, flipped, 0.0).astype(jnp.bfloat16)

    def step(source, carry):
        fill_pairs(src_ref, source, slice(None), pairs_ref, first_ref, second_ref)
        third = src_ref[source, 2]
        stacked = jnp.concatenate([third] * MODS, axis=0)
        third_grad = jnp.zeros(third.shape, jnp.float32)
        first = first_ref[...]
        first_sum = jnp.zeros((V, V // MODS, rows), jnp.float32)
        for mod in range(MODS):
            third_grad += jnp.dot(
                low_ref[mod * V : (mod + 1) * V, :], pairs_ref[mod], preferred_element_type=jnp.float32
            )
            cross = jnp.dot(mask_ref[mod], stacked, preferred_element_type=jnp.float32)
            cross = cross.reshape(V, V // MODS, rows)
            second = second_ref[pl.ds(mod, V // MODS, stride=MODS), :]
            first_sum += cross * second[None, :, :]
            grad_ref[pl.ds(mod, V // MODS, stride=MODS), :] = jnp.sum(cross * first[:, None, :], axis=0)
        cross_ref[...] = first_sum.reshape(V * V // MODS, rows)
        first_grad = jnp.zeros((V, rows), jnp.float32)
        for part in range(V // MODS):
            first_grad += cross_ref[pl.ds(part, V, stride=V // MODS), :]
        out_ref[source, 0] = first_grad.astype(jnp.bfloat16)
        out_ref[source, 1] = grad_ref[...].astype(jnp.bfloat16)
        out_ref[source, 2] = third_grad.astype(jnp.bfloat16)
        return carry

    lax.fori_loop(0, sources, step, 0)


def collect_kernel(triples_ref, grads_ref, send_ref, total_ref):
    total_ref[...] = jnp.zeros(total_ref.shape, jnp.float32)
    for marg in range(grads_ref.shape[0]):
        for which in range(3):
            attr = triples_ref[marg, which]
            total_ref[attr] = total_ref[attr] + grads_ref[marg, which].astype(jnp.float32)
    send_ref[...] = total_ref[...].astype(jnp.bfloat16)


def adam_kernel(
    parts_ref, probs_ref, logits_ref, first_ref, second_ref, out_logits_ref, out_first_ref, out_second_ref
):
    row_grad = parts_ref[0].astype(jnp.float32)
    for part in range(1, parts_ref.shape[0]):
        row_grad += parts_ref[part].astype(jnp.float32)
    probs = probs_ref[...]
    inner = jnp.sum(probs * row_grad, axis=1, keepdims=True)
    grad = 512.0 * probs * (row_grad - inner)
    grad = grad.reshape(grad.shape[0] * V, grad.shape[2]).T
    new_first = 0.9 * first_ref[...] + 0.1 * grad
    new_second = 0.999 * second_ref[...] + 0.001 * grad * grad
    first_hat = new_first / (1.0 - 0.9**ADAM_STEP)
    second_hat = new_second / (1.0 - 0.999**ADAM_STEP)
    out_logits_ref[...] = logits_ref[...] - 0.5 * first_hat / (jnp.sqrt(second_hat) + 1e-08)
    out_first_ref[...] = new_first
    out_second_ref[...] = new_second


def swap(value, axes):
    return lax.all_to_all(value, axes, 0, 0, tiled=True)


def shards(logits, first_moment, second_moment, targets, triples):
    rows, cols = logits.shape
    margs, cells = targets.shape
    attrs = cols // V
    groups = lax.axis_size(MARG_AXES)
    scale = cells / (rows * lax.axis_size(ROW_AXES))
    f32, low = jnp.float32, jnp.bfloat16
    shape = jax.ShapeDtypeStruct
    probs, copies = call(
        relax_kernel,
        (shape((attrs, V, rows), f32), shape((groups, attrs, V, rows), low)),
        (logits,),
        [VMEM],
    )
    full = swap(copies, MARG_AXES).reshape(groups * attrs, V, rows)
    picked = call(select_kernel, shape((margs, 3, V, rows), low), (triples, full), [SMEM, VMEM])
    sources = swap(picked, SHARE_AXES)
    tall, wide = V * V // MODS, V * MODS
    own, send = call(
        answer_kernel,
        (shape((wide, tall), f32), shape((wide, tall), low)),
        (sources,),
        [VMEM],
        [
            pltpu.VMEM((MODS, tall, margs * rows), low),
            pltpu.VMEM((V, margs * rows), low),
            pltpu.VMEM((V, rows), f32),
            pltpu.VMEM((V, rows), f32),
        ],
    )
    other = lax.ppermute(send, "u", [(0, 1), (1, 0)])
    place = lax.axis_index(SHARE_AXES)
    target = lax.dynamic_slice_in_dim(targets, place, 1, 0).reshape(tall, wide)
    grads = call(
        lambda *refs: backward_kernel(scale, *refs),
        shape((margs, 3, V, rows), low),
        (sources, own, other, target),
        [VMEM] * 4,
        [
            pltpu.VMEM((wide, tall), low),
            pltpu.VMEM((MODS, tall, wide), low),
            pltpu.VMEM((MODS, tall, rows), low),
            pltpu.VMEM((V, rows), f32),
            pltpu.VMEM((V, rows), f32),
            pltpu.VMEM((tall, rows), f32),
            pltpu.VMEM((V, rows), f32),
        ],
    )
    returned = swap(grads, SHARE_AXES)
    totals = call(
        collect_kernel,
        shape((groups * attrs, V, rows), low),
        (triples, returned),
        [SMEM, VMEM],
        [pltpu.VMEM((groups * attrs, V, rows), f32)],
    )
    parts = swap(totals.reshape(groups, attrs, V, rows), MARG_AXES)
    return call(
        adam_kernel,
        (shape((rows, cols), f32),) * 3,
        (parts, probs, logits, first_moment, second_moment),
        [VMEM] * 5,
    )


def solution(mesh):
    fine = Mesh(mesh.devices.reshape(PARTS), NAMES)
    table = P(ROW_AXES, MARG_AXES)
    listed = P(MARG_AXES, None)
    return jax.shard_map(
        shards,
        mesh=fine,
        in_specs=(table, table, table, listed, listed),
        out_specs=(table, table, table),
        check_vma=False,
    )
```

time: 790 us -> 98.8 us (0.13); the launches traced: 779 us -> 98.5 us
  waiting for transfers between devices: 371 us -> 31.2 us
  local copies, waits for them, and re-layouts: 228 us -> 1.94 us
  other arithmetic: 74.7 us -> 0 us
  loops' own time: 32.6 us -> 0 us
  starting transfers between devices: 0.08 us -> 17.1 us
  between operations: 14.1 us -> 0.7 us
  blocking collectives: 48.3 us -> 35.4 us
  Pallas kernels: 0 us -> 12.1 us
  matrix products: 10.1 us -> 0 us
    psum x1 -> x0, waiting for transfers between devices: 283 us -> none  [shards(): totals = lax.psum(partial_value, 'rows')]
    gather x288 -> x0, local copies, waits for them, and re-layouts: 201 us -> none
    reduce_scatter x1 -> x0, waiting for transfers between devices: 87.2 us -> none  [shards(): lax.psum_scatter(row_grad, 'marg', scatter_dimension=1, tiled=True)]
    dynamic_update_slice x48 -> x0, other arithmetic: 63.9 us -> none  [add_cols(): return lax.dynamic_update_slice_in_dim(total, current + term, start, 1)]
    all_gather x1 -> x0, blocking collectives: 48.3 us -> none  [shards(): full = lax.all_gather(probs_low, 'marg', axis=1, tiled=True)]
    all_to_all x0 -> x2, blocking collectives: none -> 35.4 us  [swap(): return lax.all_to_all(value, axes, 0, 0, tiled=True)]
    another operation x26 -> x0, loops' own time: 32.6 us -> none  [the longest x1 30.1 us: shards(): lax.scan(backward_block, start_grad, (grouped, resid_groups))]
    all_to_all x0 -> x2, waiting for transfers between devices: none -> 27.2 us  [swap(): return lax.all_to_all(value, axes, 0, 0, tiled=True)]
  transfers between devices with their start and end apart: 2 -> 3, of which waited for: 2 -> 3; matrix products, arithmetic and copies ran while one was open for 0% -> 1% of each run, Pallas kernels for 0% -> 0%
where the time goes in v1:
time: 98.8 us; the launch traced here: 98.5 us
  blocking collectives  35.4 us (36%)
  waiting for transfers between devices  31.2 us (32%)
  starting transfers between devices  17.1 us (17%)
  Pallas kernels  12.1 us (12%)
  local copies, waits for them, and re-layouts  1.94 us (2%)
    all_to_all x2, blocking collectives, swap(): return lax.all_to_all(value, axes, 0, 0, tiled=True)  35.4 us
    all_to_all x2, waiting for transfers between devices, swap(): return lax.all_to_all(value, axes, 0, 0, tiled=True)  27.2 us
    all_to_all x2, starting transfers between devices, swap(): return lax.all_to_all(value, axes, 0, 0, tiled=True)  16 us
    pallas_call x6, Pallas kernels, call(): pl.pallas_call(body, out_shape=out_shape, in_specs=specs, out_specs=jax.t...  12.1 us
    ppermute x1, waiting for transfers between devices, shards(): other = lax.ppermute(send, 'u', [(0, 1), (1, 0)])  4.05 us
  transfers between devices with their start and end apart: 3, of which 3 were waited for; matrix products, arithmetic and copies ran while one was open for 1% of the time, Pallas kernels for 0%

profile of v1, /device:TPU:32, one launch (start us, length us, event | category | flops | bytes accessed | tf_op | source)
XLA Modules:
  0.0 98.5 jit_solution(15842584341061855811)
XLA Ops:
  0.6 0.0 copy-start
  0.6 0.0 copy-start.1
  0.7 1.0 %copy-done.1 = f32[128,256]{1,0:T(8,128)S(1)} copy-done((f32[128,256]{1,0:T(8,128)S(1)}, f32[128,256]{1,0:T(8,128)}, u32[]{:S(2)}) %copy-start.1) | copy-done | bytes 131096
  1.7 0.9 shard_map.76
  2.6 10.2 %all-to-all-start = ((bf16[8,8,32,128]{3,2,1,0:T(8,128)(2,1)}), bf16[8,8,32,128]{3,2,1,0:T(8,128)(2,1)S(1)}, u32[]{:S(2)}, u32[]{:S(2)}) async-start(bf16[8,8,32,128]{3,2,1,0:T(8,128)(2,1)} %get-tuple-element.7), calls=%async_computation | async-start | bytes 1048576 | tf_op jit(solution)/shard_map/all_to_all | solution.py:149
  12.8 0.8 copy.9.triples_ref
  13.6 18.8 %all-to-all-done = bf16[8,8,32,128]{3,2,1,0:T(8,128)(2,1)S(1)} async-done(((bf16[8,8,32,128]{3,2,1,0:T(8,128)(2,1)}), bf16[8,8,32,128]{3,2,1,0:T(8,128)(2,1)S(1)}, u32[]{:S(2)}, u32[]{:S(2)}) %all-to-all-start) | async-done | bytes 524320 | tf_op jit(solution)/shard_map/all_to_all | solution.py:149
  32.4 1.4 %shard_map.77 = bf16[16,3,32,128]{3,2,1,0:T(8,128)(2,1)} custom-call(s32[16,3]{1,0:T(8,128)S(1)} %copy.9.triples_ref, bf16[64,32,128]{2,1,0:T(8,128)(2,1)S(1)} %bitcast.3), custom_call_target="tpu_custom_call" | custom-call | tf_op jit(solution)/shard_map/pallas_call | solution.py:22
  33.9 5.8 %all-to-all-start.1 = ((bf16[16,3,32,128]{3,2,1,0:T(8,128)(2,1)}), bf16[16,3,32,128]{3,2,1,0:T(8,128)(2,1)S(1)}, u32[]{:S(2)}, u32[]{:S(2)}) async-start(bf16[16,3,32,128]{3,2,1,0:T(8,128)(2,1)} %shard_map.77), calls=%async_computation.1 | async-start | bytes 786432 | tf_op jit(solution)/shard_map/all_to_all | solution.py:149
  39.7 8.3 %all-to-all-done.1.src_ref.refs_0_ = bf16[16,3,32,128]{3,2,1,0:T(8,128)(2,1)S(1)} async-done(((bf16[16,3,32,128]{3,2,1,0:T(8,128)(2,1)}), bf16[16,3,32,128]{3,2,1,0:T(8,128)(2,1)S(1)}, u32[]{:S(2)}, u32[]{:S(2)}) %all-to-all-start.1) | async-done | bytes 393248 | tf_op jit(solution)/shard_map/all_to_all | solution.py:149
  48.0 2.8 %shard_map.78 = (f32[128,256]{1,0:T(8,128)S(1)}, bf16[128,256]{1,0:T(8,128)(2,1)S(1)}) custom-call(bf16[16,3,32,128]{3,2,1,0:T(8,128)(2,1)S(1)} %all-to-all-done.1.src_ref.refs_0_), custom_call_target="tpu_custom_call" | custom-call | tf_op jit(solution)/shard_map/pallas_call | solution.py:22
  50.8 0.0 copy-start.2
  50.8 0.0 copy-start.3
  50.9 0.0 copy-start.4
  50.9 1.1 %collective-permute-start = (bf16[128,256]{1,0:T(8,128)(2,1)S(1)}, bf16[128,256]{1,0:T(8,128)(2,1)S(1)}, u32[]{:S(2)}, u32[]{:S(2)}) collective-permute-start(bf16[128,256]{1,0:T(8,128)(2,1)S(1)} %get-tuple-element.9), channel_id=1, source_target_pairs={{0,32},{32,0},{1,33},{33,1},{2,34},{34,2},{3,35},{35,3},{4,36},{36... | collective-permute-start | bytes 196616 | tf_op jit(solution)/shard_map/ppermute | solution.py:182
  52.0 0.0 copy-done
  52.0 0.1 constant_dynamic-slice_fusion
  52.1 4.0 %collective-permute-done.refs_2_ = bf16[128,256]{1,0:T(8,128)(2,1)S(1)} collective-permute-done((bf16[128,256]{1,0:T(8,128)(2,1)S(1)}, bf16[128,256]{1,0:T(8,128)(2,1)S(1)}, u32[]{:S(2)}, u32[]{:S(2)}) %collective-permute-start) | collective-permute-done | bytes 65568 | tf_op jit(solution)/shard_map/ppermute | solution.py:182
  56.1 5.0 %shard_map.79 = bf16[16,3,32,128]{3,2,1,0:T(8,128)(2,1)S(1)} custom-call(bf16[16,3,32,128]{3,2,1,0:T(8,128)(2,1)S(1)} %all-to-all-done.1.src_ref.refs_0_, f32[128,256]{1,0:T(8,128)S(1)} %get-tuple-element.8.refs_1_, bf16[128,256]{1,0:T(8,128)(2,1)S(1)} %collective-permute-done.refs_2_, f32[256,128]{1,0:T(8,128)S(1)} %bitcast.5), custom_call_target="tpu_custom_call" | custom-call | tf_op jit(solution)/shard_map/pallas_call | solution.py:22
  61.1 12.8 %all_to_all.20.grads_ref = bf16[16,3,32,128]{3,2,1,0:T(8,128)(2,1)S(1)} all-to-all(bf16[16,3,32,128]{3,2,1,0:T(8,128)(2,1)S(1)} %shard_map.79), channel_id=1, replica_groups=mesh['x'=4,'u'=2,'w'=2,'c'=2,'y'=4,'h'=2] {'x','w','c'}, dimensions={0} | all-to-all | bytes 786432 | tf_op jit(solution)/shard_map/all_to_all | solution.py:149
  74.0 0.9 shard_map.80
  74.9 22.6 %all_to_all.21.parts_ref = bf16[8,8,32,128]{3,2,1,0:T(8,128)(2,1)S(1)} all-to-all(bf16[8,8,32,128]{3,2,1,0:T(8,128)(2,1)S(1)} %bitcast.4), channel_id=1, replica_groups=mesh['x'=4,'u'=2,'w'=2,'c'=2,'y'=4,'h'=2] {'y','h'}, dimensions={0} | all-to-all | bytes 1048576 | tf_op jit(solution)/shard_map/all_to_all | solution.py:149
  97.5 0.0 copy-done.2
  97.5 0.0 copy-done.3
  97.5 0.0 copy-done.4
  97.5 1.0 shard_map.81
Async XLA Ops:
  0.6 51.3 %copy-start = (f32[16,32768]{1,0:T(8,128)S(1)}, f32[16,32768]{1,0:T(8,128)}, u32[]{:S(2)}) copy-start(f32[16,32768]{1,0:T(8,128)} %param.8) | copy-start | bytes 6291460
  0.6 1.1 %copy-start.1 = (f32[128,256]{1,0:T(8,128)S(1)}, f32[128,256]{1,0:T(8,128)}, u32[]{:S(2)}) copy-start(f32[128,256]{1,0:T(8,128)} %logits_ref.3) | copy-start | bytes 393220
  2.6 29.8 %all-to-all-start = ((bf16[8,8,32,128]{3,2,1,0:T(8,128)(2,1)}), bf16[8,8,32,128]{3,2,1,0:T(8,128)(2,1)S(1)}, u32[]{:S(2)}, u32[]{:S(2)}) async-start(bf16[8,8,32,128]{3,2,1,0:T(8,128)(2,1)} %get-tuple-element.7), calls=%async_computation | async-start | bytes 1048576 | tf_op jit(solution)/shard_map/all_to_all | solution.py:149
  33.9 14.1 %all-to-all-start.1 = ((bf16[16,3,32,128]{3,2,1,0:T(8,128)(2,1)}), bf16[16,3,32,128]{3,2,1,0:T(8,128)(2,1)S(1)}, u32[]{:S(2)}, u32[]{:S(2)}) async-start(bf16[16,3,32,128]{3,2,1,0:T(8,128)(2,1)} %shard_map.77), calls=%async_computation.1 | async-start | bytes 786432 | tf_op jit(solution)/shard_map/all_to_all | solution.py:149
  50.8 46.7 %copy-start.2 = (f32[128,256]{1,0:T(8,128)S(1)}, f32[128,256]{1,0:T(8,128)}, u32[]{:S(2)}) copy-start(f32[128,256]{1,0:T(8,128)} %logits_ref.3) | copy-start | bytes 393220
  50.8 46.6 %copy-start.3 = (f32[128,256]{1,0:T(8,128)S(1)}, f32[128,256]{1,0:T(8,128)}, u32[]{:S(2)}) copy-start(f32[128,256]{1,0:T(8,128)} %first_ref.1) | copy-start | bytes 393220
  50.9 46.6 %copy-start.4 = (f32[128,256]{1,0:T(8,128)S(1)}, f32[128,256]{1,0:T(8,128)}, u32[]{:S(2)}) copy-start(f32[128,256]{1,0:T(8,128)} %second_ref.1) | copy-start | bytes 393220
  50.9 5.3 %collective-permute-start = (bf16[128,256]{1,0:T(8,128)(2,1)S(1)}, bf16[128,256]{1,0:T(8,128)(2,1)S(1)}, u32[]{:S(2)}, u32[]{:S(2)}) collective-permute-start(bf16[128,256]{1,0:T(8,128)(2,1)S(1)} %get-tuple-element.9), channel_id=1, source_target_pairs={{0,32},{32,0},{1,33},{33,1},{2,34},{34,2},{3,35},{35,3},{4,36},{36... | collective-permute-start | bytes 196616 | tf_op jit(solution)/shard_map/ppermute | solution.py:182

commit v2 on v1

--- a/solution.py
+++ b/solution.py
@@ -23,13 +23,14 @@
         body,
         out_shape=out_shape,
         in_specs=specs,
-        out_specs=jax.tree.map(lambda unused: VMEM, out_shape),
+        out_specs=jax.tree.map(lambda leaf: SMEM if leaf.dtype == jnp.int32 else VMEM, out_shape),
         scratch_shapes=scratch,
         compiler_params=pltpu.CompilerParams(vmem_limit_bytes=LIMIT),
     )(*operands)
 
 
-def relax_kernel(logits_ref, probs_ref, send_ref):
+def relax_kernel(place_ref, logits_ref, probs_ref, send_ref, same_place_ref):
+    same_place_ref[0] = place_ref[0]
     flipped = logits_ref[...].T
     copies = send_ref.shape[0]
     for attr in range(probs_ref.shape[0]):
@@ -46,7 +47,7 @@
 def select_kernel(triples_ref, full_ref, send_ref):
     for marg in range(send_ref.shape[0]):
         for which in range(3):
-            send_ref[marg, which] = full_ref[triples_ref[marg, which]]
+            send_ref[marg, which] = full_ref[triples_ref[which, marg]]
 
 
 def fill_pairs(src_ref, source, lanes, pairs_ref, first_ref, second_ref):
@@ -59,7 +60,10 @@
         pairs_ref[mod, :, lanes] = both.reshape(V * V // MODS, both.shape[2]).astype(jnp.bfloat16)
 
 
-def answer_kernel(src_ref, own_ref, send_ref, pairs_ref, third_ref, first_ref, second_ref):
+def answer_kernel(
+    place_ref, src_ref, own_ref, send_ref, same_place_ref, pairs_ref, third_ref, first_ref, second_ref
+):
+    same_place_ref[0] = place_ref[0]
     sources, unused, unused2, rows = src_ref.shape
 
     def fill(source, carry):
@@ -121,7 +125,7 @@
     total_ref[...] = jnp.zeros(total_ref.shape, jnp.float32)
     for marg in range(grads_ref.shape[0]):
         for which in range(3):
-            attr = triples_ref[marg, which]
+            attr = triples_ref[which, marg]
             total_ref[attr] = total_ref[attr] + grads_ref[marg, which].astype(jnp.float32)
     send_ref[...] = total_ref[...].astype(jnp.bfloat16)
 
@@ -157,21 +161,24 @@
     scale = cells / (rows * lax.axis_size(ROW_AXES))
     f32, low = jnp.float32, jnp.bfloat16
     shape = jax.ShapeDtypeStruct
-    probs, copies = call(
+    attributes = triples.T
+    place = lax.axis_index(SHARE_AXES).astype(jnp.int32).reshape(1)
+    scalar = shape((1,), jnp.int32)
+    probs, copies, place = call(
         relax_kernel,
-        (shape((attrs, V, rows), f32), shape((groups, attrs, V, rows), low)),
-        (logits,),
-        [VMEM],
+        (shape((attrs, V, rows), f32), shape((groups, attrs, V, rows), low), scalar),
+        (place, logits),
+        [SMEM, VMEM],
     )
     full = swap(copies, MARG_AXES).reshape(groups * attrs, V, rows)
-    picked = call(select_kernel, shape((margs, 3, V, rows), low), (triples, full), [SMEM, VMEM])
+    picked = call(select_kernel, shape((margs, 3, V, rows), low), (attributes, full), [SMEM, VMEM])
     sources = swap(picked, SHARE_AXES)
     tall, wide = V * V // MODS, V * MODS
-    own, send = call(
+    own, send, place = call(
         answer_kernel,
-        (shape((wide, tall), f32), shape((wide, tall), low)),
-        (sources,),
-        [VMEM],
+        (shape((wide, tall), f32), shape((wide, tall), low), scalar),
+        (place, sources),
+        [SMEM, VMEM],
         [
             pltpu.VMEM((MODS, tall, margs * rows), low),
             pltpu.VMEM((V, margs * rows), low),
@@ -180,8 +187,7 @@
         ],
     )
     other = lax.ppermute(send, "u", [(0, 1), (1, 0)])
-    place = lax.axis_index(SHARE_AXES)
-    target = lax.dynamic_slice_in_dim(targets, place, 1, 0).reshape(tall, wide)
+    target = lax.dynamic_slice_in_dim(targets, place[0], 1, 0).reshape(tall, wide)
     grads = call(
         lambda *refs: backward_kernel(scale, *refs),
         shape((margs, 3, V, rows), low),
@@ -201,7 +207,7 @@
     totals = call(
         collect_kernel,
         shape((groups * attrs, V, rows), low),
-        (triples, returned),
+        (attributes, returned),
         [SMEM, VMEM],
         [pltpu.VMEM((groups * attrs, V, rows), f32)],
     )

time: 98.8 us -> 99.7 us (level)
  blocking collectives: 35.4 us -> 78.9 us
  waiting for transfers between devices: 31.2 us -> 3.38 us
  starting transfers between devices: 17.1 us -> 1.11 us
  between operations: 0.7 us -> 2.73 us
    all_to_all x2 -> x4, blocking collectives: 35.4 us -> 78.9 us  [swap(): return lax.all_to_all(value, axes, 0, 0, tiled=True)]
    all_to_all x2 -> x0, waiting for transfers between devices: 27.2 us -> none  [swap(): return lax.all_to_all(value, axes, 0, 0, tiled=True)]
    all_to_all x2 -> x0, starting transfers between devices: 16 us -> none  [swap(): return lax.all_to_all(value, axes, 0, 0, tiled=True)]
  transfers between devices with their start and end apart: 3 -> 1, of which waited for: 3 -> 1; matrix products, arithmetic and copies ran while one was open for 1% -> 0% of each run, Pallas kernels for 0% -> 0%
where the time goes in v2:
time: 99.7 us; the launch traced here: 99.4 us
  blocking collectives  78.9 us (79%)
  Pallas kernels  11.4 us (11%)
  waiting for transfers between devices  3.38 us (3%)
  between operations  2.73 us (3%)
  local copies, waits for them, and re-layouts  1.86 us (2%)
  starting transfers between devices  1.11 us (1%)
    all_to_all x4, blocking collectives, swap(): return lax.all_to_all(value, axes, 0, 0, tiled=True)  78.9 us
    pallas_call x6, Pallas kernels, call(): pl.pallas_call(body, out_shape=out_shape, in_specs=specs, out_specs=jax.t...  11.4 us
    ppermute x1, waiting for transfers between devices, shards(): other = lax.ppermute(send, 'u', [(0, 1), (1, 0)])  3.38 us
  transfers between devices with their start and end apart: 1, of which 1 were waited for; matrix products, arithmetic and copies ran while one was open for 0% of the time, Pallas kernels for 0%

profile of v2, /device:TPU:32, one launch (start us, length us, event | category | flops | bytes accessed | tf_op | source)
XLA Modules:
  0.0 99.4 jit_solution(4013291381236581107)
XLA Ops:
  0.6 0.0 copy-start
  0.7 0.0 copy-start.1
  0.7 1.0 %copy-done.1 = f32[128,256]{1,0:T(8,128)S(1)} copy-done((f32[128,256]{1,0:T(8,128)S(1)}, f32[128,256]{1,0:T(8,128)}, u32[]{:S(2)}) %copy-start.1) | copy-done | bytes 131096
  1.7 0.5 shard_map.76
  2.2 29.6 %all_to_all.20 = bf16[8,8,32,128]{3,2,1,0:T(8,128)(2,1)S(1)} all-to-all(bf16[8,8,32,128]{3,2,1,0:T(8,128)(2,1)S(1)} %get-tuple-element.9), channel_id=1, replica_groups=mesh['x'=4,'u'=2,'w'=2,'c'=2,'y'=4,'h'=2] {'y','h'}, dimensions={0} | all-to-all | bytes 1048576 | tf_op jit(solution)/shard_map/all_to_all | solution.py:153
  31.8 0.0 copy-start.5
  31.8 0.7 copy-done.5
  32.5 0.0 copy-start.6
  32.5 0.6 shard_map.77
  33.1 13.9 %all_to_all.21.src_ref.refs_0_ = bf16[16,3,32,128]{3,2,1,0:T(8,128)(2,1)S(1)} all-to-all(bf16[16,3,32,128]{3,2,1,0:T(8,128)(2,1)S(1)} %shard_map.77), channel_id=1, replica_groups=mesh['x'=4,'u'=2,'w'=2,'c'=2,'y'=4,'h'=2] {'x','w','c'}, dimensions={0} | all-to-all | bytes 786432 | tf_op jit(solution)/shard_map/all_to_all | solution.py:153
  47.0 3.5 %shard_map.78 = (f32[128,256]{1,0:T(8,128)S(1)}, bf16[128,256]{1,0:T(8,128)(2,1)S(1)}, s32[1]{0:T(128)}) custom-call(s32[1]{0:T(128)} %get-tuple-element.10.place_ref, bf16[16,3,32,128]{3,2,1,0:T(8,128)(2,1)S(1)} %all_to_all.21.src_ref.refs_0_), custom_call_target="tpu_custom_call" | custom-call | tf_op jit(solution)/shard_map/pallas_call | solution.py:22
  50.5 0.0 copy-start.2
  50.5 0.0 copy-start.3
  50.6 0.0 copy-start.4
  51.9 1.1 %collective-permute-start = (bf16[128,256]{1,0:T(8,128)(2,1)S(1)}, bf16[128,256]{1,0:T(8,128)(2,1)S(1)}, u32[]{:S(2)}, u32[]{:S(2)}) collective-permute-start(bf16[128,256]{1,0:T(8,128)(2,1)S(1)} %get-tuple-element.12), channel_id=1, source_target_pairs={{0,32},{32,0},{1,33},{33,1},{2,34},{34,2},{3,35},{35,3},{4,36},{36... | collective-permute-start | bytes 196616 | tf_op jit(solution)/shard_map/ppermute | solution.py:189
  53.7 0.0 copy-done
  53.7 0.1 constant_dynamic-slice_fusion
  53.8 3.4 %collective-permute-done.refs_2_ = bf16[128,256]{1,0:T(8,128)(2,1)S(1)} collective-permute-done((bf16[128,256]{1,0:T(8,128)(2,1)S(1)}, bf16[128,256]{1,0:T(8,128)(2,1)S(1)}, u32[]{:S(2)}, u32[]{:S(2)}) %collective-permute-start) | collective-permute-done | bytes 65568 | tf_op jit(solution)/shard_map/ppermute | solution.py:189
  57.2 5.0 %shard_map.79 = bf16[16,3,32,128]{3,2,1,0:T(8,128)(2,1)S(1)} custom-call(bf16[16,3,32,128]{3,2,1,0:T(8,128)(2,1)S(1)} %all_to_all.21.src_ref.refs_0_, f32[128,256]{1,0:T(8,128)S(1)} %get-tuple-element.11.refs_1_, bf16[128,256]{1,0:T(8,128)(2,1)S(1)} %collective-permute-done.refs_2_, f32[256,128]{1,0:T(8,128)S(1)} %bitcast.8), custom_call_target="tpu_custom_call" | custom-call | tf_op jit(solution)/shard_map/pallas_call | solution.py:22
  62.2 12.8 %all_to_all.22.grads_ref = bf16[16,3,32,128]{3,2,1,0:T(8,128)(2,1)S(1)} all-to-all(bf16[16,3,32,128]{3,2,1,0:T(8,128)(2,1)S(1)} %shard_map.79), channel_id=1, replica_groups=mesh['x'=4,'u'=2,'w'=2,'c'=2,'y'=4,'h'=2] {'x','w','c'}, dimensions={0} | all-to-all | bytes 786432 | tf_op jit(solution)/shard_map/all_to_all | solution.py:153
  75.0 0.0 copy-done.6
  75.0 0.8 shard_map.80
  75.8 22.6 %all_to_all.23.parts_ref = bf16[8,8,32,128]{3,2,1,0:T(8,128)(2,1)S(1)} all-to-all(bf16[8,8,32,128]{3,2,1,0:T(8,128)(2,1)S(1)} %bitcast.7), channel_id=1, replica_groups=mesh['x'=4,'u'=2,'w'=2,'c'=2,'y'=4,'h'=2] {'y','h'}, dimensions={0} | all-to-all | bytes 1048576 | tf_op jit(solution)/shard_map/all_to_all | solution.py:153
  98.4 0.0 copy-done.2
  98.4 0.0 copy-done.3
  98.4 0.0 copy-done.4
  98.4 1.0 shard_map.81
Async XLA Ops:
  0.6 53.0 %copy-start = (f32[16,32768]{1,0:T(8,128)S(1)}, f32[16,32768]{1,0:T(8,128)}, u32[]{:S(2)}) copy-start(f32[16,32768]{1,0:T(8,128)} %param.8) | copy-start | bytes 6291460
  0.7 1.1 %copy-start.1 = (f32[128,256]{1,0:T(8,128)S(1)}, f32[128,256]{1,0:T(8,128)}, u32[]{:S(2)}) copy-start(f32[128,256]{1,0:T(8,128)} %logits_ref.3) | copy-start | bytes 393220
  31.8 0.7 copy-start.5
  32.5 42.5 %copy-start.6 = (s32[16,3]{0,1:T(4,128)S(1)}, s32[16,3]{0,1:T(4,128)}, u32[]{:S(2)}) copy-start(s32[16,3]{0,1:T(4,128)} %param.9) | copy-start | bytes 580
  50.5 47.9 %copy-start.2 = (f32[128,256]{1,0:T(8,128)S(1)}, f32[128,256]{1,0:T(8,128)}, u32[]{:S(2)}) copy-start(f32[128,256]{1,0:T(8,128)} %logits_ref.3) | copy-start | bytes 393220
  50.5 47.9 %copy-start.3 = (f32[128,256]{1,0:T(8,128)S(1)}, f32[128,256]{1,0:T(8,128)}, u32[]{:S(2)}) copy-start(f32[128,256]{1,0:T(8,128)} %first_ref.1) | copy-start | bytes 393220
  50.6 47.9 %copy-start.4 = (f32[128,256]{1,0:T(8,128)S(1)}, f32[128,256]{1,0:T(8,128)}, u32[]{:S(2)}) copy-start(f32[128,256]{1,0:T(8,128)} %second_ref.1) | copy-start | bytes 393220
  51.9 5.3 %collective-permute-start = (bf16[128,256]{1,0:T(8,128)(2,1)S(1)}, bf16[128,256]{1,0:T(8,128)(2,1)S(1)}, u32[]{:S(2)}, u32[]{:S(2)}) collective-permute-start(bf16[128,256]{1,0:T(8,128)(2,1)S(1)} %get-tuple-element.12), channel_id=1, source_target_pairs={{0,32},{32,0},{1,33},{33,1},{2,34},{34,2},{3,35},{35,3},{4,36},{36... | collective-permute-start | bytes 196616 | tf_op jit(solution)/shard_map/ppermute | solution.py:189

commit v3 on v1

v3 whole, which is shorter than its diff:
```python
import jax
import jax.numpy as jnp
from jax import lax
from jax.experimental import pallas as pl
from jax.experimental.pallas import tpu as pltpu
from jax.sharding import Mesh, PartitionSpec as P

V = 32
ADAM_STEP = 4
PARTS = (4, 2, 2, 2, 4, 2)
NAMES = ("x", "u", "w", "c", "y", "h")
ROW_AXES = ("x", "u", "w", "c")
MARG_AXES = ("y", "h")
PLACE_AXES = ("x", "w", "c")
SHARE_AXES = ("x", "w", "c", "y")
CHUNKS = 4
CHUNK = 32
LANES = CHUNKS * CHUNK
SUB = V // CHUNKS
MODS = 4
VMEM = pl.BlockSpec(memory_space=pltpu.VMEM)
SMEM = pl.BlockSpec(memory_space=pltpu.SMEM)
ANY = pl.BlockSpec(memory_space=pl.ANY)
LIMIT = 40 * 1024 * 1024
F32 = jnp.float32
LOW = jnp.bfloat16


def call(body, out_shape, operands, specs, scratch=()):
    return pl.pallas_call(
        body,
        out_shape=out_shape,
        in_specs=specs,
        out_specs=jax.tree.map(lambda unused: VMEM, out_shape),
        scratch_shapes=scratch,
        compiler_params=pltpu.CompilerParams(vmem_limit_bytes=LIMIT),
    )(*operands)


def exchange(blocks):
    lane = lax.broadcasted_iota(jnp.int32, blocks[0].shape, 1)
    blocks = list(blocks)
    for width, pairs in ((2 * CHUNK, ((0, 2), (1, 3))), (CHUNK, ((0, 1), (2, 3)))):
        low_part = (lane // width) % 2 == 0
        for a, b in pairs:
            left, right = blocks[a], blocks[b]
            blocks[a] = jnp.where(low_part, left, pltpu.roll(right, width, 1))
            blocks[b] = jnp.where(low_part, pltpu.roll(left, LANES - width, 1), right)
    return blocks


def relax_kernel(side_ref, triples_ref, logits_ref, target_ref, probs_ref, send_ref, triple_ref):
    flipped = logits_ref[...].T
    attrs = probs_ref.shape[0]
    halves = send_ref.shape[0] // CHUNKS
    for attr in range(attrs):
        block = flipped[attr * V : (attr + 1) * V, :]
        top = jnp.max(block, axis=0, keepdims=True)
        expo = jnp.exp(block - top)
        probs = expo / jnp.sum(expo, axis=0, keepdims=True)
        probs_ref[attr] = probs
        chunks = exchange([probs[part * SUB : (part + 1) * SUB, :] for part in range(CHUNKS)])
        for chunk in range(CHUNKS):
            low = chunks[chunk].astype(LOW)
            for half in range(halves):
                send_ref[chunk * halves + half, attr] = low
    triple_ref[...] = jnp.zeros(triple_ref.shape, F32)
    triple_ref[0:3, 0 : triples_ref.shape[1]] = triples_ref[...].astype(F32)
    for half in range(halves):
        mine = jnp.where(side_ref[0] == half, 1.0, 0.0)
        tile = (triple_ref[...] * mine).astype(LOW)
        for chunk in range(CHUNKS):
            send_ref[chunk * halves + half, attrs] = tile


def select_kernel(full_ref, send_ref, triples_ref, scalar_ref, sem):
    groups, slots = full_ref.shape[0], full_ref.shape[1]
    attrs = slots - 1
    halves = groups // CHUNKS
    for chunk in range(CHUNKS):
        tile = full_ref[chunk * halves, attrs].astype(F32)
        for half in range(1, halves):
            tile += full_ref[chunk * halves + half, attrs].astype(F32)
        triples_ref[chunk] = tile.astype(jnp.int32)
    copy = pltpu.make_async_copy(triples_ref, scalar_ref, sem)
    copy.start()
    copy.wait()

    def pick(place, carry):
        for chunk in range(CHUNKS):
            for which in range(3):
                attr = scalar_ref[chunk, which, place]
                send_ref[place * CHUNKS + chunk, which] = full_ref[attr // attrs, attr % attrs]
        return carry

    lax.fori_loop(0, send_ref.shape[0] // CHUNKS, pick, 0, unroll=4)


def unpack(src_ref, shard):
    packed = [src_ref[shard * CHUNKS + chunk].astype(F32).reshape(3 * SUB, LANES) for chunk in range(CHUNKS)]
    parts = exchange(packed)
    return [
        jnp.concatenate([part[which * SUB : (which + 1) * SUB, :] for part in parts], axis=0) for which in range(3)
    ]


def answer_kernel(src_ref, own_ref, send_ref, table_ref, pairs_ref):
    shards = table_ref.shape[0]

    def fill(step):
        for part in range(2):
            shard = 2 * step + part
            first, second, third = [value.astype(LOW) for value in unpack(src_ref, shard)]
            table_ref[shard, 0] = first
            table_ref[shard, 1] = second
            table_ref[shard, 2] = third
            for value in range(V):
                row = jnp.broadcast_to(second[value : value + 1, :], first.shape)
                mod, rest = value % MODS, value // MODS
                pairs_ref[step, mod, rest * V : (rest + 1) * V, part * LANES : (part + 1) * LANES] = first * row

    def add(step):
        third = jnp.concatenate([table_ref[2 * step, 2], table_ref[2 * step + 1, 2]], axis=1)
        for mod in range(MODS):
            own_ref[mod * V : (mod + 1) * V, :] += lax.dot_general(
                third, pairs_ref[step, mod], (((1,), (1,)), ((), ())), preferred_element_type=F32
            )

    own_ref[...] = jnp.zeros(own_ref.shape, F32)
    fill(0)

    def both(step, carry):
        add(step - 1)
        fill(step)
        return carry

    lax.fori_loop(1, shards // 2, both, 0)
    add(shards // 2 - 1)
    send_ref[...] = own_ref[...].astype(LOW)


def base_kernel(scale, own_ref, target_ref, base_ref):
    rows = [target_ref[pl.ds(rest, V, stride=SUB), :] for rest in range(SUB)]
    base_ref[...] = scale * own_ref[...] - jnp.concatenate(rows, axis=0).T


def backward_kernel(scale, table_ref, pairs_ref, base_ref, other_ref, out_ref, low_ref, mask_ref, row_ref, sum_ref):
    steps = pairs_ref.shape[0]
    wide = 2 * LANES
    resid = base_ref[...] + scale * other_ref[...].astype(F32)
    low_ref[...] = resid.astype(LOW)
    flipped = resid.T
    lane_mod = lax.broadcasted_iota(jnp.int32, flipped.shape, 1) // V
    for mod in range(MODS):
        mask_ref[mod] = jnp.where(lane_mod == mod, flipped, 0.0).astype(LOW)

    def step(index, carry):
        pair = [
            jnp.concatenate([table_ref[2 * index, which], table_ref[2 * index + 1, which]], axis=1)
            for which in range(3)
        ]
        first = pair[0].astype(F32)
        row_ref[...] = pair[1].astype(F32)
        stacked = jnp.concatenate([pair[2]] * MODS, axis=0)
        third_grad = jnp.zeros((V, wide), F32)
        first_grad = jnp.zeros((V, wide), F32)
        for mod in range(MODS):
            third_grad += jnp.dot(
                low_ref[mod * V : (mod + 1) * V, :], pairs_ref[index, mod], preferred_element_type=F32
            )
            cross = jnp.dot(mask_ref[mod], stacked, preferred_element_type=F32)
            for rest in range(SUB):
                value = rest * MODS + mod
                block = cross[rest * V : (rest + 1) * V, :]
                first_grad += block * row_ref[pl.ds(value, 1), :]
                product = block * first
                partial = product[0:8]
                for part in range(1, V // 8):
                    partial += product[8 * part : 8 * part + 8]
                for half in range(2):
                    sum_ref[half, value * 8 : value * 8 + 8, :] = partial[:, half * LANES : (half + 1) * LANES]
        for half in range(2):
            lanes = slice(half * LANES, (half + 1) * LANES)
            second_grad = jnp.zeros((V, LANES), F32)
            for part in range(8):
                second_grad += sum_ref[half, pl.ds(part, V, stride=8), :]
            grads = (first_grad[:, lanes], second_grad, third_grad[:, lanes])
            parts = [
                jnp.concatenate([grad[part * SUB : (part + 1) * SUB, :] for grad in grads], axis=0)
                for part in range(CHUNKS)
            ]
            for chunk, packed in enumerate(exchange(parts)):
                place = (2 * index + half) * CHUNKS + chunk
                out_ref[place] = packed.reshape(3, SUB, LANES).astype(LOW)
        return carry

    lax.fori_loop(0, steps, step, 0)


def collect_kernel(triples_ref, grads_ref, send_ref, total_ref):
    groups, attrs = send_ref.shape[0], send_ref.shape[1]
    total_ref[...] = jnp.zeros(total_ref.shape, F32)

    def add(place, carry):
        for chunk in range(CHUNKS):
            for which in range(3):
                attr = triples_ref[chunk, which, place]
                term = grads_ref[place * CHUNKS + chunk, which].astype(F32)
                total_ref[which, attr] = total_ref[which, attr] + term
        return carry

    lax.fori_loop(0, grads_ref.shape[0] // CHUNKS, add, 0, unroll=4)
    total = total_ref[0] + total_ref[1] + total_ref[2]
    send_ref[...] = total.reshape(groups, attrs, SUB, LANES).astype(LOW)


def adam_kernel(
    parts_ref, probs_ref, logits_ref, first_ref, second_ref, out_logits_ref, out_first_ref, out_second_ref, grad_ref
):
    groups, attrs = parts_ref.shape[0], parts_ref.shape[1]
    halves = groups // CHUNKS
    chunks = []
    for chunk in range(CHUNKS):
        total = parts_ref[chunk * halves].astype(F32)
        for half in range(1, halves):
            total += parts_ref[chunk * halves + half].astype(F32)
        chunks.append(total.reshape(attrs * SUB, LANES))
    parts = exchange(chunks)
    for attr in range(attrs):
        row_grad = jnp.concatenate([part[attr * SUB : (attr + 1) * SUB, :] for part in parts], axis=0)
        probs = probs_ref[attr]
        inner = jnp.sum(probs * row_grad, axis=0, keepdims=True)
        grad_ref[attr * V : (attr + 1) * V, :] = 512.0 * probs * (row_grad - inner)
    grad = grad_ref[...].T
    new_first = 0.9 * first_ref[...] + 0.1 * grad
    new_second = 0.999 * second_ref[...] + 0.001 * grad * grad
    first_hat = new_first / (1.0 - 0.9**ADAM_STEP)
    second_hat = new_second / (1.0 - 0.999**ADAM_STEP)
    out_logits_ref[...] = logits_ref[...] - 0.5 * first_hat / (jnp.sqrt(second_hat) + 1e-08)
    out_first_ref[...] = new_first
    out_second_ref[...] = new_second


def swap(value, axes):
    return lax.all_to_all(value, axes, 0, 0, tiled=True)


def answers(src):
    shape = jax.ShapeDtypeStruct
    shards = src.shape[0] // CHUNKS
    tall, wide = V * V // MODS, V * MODS
    return call(
        answer_kernel,
        (
            shape((wide, tall), F32),
            shape((wide, tall), LOW),
            shape((shards, 3, V, LANES), LOW),
            shape((shards // 2, MODS, tall, 2 * LANES), LOW),
        ),
        (src,),
        [VMEM],
    )


def backward(scale, table, pairs, base, other):
    shards = table.shape[0]
    tall, wide = V * V // MODS, V * MODS
    return call(
        lambda *refs: backward_kernel(scale, *refs),
        jax.ShapeDtypeStruct((shards * CHUNKS, 3, SUB, LANES), LOW),
        (table, pairs, base, other),
        [VMEM] * 4,
        [
            pltpu.VMEM((wide, tall), LOW),
            pltpu.VMEM((MODS, tall, wide), LOW),
            pltpu.VMEM((V, 2 * LANES), F32),
            pltpu.VMEM((2, 8 * V, LANES), F32),
        ],
    )


def shards(logits, first_moment, second_moment, targets, triples):
    rows, cols = logits.shape
    margs, cells = targets.shape
    attrs = cols // V
    groups = lax.axis_size(MARG_AXES)
    scale = cells / (rows * lax.axis_size(ROW_AXES))
    shape = jax.ShapeDtypeStruct
    tall, wide = V * V // MODS, V * MODS
    place = lax.axis_index(PLACE_AXES)
    target = lax.dynamic_slice_in_dim(targets, place, 1, 0).reshape(tall, wide)
    side = lax.axis_index("h").astype(jnp.int32).reshape(1)
    probs, copies = call(
        relax_kernel,
        (shape((attrs, V, rows), F32), shape((groups, attrs + 1, SUB, LANES), LOW)),
        (side, triples.T, logits, target),
        [SMEM, VMEM, VMEM, ANY],
        [pltpu.VMEM((SUB, LANES), F32)],
    )
    full = swap(copies, MARG_AXES)
    picked, attributes = call(
        select_kernel,
        (shape((margs * CHUNKS, 3, SUB, LANES), LOW), shape((CHUNKS, SUB, LANES), jnp.int32)),
        (full,),
        [VMEM],
        [pltpu.SMEM((CHUNKS, SUB, LANES), jnp.int32), pltpu.SemaphoreType.DMA],
    )
    own, send, table, pairs = answers(swap(picked, SHARE_AXES))
    other = lax.ppermute(send, "u", [(0, 1), (1, 0)])
    base = call(lambda *refs: base_kernel(scale, *refs), shape((wide, tall), F32), (own, target), [VMEM] * 2)
    returned = swap(backward(scale, table, pairs, base, other), SHARE_AXES)
    totals = call(
        collect_kernel,
        shape((groups, attrs, SUB, LANES), LOW),
        (attributes, returned),
        [SMEM, VMEM],
        [pltpu.VMEM((3, groups * attrs, SUB, LANES), F32)],
    )
    return call(
        adam_kernel,
        (shape((rows, cols), F32),) * 3,
        (swap(totals, MARG_AXES), probs, logits, first_moment, second_moment),
        [VMEM] * 5,
        [pltpu.VMEM((cols, rows), F32)],
    )


def solution(mesh):
    fine = Mesh(mesh.devices.reshape(PARTS), NAMES)
    table = P(ROW_AXES, MARG_AXES)
    listed = P(MARG_AXES, None)
    return jax.shard_map(
        shards,
        mesh=fine,
        in_specs=(table, table, table, listed, listed),
        out_specs=(table, table, table),
        check_vma=False,
    )
```

time: 98.8 us -> 89.3 us (0.904)
  blocking collectives: 35.4 us -> 68.2 us
  waiting for transfers between devices: 31.2 us -> 4.07 us
  starting transfers between devices: 17.1 us -> 1.08 us
  local copies, waits for them, and re-layouts: 1.94 us -> 3.27 us
    all_to_all x2 -> x4, blocking collectives: 35.4 us -> 68.2 us  [swap(): return lax.all_to_all(value, axes, 0, 0, tiled=True)]
    all_to_all x2 -> x0, waiting for transfers between devices: 27.2 us -> none  [swap(): return lax.all_to_all(value, axes, 0, 0, tiled=True)]
    all_to_all x2 -> x0, starting transfers between devices: 16 us -> none  [swap(): return lax.all_to_all(value, axes, 0, 0, tiled=True)]
    unnamed x11 -> x12, local copies, waits for them, and re-layouts: 1.84 us -> 3.17 us
    pallas_call x6 -> x7, Pallas kernels: 12.1 us -> 11.6 us  [call(): pl.pallas_call(body, out_shape=out_shape, in_specs=specs, out_specs=jax.t...]
  transfers between devices with their start and end apart: 3 -> 1, of which waited for: 3 -> 1; matrix products, arithmetic and copies ran while one was open for 1% -> 0% of each run, Pallas kernels for 0% -> 0%
where the time goes in v3:
time: 89.3 us; the launch traced here: 89 us
  blocking collectives  68.2 us (76%)
  Pallas kernels  11.6 us (13%)
  waiting for transfers between devices  4.07 us (5%)
  local copies, waits for them, and re-layouts  3.27 us (4%)
  starting transfers between devices  1.08 us (1%)
    all_to_all x4, blocking collectives, swap(): return lax.all_to_all(value, axes, 0, 0, tiled=True)  68.2 us
    pallas_call x7, Pallas kernels, call(): pl.pallas_call(body, out_shape=out_shape, in_specs=specs, out_specs=jax.t...  11.6 us
    ppermute x1, waiting for transfers between devices, shards(): other = lax.ppermute(send, 'u', [(0, 1), (1, 0)])  4.07 us
    unnamed x12, local copies, waits for them, and re-layouts  3.17 us
  transfers between devices with their start and end apart: 1, of which 1 were waited for; matrix products, arithmetic and copies ran while one was open for 0% of the time, Pallas kernels for 0%

profile of v3, /device:TPU:32, one launch (start us, length us, event | category | flops | bytes accessed | tf_op | source)
XLA Modules:
  0.0 89.0 jit_solution(12029767526898866085)
XLA Ops:
  0.6 0.0 copy-start
  0.7 1.6 %copy-done = f32[16,32768]{1,0:T(8,128)S(1)} copy-done((f32[16,32768]{1,0:T(8,128)S(1)}, f32[16,32768]{1,0:T(8,128)}, u32[]{:S(2)}) %copy-start) | copy-done | bytes 2097176
  2.2 0.1 constant_dynamic-slice_fusion
  2.3 0.0 copy-start.1
  2.3 0.9 %copy-done.1 = f32[128,256]{1,0:T(8,128)S(1)} copy-done((f32[128,256]{1,0:T(8,128)S(1)}, f32[128,256]{1,0:T(8,128)}, u32[]{:S(2)}) %copy-start.1) | copy-done | bytes 131096
  3.2 0.0 copy-start.5
  3.2 0.7 copy-done.5
  3.9 0.3 shard_map.76
  4.2 21.6 %all_to_all.20.full_ref = bf16[8,9,8,128]{3,2,1,0:T(8,128)(2,1)S(1)} all-to-all(bf16[8,9,8,128]{3,2,1,0:T(8,128)(2,1)S(1)} %get-tuple-element.11), channel_id=1, replica_groups=mesh['x'=4,'u'=2,'w'=2,'c'=2,'y'=4,'h'=2] {'y','h'}, dimensions={0} | all-to-all | bytes 294912 | tf_op jit(solution)/shard_map/all_to_all | solution.py:245
  25.8 2.2 %shard_map.77 = (bf16[64,3,8,128]{3,2,1,0:T(8,128)(2,1)S(1)}, s32[4,8,128]{2,1,0:T(8,128)S(1)}) custom-call(bf16[8,9,8,128]{3,2,1,0:T(8,128)(2,1)S(1)} %all_to_all.20.full_ref), custom_call_target="tpu_custom_call" | custom-call | tf_op jit(solution)/shard_map/pallas_call | solution.py:30
  28.0 16.4 %all_to_all.21.src_ref = bf16[64,3,8,128]{3,2,1,0:T(8,128)(2,1)S(1)} all-to-all(bf16[64,3,8,128]{3,2,1,0:T(8,128)(2,1)S(1)} %get-tuple-element.13), channel_id=1, replica_groups=mesh['x'=4,'u'=2,'w'=2,'c'=2,'y'=4,'h'=2] {'x','w','c','y'}, dimensions={0} | all-to-all | bytes 786432 | tf_op jit(solution)/shard_map/all_to_all | solution.py:245
  44.5 2.4 %shard_map.78 = (f32[128,256]{1,0:T(8,128)S(1)}, bf16[128,256]{1,0:T(8,128)(2,1)S(1)}, bf16[16,3,32,128]{3,2,1,0:T(8,128)(2,1)S(1)}, bf16[8,4,256,256]{3,2,1,0:T(8,128)(2,1)S(1)}) custom-call(bf16[64,3,8,128]{3,2,1,0:T(8,128)(2,1)S(1)} %all_to_all.21.src_ref), custom_call_target="tpu_custom_call" | custom-call | tf_op jit(solution)/shard_map/pallas_call | solution.py:30
  46.8 1.1 %collective-permute-start = (bf16[128,256]{1,0:T(8,128)(2,1)S(1)}, bf16[128,256]{1,0:T(8,128)(2,1)S(1)}, u32[]{:S(2)}, u32[]{:S(2)}) collective-permute-start(bf16[128,256]{1,0:T(8,128)(2,1)S(1)} %get-tuple-element.17), channel_id=1, source_target_pairs={{0,32},{32,0},{1,33},{33,1},{2,34},{34,2},{3,35},{35,3},{4,36},{36... | collective-permute-start | bytes 196616 | tf_op jit(solution)/shard_map/ppermute | solution.py:309
  47.9 0.1 shard_map.79.refs_2_
  48.0 4.1 %collective-permute-done.refs_3_ = bf16[128,256]{1,0:T(8,128)(2,1)S(1)} collective-permute-done((bf16[128,256]{1,0:T(8,128)(2,1)S(1)}, bf16[128,256]{1,0:T(8,128)(2,1)S(1)}, u32[]{:S(2)}, u32[]{:S(2)}) %collective-permute-start) | collective-permute-done | bytes 65568 | tf_op jit(solution)/shard_map/ppermute | solution.py:309
  52.1 0.0 copy-start.2
  52.1 0.0 copy-start.3
  52.1 0.0 copy-start.4
  52.1 4.1 %shard_map.80 = bf16[64,3,8,128]{3,2,1,0:T(8,128)(2,1)S(1)} custom-call(bf16[16,3,32,128]{3,2,1,0:T(8,128)(2,1)S(1)} %get-tuple-element.14.refs_0_, bf16[8,4,256,256]{3,2,1,0:T(8,128)(2,1)S(1)} %get-tuple-element.15.refs_1_, f32[128,256]{1,0:T(8,128)S(1)} %shard_map.79.refs_2_, bf16[128,256]{1,0:T(8,128)(2,1)S(1)} %collective-permute-done.refs_3_), custom_call_target="tpu_custom_call" | custom-call | tf_op jit(solution)/shard_map/pallas_call | solution.py:30
  56.3 16.0 %all_to_all.22.grads_ref = bf16[64,3,8,128]{3,2,1,0:T(8,128)(2,1)S(1)} all-to-all(bf16[64,3,8,128]{3,2,1,0:T(8,128)(2,1)S(1)} %shard_map.80), channel_id=1, replica_groups=mesh['x'=4,'u'=2,'w'=2,'c'=2,'y'=4,'h'=2] {'x','w','c','y'}, dimensions={0} | all-to-all | bytes 786432 | tf_op jit(solution)/shard_map/all_to_all | solution.py:245
  72.3 1.5 %shard_map.81 = bf16[8,8,8,128]{3,2,1,0:T(8,128)(2,1)S(1)} custom-call(s32[4,8,128]{2,1,0:T(8,128)S(1)} %get-tuple-element.12.triples_ref, bf16[64,3,8,128]{3,2,1,0:T(8,128)(2,1)S(1)} %all_to_all.22.grads_ref), custom_call_target="tpu_custom_call" | custom-call | tf_op jit(solution)/shard_map/pallas_call | solution.py:30
  73.8 14.1 %all_to_all.23.parts_ref = bf16[8,8,8,128]{3,2,1,0:T(8,128)(2,1)S(1)} all-to-all(bf16[8,8,8,128]{3,2,1,0:T(8,128)(2,1)S(1)} %shard_map.81), channel_id=1, replica_groups=mesh['x'=4,'u'=2,'w'=2,'c'=2,'y'=4,'h'=2] {'y','h'}, dimensions={0} | all-to-all | bytes 262144 | tf_op jit(solution)/shard_map/all_to_all | solution.py:245
  88.0 0.0 copy-done.2
  88.0 0.0 copy-done.3
  88.0 0.0 copy-done.4
  88.0 1.1 %shard_map.82 = (f32[128,256]{1,0:T(8,128)}, f32[128,256]{1,0:T(8,128)}, f32[128,256]{1,0:T(8,128)}) custom-call(bf16[8,8,8,128]{3,2,1,0:T(8,128)(2,1)S(1)} %all_to_all.23.parts_ref, f32[8,32,128]{2,1,0:T(8,128)S(1)} %get-tuple-element.18.probs_ref, f32[128,256]{1,0:T(8,128)S(1)} %copy-done.2, f32[128,256]{1,0:T(8,128)S(1)} %copy-done.3, ...), custom_call_target="tpu_custom_call" | custom-call | tf_op jit(solution)/shard_map/pallas_call | solution.py:30
Async XLA Ops:
  0.6 1.6 %copy-start = (f32[16,32768]{1,0:T(8,128)S(1)}, f32[16,32768]{1,0:T(8,128)}, u32[]{:S(2)}) copy-start(f32[16,32768]{1,0:T(8,128)} %param.8) | copy-start | bytes 6291460
  2.3 0.9 %copy-start.1 = (f32[128,256]{1,0:T(8,128)S(1)}, f32[128,256]{1,0:T(8,128)}, u32[]{:S(2)}) copy-start(f32[128,256]{1,0:T(8,128)} %logits_ref.3) | copy-start | bytes 393220
  3.2 0.7 copy-start.5
  46.8 5.3 %collective-permute-start = (bf16[128,256]{1,0:T(8,128)(2,1)S(1)}, bf16[128,256]{1,0:T(8,128)(2,1)S(1)}, u32[]{:S(2)}, u32[]{:S(2)}) collective-permute-start(bf16[128,256]{1,0:T(8,128)(2,1)S(1)} %get-tuple-element.17), channel_id=1, source_target_pairs={{0,32},{32,0},{1,33},{33,1},{2,34},{34,2},{3,35},{35,3},{4,36},{36... | collective-permute-start | bytes 196616 | tf_op jit(solution)/shard_map/ppermute | solution.py:309
  52.1 35.9 %copy-start.2 = (f32[128,256]{1,0:T(8,128)S(1)}, f32[128,256]{1,0:T(8,128)}, u32[]{:S(2)}) copy-start(f32[128,256]{1,0:T(8,128)} %logits_ref.3) | copy-start | bytes 393220
  52.1 35.9 %copy-start.3 = (f32[128,256]{1,0:T(8,128)S(1)}, f32[128,256]{1,0:T(8,128)}, u32[]{:S(2)}) copy-start(f32[128,256]{1,0:T(8,128)} %first_ref.1) | copy-start | bytes 393220
  52.1 35.9 %copy-start.4 = (f32[128,256]{1,0:T(8,128)S(1)}, f32[128,256]{1,0:T(8,128)}, u32[]{:S(2)}) copy-start(f32[128,256]{1,0:T(8,128)} %second_ref.1) | copy-start | bytes 393220

commit v4 on v3

--- a/solution.py
+++ b/solution.py
@@ -22,18 +22,19 @@
 SMEM = pl.BlockSpec(memory_space=pltpu.SMEM)
 ANY = pl.BlockSpec(memory_space=pl.ANY)
 LIMIT = 40 * 1024 * 1024
+HIGH_LIMIT = 60 * 1024 * 1024
 F32 = jnp.float32
 LOW = jnp.bfloat16
 
 
-def call(body, out_shape, operands, specs, scratch=()):
+def call(body, out_shape, operands, specs, scratch=(), limit=LIMIT):
     return pl.pallas_call(
         body,
         out_shape=out_shape,
         in_specs=specs,
         out_specs=jax.tree.map(lambda unused: VMEM, out_shape),
         scratch_shapes=scratch,
-        compiler_params=pltpu.CompilerParams(vmem_limit_bytes=LIMIT),
+        compiler_params=pltpu.CompilerParams(vmem_limit_bytes=limit),
     )(*operands)
 
 
@@ -49,7 +50,15 @@
     return blocks
 
 
-def relax_kernel(side_ref, triples_ref, logits_ref, target_ref, probs_ref, send_ref, triple_ref):
+def relax_kernel(
+    place_ref, triples_any, logits_any, probs_ref, send_ref, triple_ref, triples_ref, logits_ref, triples_sem, logits_sem
+):
+    triples_copy = pltpu.make_async_copy(triples_any, triples_ref, triples_sem)
+    logits_copy = pltpu.make_async_copy(logits_any, logits_ref, logits_sem)
+    logits_copy.start()
+    triples_copy.start()
+    logits_copy.wait()
+    triples_copy.wait()
     flipped = logits_ref[...].T
     attrs = probs_ref.shape[0]
     halves = send_ref.shape[0] // CHUNKS
@@ -67,33 +76,29 @@
     triple_ref[...] = jnp.zeros(triple_ref.shape, F32)
     triple_ref[0:3, 0 : triples_ref.shape[1]] = triples_ref[...].astype(F32)
     for half in range(halves):
-        mine = jnp.where(side_ref[0] == half, 1.0, 0.0)
+        mine = jnp.where(place_ref[1] == half, 1.0, 0.0)
         tile = (triple_ref[...] * mine).astype(LOW)
         for chunk in range(CHUNKS):
             send_ref[chunk * halves + half, attrs] = tile
 
 
-def select_kernel(full_ref, send_ref, triples_ref, scalar_ref, sem):
-    groups, slots = full_ref.shape[0], full_ref.shape[1]
-    attrs = slots - 1
-    halves = groups // CHUNKS
+def select_kernel(full_ref, send_ref, triples_ref, index_ref, scalar_ref, sem):
+    slots = full_ref.shape[0] // (2 * CHUNKS)
+    places = send_ref.shape[0] // CHUNKS
+    triples = jnp.zeros(triples_ref.shape, F32)
     for chunk in range(CHUNKS):
-        tile = full_ref[chunk * halves, attrs].astype(F32)
-        for half in range(1, halves):
-            tile += full_ref[chunk * halves + half, attrs].astype(F32)
-        triples_ref[chunk] = tile.astype(jnp.int32)
-    copy = pltpu.make_async_copy(triples_ref, scalar_ref, sem)
+        tile = full_ref[2 * chunk * slots + slots - 1].astype(F32) + full_ref[(2 * chunk + 2) * slots - 1].astype(F32)
+        triples += pltpu.roll(tile, chunk * places, 1) if chunk else tile
+    attrs = triples.astype(jnp.int32)
+    triples_ref[...] = attrs
+    index_ref[...] = attrs + attrs // (slots - 1)
+    copy = pltpu.make_async_copy(index_ref, scalar_ref, sem)
     copy.start()
     copy.wait()
-
-    def pick(place, carry):
+    for place in range(places):
         for chunk in range(CHUNKS):
             for which in range(3):
-                attr = scalar_ref[chunk, which, place]
-                send_ref[place * CHUNKS + chunk, which] = full_ref[attr // attrs, attr % attrs]
-        return carry
-
-    lax.fori_loop(0, send_ref.shape[0] // CHUNKS, pick, 0, unroll=4)
+                send_ref[place * CHUNKS + chunk, which] = full_ref[scalar_ref[which, chunk * places + place]]
 
 
 def unpack(src_ref, shard):
@@ -134,14 +139,24 @@
         fill(step)
         return carry
 
-    lax.fori_loop(1, shards // 2, both, 0)
+    lax.fori_loop(1, shards // 2, both, 0, unroll=shards // 2 - 1)
     add(shards // 2 - 1)
     send_ref[...] = own_ref[...].astype(LOW)
 
 
-def base_kernel(scale, own_ref, target_ref, base_ref):
-    rows = [target_ref[pl.ds(rest, V, stride=SUB), :] for rest in range(SUB)]
-    base_ref[...] = scale * own_ref[...] - jnp.concatenate(rows, axis=0).T
+def base_kernel(scale, place_ref, own_ref, targets_any, base_ref, block_ref, target_ref, sem):
+    place = place_ref[0]
+    start = pl.multiple_of(place // 8 * 8, 8)
+    copy = pltpu.make_async_copy(targets_any.at[pl.ds(start, 8), :], block_ref, sem)
+    copy.start()
+    copy.wait()
+    mine = lax.broadcasted_iota(jnp.int32, (8, LANES), 0) == lax.rem(place, 8)
+    for rest in range(SUB):
+        for value in range(V):
+            tile = block_ref[:, pl.ds((value * SUB + rest) * LANES, LANES)]
+            row = jnp.sum(jnp.where(mine, tile, 0.0), axis=0, keepdims=True)
+            target_ref[pl.ds(rest * V + value, 1), :] = row
+    base_ref[...] = scale * own_ref[...] - target_ref[...].T
 
 
 def backward_kernel(scale, table_ref, pairs_ref, base_ref, other_ref, out_ref, low_ref, mask_ref, row_ref, sum_ref):
@@ -194,23 +209,20 @@
                 out_ref[place] = packed.reshape(3, SUB, LANES).astype(LOW)
         return carry
 
-    lax.fori_loop(0, steps, step, 0)
-
-
-def collect_kernel(triples_ref, grads_ref, send_ref, total_ref):
+    lax.fori_loop(0, steps, step, 0, unroll=steps)
+
+
+def collect_kernel(triples_ref, grads_ref, send_ref, *total_refs):
     groups, attrs = send_ref.shape[0], send_ref.shape[1]
-    total_ref[...] = jnp.zeros(total_ref.shape, F32)
-
-    def add(place, carry):
+    places = grads_ref.shape[0] // CHUNKS
+    for total_ref in total_refs:
+        total_ref[...] = jnp.zeros(total_ref.shape, F32)
+    for place in range(places):
         for chunk in range(CHUNKS):
-            for which in range(3):
-                attr = triples_ref[chunk, which, place]
-                term = grads_ref[place * CHUNKS + chunk, which].astype(F32)
-                total_ref[which, attr] = total_ref[which, attr] + term
-        return carry
-
-    lax.fori_loop(0, grads_ref.shape[0] // CHUNKS, add, 0, unroll=4)
-    total = total_ref[0] + total_ref[1] + total_ref[2]
+            for which, total_ref in enumerate(total_refs):
+                attr = triples_ref[which, chunk * places + place]
+                total_ref[attr] = total_ref[attr] + grads_ref[place * CHUNKS + chunk, which].astype(F32)
+    total = total_refs[0][...] + total_refs[1][...] + total_refs[2][...]
     send_ref[...] = total.reshape(groups, attrs, SUB, LANES).astype(LOW)
 
 
@@ -287,34 +299,45 @@
     scale = cells / (rows * lax.axis_size(ROW_AXES))
     shape = jax.ShapeDtypeStruct
     tall, wide = V * V // MODS, V * MODS
-    place = lax.axis_index(PLACE_AXES)
-    target = lax.dynamic_slice_in_dim(targets, place, 1, 0).reshape(tall, wide)
-    side = lax.axis_index("h").astype(jnp.int32).reshape(1)
+    place = jnp.stack([lax.axis_index(PLACE_AXES), lax.axis_index("h")]).astype(jnp.int32)
     probs, copies = call(
         relax_kernel,
         (shape((attrs, V, rows), F32), shape((groups, attrs + 1, SUB, LANES), LOW)),
-        (side, triples.T, logits, target),
-        [SMEM, VMEM, VMEM, ANY],
-        [pltpu.VMEM((SUB, LANES), F32)],
+        (place, triples.T, logits),
+        [SMEM, ANY, ANY],
+        [
+            pltpu.VMEM((SUB, LANES), F32),
+            pltpu.VMEM((3, margs), jnp.int32),
+            pltpu.VMEM((rows, cols), F32),
+            pltpu.SemaphoreType.DMA,
+            pltpu.SemaphoreType.DMA,
+        ],
+        HIGH_LIMIT,
     )
     full = swap(copies, MARG_AXES)
     picked, attributes = call(
         select_kernel,
-        (shape((margs * CHUNKS, 3, SUB, LANES), LOW), shape((CHUNKS, SUB, LANES), jnp.int32)),
-        (full,),
+        (shape((margs * CHUNKS, 3, SUB, LANES), LOW), shape((SUB, LANES), jnp.int32)),
+        (full.reshape(groups * (attrs + 1), SUB, LANES),),
         [VMEM],
-        [pltpu.SMEM((CHUNKS, SUB, LANES), jnp.int32), pltpu.SemaphoreType.DMA],
+        [pltpu.VMEM((SUB, LANES), jnp.int32), pltpu.SMEM((SUB, LANES), jnp.int32), pltpu.SemaphoreType.DMA],
     )
     own, send, table, pairs = answers(swap(picked, SHARE_AXES))
     other = lax.ppermute(send, "u", [(0, 1), (1, 0)])
-    base = call(lambda *refs: base_kernel(scale, *refs), shape((wide, tall), F32), (own, target), [VMEM] * 2)
+    base = call(
+        lambda *refs: base_kernel(scale, *refs),
+        shape((wide, tall), F32),
+        (place, own, targets),
+        [SMEM, VMEM, ANY],
+        [pltpu.VMEM((8, cells), F32), pltpu.VMEM((tall, wide), F32), pltpu.SemaphoreType.DMA],
+    )
     returned = swap(backward(scale, table, pairs, base, other), SHARE_AXES)
     totals = call(
         collect_kernel,
         shape((groups, attrs, SUB, LANES), LOW),
         (attributes, returned),
         [SMEM, VMEM],
-        [pltpu.VMEM((3, groups * attrs, SUB, LANES), F32)],
+        [pltpu.VMEM((groups * attrs, SUB, LANES), F32)] * 3,
     )
     return call(
         adam_kernel,

time: 89.3 us -> 84.8 us (0.950)
  waiting for transfers between devices: 4.07 us -> 0.9 us
  Pallas kernels: 11.6 us -> 10.4 us
  local copies, waits for them, and re-layouts: 3.27 us -> 2.26 us
    ppermute x1, waiting for transfers between devices: 4.07 us -> 0.9 us  [shards(): other = lax.ppermute(send, 'u', [(0, 1), (1, 0)])]
    pallas_call x7, Pallas kernels: 11.6 us -> 10.4 us  [call(): pl.pallas_call(body, out_shape=out_shape, in_specs=specs, out_specs=jax.t...]
    unnamed x12, local copies, waits for them, and re-layouts: 3.17 us -> 2.26 us
  transfers between devices with their start and end apart: 1 -> 1, of which waited for: 1 -> 1; matrix products, arithmetic and copies ran while one was open for 0% -> 0% of each run, Pallas kernels for 0% -> 1%
where the time goes in v4:
time: 84.8 us; the launch traced here: 84.4 us
  blocking collectives  68.5 us (81%)
  Pallas kernels  10.4 us (12%)
  local copies, waits for them, and re-layouts  2.26 us (3%)
  starting transfers between devices  1.08 us (1%)
  waiting for transfers between devices  0.9 us (1%)
    all_to_all x4, blocking collectives, swap(): return lax.all_to_all(value, axes, 0, 0, tiled=True)  68.5 us
    pallas_call x7, Pallas kernels, call(): pl.pallas_call(body, out_shape=out_shape, in_specs=specs, out_specs=jax.t...  10.4 us
    unnamed x12, local copies, waits for them, and re-layouts  2.26 us
  transfers between devices with their start and end apart: 1, of which 1 were waited for; matrix products, arithmetic and copies ran while one was open for 0% of the time, Pallas kernels for 1%

profile of v4, /device:TPU:32, one launch (start us, length us, event | category | flops | bytes accessed | tf_op | source)
XLA Modules:
  0.0 84.4 jit_solution(75855717591999191)
XLA Ops:
  0.6 0.6 pad_add_fusion.place_ref.refs_0_
  1.2 2.5 %shard_map.76 = (f32[8,32,128]{2,1,0:T(8,128)}, bf16[8,9,8,128]{3,2,1,0:T(8,128)(2,1)}) custom-call(s32[2]{0:T(128)} %pad_add_fusion.place_ref.refs_0_, s32[3,16]{1,0:T(4,128)} %bitcast.5, f32[128,256]{1,0:T(8,128)} %logits_ref.1), custom_call_target="tpu_custom_call" | custom-call | tf_op jit(solution)/shard_map/pallas_call | solution.py:31
  3.7 21.9 %all_to_all.20 = bf16[8,9,8,128]{3,2,1,0:T(8,128)(2,1)S(1)} all-to-all(bf16[8,9,8,128]{3,2,1,0:T(8,128)(2,1)} %get-tuple-element.11), channel_id=1, replica_groups=mesh['x'=4,'u'=2,'w'=2,'c'=2,'y'=4,'h'=2] {'y','h'}, dimensions={0} | all-to-all | bytes 294912 | tf_op jit(solution)/shard_map/all_to_all | solution.py:257
  25.6 0.9 %shard_map.77 = (bf16[64,3,8,128]{3,2,1,0:T(8,128)(2,1)S(1)}, s32[8,128]{1,0:T(8,128)S(1)}) custom-call(bf16[72,8,128]{2,1,0:T(8,128)(2,1)S(1)} %bitcast.4), custom_call_target="tpu_custom_call" | custom-call | tf_op jit(solution)/shard_map/pallas_call | solution.py:31
  26.5 16.4 %all_to_all.21.src_ref = bf16[64,3,8,128]{3,2,1,0:T(8,128)(2,1)S(1)} all-to-all(bf16[64,3,8,128]{3,2,1,0:T(8,128)(2,1)S(1)} %get-tuple-element.13), channel_id=1, replica_groups=mesh['x'=4,'u'=2,'w'=2,'c'=2,'y'=4,'h'=2] {'x','w','c','y'}, dimensions={0} | all-to-all | bytes 786432 | tf_op jit(solution)/shard_map/all_to_all | solution.py:257
  42.9 1.6 %shard_map.78 = (f32[128,256]{1,0:T(8,128)S(1)}, bf16[128,256]{1,0:T(8,128)(2,1)S(1)}, bf16[16,3,32,128]{3,2,1,0:T(8,128)(2,1)S(1)}, bf16[8,4,256,256]{3,2,1,0:T(8,128)(2,1)S(1)}) custom-call(bf16[64,3,8,128]{3,2,1,0:T(8,128)(2,1)S(1)} %all_to_all.21.src_ref), custom_call_target="tpu_custom_call" | custom-call | tf_op jit(solution)/shard_map/pallas_call | solution.py:31
  44.6 1.1 %collective-permute-start = (bf16[128,256]{1,0:T(8,128)(2,1)S(1)}, bf16[128,256]{1,0:T(8,128)(2,1)S(1)}, u32[]{:S(2)}, u32[]{:S(2)}) collective-permute-start(bf16[128,256]{1,0:T(8,128)(2,1)S(1)} %get-tuple-element.17), channel_id=1, source_target_pairs={{0,32},{32,0},{1,33},{33,1},{2,34},{34,2},{3,35},{35,3},{4,36},{36... | collective-permute-start | bytes 196616 | tf_op jit(solution)/shard_map/ppermute | solution.py:326
  45.6 0.0 copy-start
  45.6 1.6 %copy-done = f32[16,32768]{1,0:T(8,128)S(1)} copy-done((f32[16,32768]{1,0:T(8,128)S(1)}, f32[16,32768]{1,0:T(8,128)}, u32[]{:S(2)}) %copy-start) | copy-done | bytes 2097176
  47.2 0.0 copy-start.5
  47.2 0.7 copy-done.5
  47.9 0.0 copy-start.1
  47.9 0.0 copy-start.2
  47.9 0.0 copy-start.3
  47.9 0.0 copy-start.4
  47.9 1.0 %shard_map.79.refs_2_ = f32[128,256]{1,0:T(8,128)S(1)} custom-call(s32[2]{0:T(128)S(1)} %copy-done.5, f32[128,256]{1,0:T(8,128)S(1)} %get-tuple-element.16.refs_1_, f32[16,32768]{1,0:T(8,128)S(1)} %copy-done), custom_call_target="tpu_custom_call" | custom-call | tf_op jit(solution)/shard_map/pallas_call | solution.py:31
  48.9 0.9 %collective-permute-done.refs_3_ = bf16[128,256]{1,0:T(8,128)(2,1)S(1)} collective-permute-done((bf16[128,256]{1,0:T(8,128)(2,1)S(1)}, bf16[128,256]{1,0:T(8,128)(2,1)S(1)}, u32[]{:S(2)}, u32[]{:S(2)}) %collective-permute-start) | collective-permute-done | bytes 65568 | tf_op jit(solution)/shard_map/ppermute | solution.py:326
  49.8 2.3 %shard_map.80 = bf16[64,3,8,128]{3,2,1,0:T(8,128)(2,1)S(1)} custom-call(bf16[16,3,32,128]{3,2,1,0:T(8,128)(2,1)S(1)} %get-tuple-element.14.refs_0_, bf16[8,4,256,256]{3,2,1,0:T(8,128)(2,1)S(1)} %get-tuple-element.15.refs_1_, f32[128,256]{1,0:T(8,128)S(1)} %shard_map.79.refs_2_, bf16[128,256]{1,0:T(8,128)(2,1)S(1)} %collective-permute-done.refs_3_), custom_call_target="tpu_custom_call" | custom-call | tf_op jit(solution)/shard_map/pallas_call | solution.py:31
  52.1 16.0 %all_to_all.22.grads_ref = bf16[64,3,8,128]{3,2,1,0:T(8,128)(2,1)S(1)} all-to-all(bf16[64,3,8,128]{3,2,1,0:T(8,128)(2,1)S(1)} %shard_map.80), channel_id=1, replica_groups=mesh['x'=4,'u'=2,'w'=2,'c'=2,'y'=4,'h'=2] {'x','w','c','y'}, dimensions={0} | all-to-all | bytes 786432 | tf_op jit(solution)/shard_map/all_to_all | solution.py:257
  68.2 1.0 %shard_map.81 = bf16[8,8,8,128]{3,2,1,0:T(8,128)(2,1)S(1)} custom-call(s32[8,128]{1,0:T(8,128)S(1)} %get-tuple-element.12.triples_ref, bf16[64,3,8,128]{3,2,1,0:T(8,128)(2,1)S(1)} %all_to_all.22.grads_ref), custom_call_target="tpu_custom_call" | custom-call | tf_op jit(solution)/shard_map/pallas_call | solution.py:31
  69.2 14.1 %all_to_all.23.parts_ref = bf16[8,8,8,128]{3,2,1,0:T(8,128)(2,1)S(1)} all-to-all(bf16[8,8,8,128]{3,2,1,0:T(8,128)(2,1)S(1)} %shard_map.81), channel_id=1, replica_groups=mesh['x'=4,'u'=2,'w'=2,'c'=2,'y'=4,'h'=2] {'y','h'}, dimensions={0} | all-to-all | bytes 262144 | tf_op jit(solution)/shard_map/all_to_all | solution.py:257
  83.3 0.0 copy-done.1
  83.3 0.0 copy-done.2
  83.3 0.0 copy-done.3
  83.3 0.0 copy-done.4
  83.3 1.1 %shard_map.82 = (f32[128,256]{1,0:T(8,128)}, f32[128,256]{1,0:T(8,128)}, f32[128,256]{1,0:T(8,128)}) custom-call(bf16[8,8,8,128]{3,2,1,0:T(8,128)(2,1)S(1)} %all_to_all.23.parts_ref, f32[8,32,128]{2,1,0:T(8,128)S(1)} %copy-done.4, f32[128,256]{1,0:T(8,128)S(1)} %copy-done.1, f32[128,256]{1,0:T(8,128)S(1)} %copy-done.2, f32[128,256]{1,0:T(8,128)S(1)} %copy-done.3), custom_call_target="tpu_custom_call" | custom-call | tf_op jit(solution)/shard_map/pallas_call | solution.py:31
Async XLA Ops:
  44.6 5.3 %collective-permute-start = (bf16[128,256]{1,0:T(8,128)(2,1)S(1)}, bf16[128,256]{1,0:T(8,128)(2,1)S(1)}, u32[]{:S(2)}, u32[]{:S(2)}) collective-permute-start(bf16[128,256]{1,0:T(8,128)(2,1)S(1)} %get-tuple-element.17), channel_id=1, source_target_pairs={{0,32},{32,0},{1,33},{33,1},{2,34},{34,2},{3,35},{35,3},{4,36},{36... | collective-permute-start | bytes 196616 | tf_op jit(solution)/shard_map/ppermute | solution.py:326
  45.6 1.6 %copy-start = (f32[16,32768]{1,0:T(8,128)S(1)}, f32[16,32768]{1,0:T(8,128)}, u32[]{:S(2)}) copy-start(f32[16,32768]{1,0:T(8,128)} %refs_2_.1) | copy-start | bytes 6291460
  47.2 0.7 copy-start.5
  47.9 35.4 %copy-start.1 = (f32[128,256]{1,0:T(8,128)S(1)}, f32[128,256]{1,0:T(8,128)}, u32[]{:S(2)}) copy-start(f32[128,256]{1,0:T(8,128)} %logits_ref.1) | copy-start | bytes 393220
  47.9 35.4 %copy-start.2 = (f32[128,256]{1,0:T(8,128)S(1)}, f32[128,256]{1,0:T(8,128)}, u32[]{:S(2)}) copy-start(f32[128,256]{1,0:T(8,128)} %first_ref.1) | copy-start | bytes 393220
  47.9 35.4 %copy-start.3 = (f32[128,256]{1,0:T(8,128)S(1)}, f32[128,256]{1,0:T(8,128)}, u32[]{:S(2)}) copy-start(f32[128,256]{1,0:T(8,128)} %second_ref.1) | copy-start | bytes 393220
  47.9 35.4 %copy-start.4 = (f32[8,32,128]{2,1,0:T(8,128)S(1)}, f32[8,32,128]{2,1,0:T(8,128)}, u32[]{:S(2)}) copy-start(f32[8,32,128]{2,1,0:T(8,128)} %get-tuple-element.18.probs_ref) | copy-start | bytes 393220

commit v5 on v4

--- a/solution.py
+++ b/solution.py
@@ -22,19 +22,18 @@
 SMEM = pl.BlockSpec(memory_space=pltpu.SMEM)
 ANY = pl.BlockSpec(memory_space=pl.ANY)
 LIMIT = 40 * 1024 * 1024
-HIGH_LIMIT = 60 * 1024 * 1024
 F32 = jnp.float32
 LOW = jnp.bfloat16
 
 
-def call(body, out_shape, operands, specs, scratch=(), limit=LIMIT):
+def call(body, out_shape, operands, specs, scratch=()):
     return pl.pallas_call(
         body,
         out_shape=out_shape,
         in_specs=specs,
         out_specs=jax.tree.map(lambda unused: VMEM, out_shape),
         scratch_shapes=scratch,
-        compiler_params=pltpu.CompilerParams(vmem_limit_bytes=limit),
+        compiler_params=pltpu.CompilerParams(vmem_limit_bytes=LIMIT),
     )(*operands)
 
 
@@ -50,15 +49,7 @@
     return blocks
 
 
-def relax_kernel(
-    place_ref, triples_any, logits_any, probs_ref, send_ref, triple_ref, triples_ref, logits_ref, triples_sem, logits_sem
-):
-    triples_copy = pltpu.make_async_copy(triples_any, triples_ref, triples_sem)
-    logits_copy = pltpu.make_async_copy(logits_any, logits_ref, logits_sem)
-    logits_copy.start()
-    triples_copy.start()
-    logits_copy.wait()
-    triples_copy.wait()
+def relax_kernel(side_ref, triples_ref, logits_ref, probs_ref, send_ref, tile_ref):
     flipped = logits_ref[...].T
     attrs = probs_ref.shape[0]
     halves = send_ref.shape[0] // CHUNKS
@@ -73,11 +64,10 @@
             low = chunks[chunk].astype(LOW)
             for half in range(halves):
                 send_ref[chunk * halves + half, attr] = low
-    triple_ref[...] = jnp.zeros(triple_ref.shape, F32)
-    triple_ref[0:3, 0 : triples_ref.shape[1]] = triples_ref[...].astype(F32)
+    tile_ref[...] = jnp.zeros(tile_ref.shape, F32)
+    tile_ref[0:3, 0 : triples_ref.shape[1]] = triples_ref[...].astype(F32)
     for half in range(halves):
-        mine = jnp.where(place_ref[1] == half, 1.0, 0.0)
-        tile = (triple_ref[...] * mine).astype(LOW)
+        tile = (tile_ref[...] * jnp.where(side_ref[0] == half, 1.0, 0.0)).astype(LOW)
         for chunk in range(CHUNKS):
             send_ref[chunk * halves + half, attrs] = tile
 
@@ -299,20 +289,14 @@
     scale = cells / (rows * lax.axis_size(ROW_AXES))
     shape = jax.ShapeDtypeStruct
     tall, wide = V * V // MODS, V * MODS
-    place = jnp.stack([lax.axis_index(PLACE_AXES), lax.axis_index("h")]).astype(jnp.int32)
+    place = lax.axis_index(PLACE_AXES).astype(jnp.int32).reshape(1)
+    side = lax.axis_index("h").astype(jnp.int32).reshape(1)
     probs, copies = call(
         relax_kernel,
         (shape((attrs, V, rows), F32), shape((groups, attrs + 1, SUB, LANES), LOW)),
-        (place, triples.T, logits),
-        [SMEM, ANY, ANY],
-        [
-            pltpu.VMEM((SUB, LANES), F32),
-            pltpu.VMEM((3, margs), jnp.int32),
-            pltpu.VMEM((rows, cols), F32),
-            pltpu.SemaphoreType.DMA,
-            pltpu.SemaphoreType.DMA,
-        ],
-        HIGH_LIMIT,
+        (side, triples.T, logits),
+        [SMEM, VMEM, VMEM],
+        [pltpu.VMEM((SUB, LANES), F32)],
     )
     full = swap(copies, MARG_AXES)
     picked, attributes = call(

time: 84.8 us -> 87.3 us (1.029)
  local copies, waits for them, and re-layouts: 2.26 us -> 7.32 us
  Pallas kernels: 10.4 us -> 7.6 us
  waiting for transfers between devices: 0.9 us -> 2.11 us
    unnamed x12 -> x16, local copies, waits for them, and re-layouts: 2.26 us -> 7.32 us
    pallas_call x7, Pallas kernels: 10.4 us -> 7.6 us  [call(): pl.pallas_call(body, out_shape=out_shape, in_specs=specs, out_specs=jax.t...]
    ppermute x1, waiting for transfers between devices: 0.9 us -> 2.11 us  [shards(): other = lax.ppermute(send, 'u', [(0, 1), (1, 0)])]
where the time goes in v5:
time: 87.3 us; the launch traced here: 87 us
  blocking collectives  68.2 us (78%)
  Pallas kernels  7.6 us (9%)
  local copies, waits for them, and re-layouts  7.32 us (8%)
  waiting for transfers between devices  2.11 us (2%)
  starting transfers between devices  1 us (1%)
    all_to_all x4, blocking collectives, swap(): return lax.all_to_all(value, axes, 0, 0, tiled=True)  68.2 us
    pallas_call x7, Pallas kernels, call(): pl.pallas_call(body, out_shape=out_shape, in_specs=specs, out_specs=jax.t...  7.6 us
    unnamed x16, local copies, waits for them, and re-layouts  7.32 us
    ppermute x1, waiting for transfers between devices, shards(): other = lax.ppermute(send, 'u', [(0, 1), (1, 0)])  2.11 us
  transfers between devices with their start and end apart: 1, of which 1 were waited for; matrix products, arithmetic and copies ran while one was open for 0% of the time, Pallas kernels for 1%

profile of v5, /device:TPU:32, one launch (start us, length us, event | category | flops | bytes accessed | tf_op | source)
XLA Modules:
  0.0 87.0 jit_solution(9304244698773458829)
XLA Ops:
  0.6 0.0 copy-start.3
  0.6 0.9 %copy-done.3 = f32[128,256]{1,0:T(8,128)S(1)} copy-done((f32[128,256]{1,0:T(8,128)S(1)}, f32[128,256]{1,0:T(8,128)}, u32[]{:S(2)}) %copy-start.3) | copy-done | bytes 131096
  1.5 0.0 copy-start.7
  1.5 0.7 copy-done.7
  2.2 0.3 shard_map.76
  2.5 21.6 %all_to_all.20 = bf16[8,9,8,128]{3,2,1,0:T(8,128)(2,1)S(1)} all-to-all(bf16[8,9,8,128]{3,2,1,0:T(8,128)(2,1)S(1)} %get-tuple-element.11), channel_id=1, replica_groups=mesh['x'=4,'u'=2,'w'=2,'c'=2,'y'=4,'h'=2] {'y','h'}, dimensions={0} | all-to-all | bytes 294912 | tf_op jit(solution)/shard_map/all_to_all | solution.py:247
  24.2 0.9 shard_map.77
  25.0 16.4 %all_to_all.21.src_ref = bf16[64,3,8,128]{3,2,1,0:T(8,128)(2,1)S(1)} all-to-all(bf16[64,3,8,128]{3,2,1,0:T(8,128)(2,1)S(1)} %get-tuple-element.13), channel_id=1, replica_groups=mesh['x'=4,'u'=2,'w'=2,'c'=2,'y'=4,'h'=2] {'x','w','c','y'}, dimensions={0} | all-to-all | bytes 786432 | tf_op jit(solution)/shard_map/all_to_all | solution.py:247
  41.5 1.6 %shard_map.78 = (f32[128,256]{1,0:T(8,128)S(1)}, bf16[128,256]{1,0:T(8,128)(2,1)S(1)}, bf16[16,3,32,128]{3,2,1,0:T(8,128)(2,1)S(1)}, bf16[8,4,256,256]{3,2,1,0:T(8,128)(2,1)S(1)}) custom-call(bf16[64,3,8,128]{3,2,1,0:T(8,128)(2,1)S(1)} %all_to_all.21.src_ref), custom_call_target="tpu_custom_call" | custom-call | tf_op jit(solution)/shard_map/pallas_call | solution.py:30
  43.1 0.0 copy-start
  43.1 1.9 %copy-done = bf16[8,4,256,256]{3,2,1,0:T(8,128)(2,1)} copy-done((bf16[8,4,256,256]{3,2,1,0:T(8,128)(2,1)}, bf16[8,4,256,256]{3,2,1,0:T(8,128)(2,1)S(1)}, u32[]{:S(2)}) %copy-start) | copy-done | bytes 4194328
  45.1 1.0 %collective-permute-start = (bf16[128,256]{1,0:T(8,128)(2,1)S(1)}, bf16[128,256]{1,0:T(8,128)(2,1)S(1)}, u32[]{:S(2)}, u32[]{:S(2)}) collective-permute-start(bf16[128,256]{1,0:T(8,128)(2,1)S(1)} %get-tuple-element.17), channel_id=1, source_target_pairs={{0,32},{32,0},{1,33},{33,1},{2,34},{34,2},{3,35},{35,3},{4,36},{36... | collective-permute-start | bytes 196616 | tf_op jit(solution)/shard_map/ppermute | solution.py:310
  46.1 0.0 copy-start.2
  46.1 1.6 %copy-done.2 = f32[16,32768]{1,0:T(8,128)S(1)} copy-done((f32[16,32768]{1,0:T(8,128)S(1)}, f32[16,32768]{1,0:T(8,128)}, u32[]{:S(2)}) %copy-start.2) | copy-done | bytes 2097176
  47.7 0.0 copy-start.4
  47.7 0.0 copy-start.5
  47.7 0.0 copy-start.6
  47.7 0.5 shard_map.79.refs_2_
  48.1 2.1 %collective-permute-done.refs_3_ = bf16[128,256]{1,0:T(8,128)(2,1)S(1)} collective-permute-done((bf16[128,256]{1,0:T(8,128)(2,1)S(1)}, bf16[128,256]{1,0:T(8,128)(2,1)S(1)}, u32[]{:S(2)}, u32[]{:S(2)}) %collective-permute-start) | collective-permute-done | bytes 65568 | tf_op jit(solution)/shard_map/ppermute | solution.py:310
  50.2 0.0 copy-start.1
  50.2 2.2 %copy-done.1 = bf16[8,4,256,256]{3,2,1,0:T(8,128)(2,1)S(1)} copy-done((bf16[8,4,256,256]{3,2,1,0:T(8,128)(2,1)S(1)}, bf16[8,4,256,256]{3,2,1,0:T(8,128)(2,1)}, u32[]{:S(2)}) %copy-start.1) | copy-done | bytes 4194328
  52.4 2.3 %shard_map.80 = bf16[64,3,8,128]{3,2,1,0:T(8,128)(2,1)S(1)} custom-call(bf16[16,3,32,128]{3,2,1,0:T(8,128)(2,1)S(1)} %get-tuple-element.14.refs_0_, bf16[8,4,256,256]{3,2,1,0:T(8,128)(2,1)S(1)} %copy-done.1, f32[128,256]{1,0:T(8,128)S(1)} %shard_map.79.refs_2_, bf16[128,256]{1,0:T(8,128)(2,1)S(1)} %collective-permute-done.refs_3_), custom_call_target="tpu_custom_call" | custom-call | tf_op jit(solution)/shard_map/pallas_call | solution.py:30
  54.7 16.0 %all_to_all.22.grads_ref = bf16[64,3,8,128]{3,2,1,0:T(8,128)(2,1)S(1)} all-to-all(bf16[64,3,8,128]{3,2,1,0:T(8,128)(2,1)S(1)} %shard_map.80), channel_id=1, replica_groups=mesh['x'=4,'u'=2,'w'=2,'c'=2,'y'=4,'h'=2] {'x','w','c','y'}, dimensions={0} | all-to-all | bytes 786432 | tf_op jit(solution)/shard_map/all_to_all | solution.py:247
  70.7 1.0 %shard_map.81 = bf16[8,8,8,128]{3,2,1,0:T(8,128)(2,1)S(1)} custom-call(s32[8,128]{1,0:T(8,128)S(1)} %get-tuple-element.12.triples_ref, bf16[64,3,8,128]{3,2,1,0:T(8,128)(2,1)S(1)} %all_to_all.22.grads_ref), custom_call_target="tpu_custom_call" | custom-call | tf_op jit(solution)/shard_map/pallas_call | solution.py:30
  71.8 14.1 %all_to_all.23.parts_ref = bf16[8,8,8,128]{3,2,1,0:T(8,128)(2,1)S(1)} all-to-all(bf16[8,8,8,128]{3,2,1,0:T(8,128)(2,1)S(1)} %shard_map.81), channel_id=1, replica_groups=mesh['x'=4,'u'=2,'w'=2,'c'=2,'y'=4,'h'=2] {'y','h'}, dimensions={0} | all-to-all | bytes 262144 | tf_op jit(solution)/shard_map/all_to_all | solution.py:247
  85.9 0.0 copy-done.4
  85.9 0.0 copy-done.5
  85.9 0.0 copy-done.6
  85.9 1.1 %shard_map.82 = (f32[128,256]{1,0:T(8,128)}, f32[128,256]{1,0:T(8,128)}, f32[128,256]{1,0:T(8,128)}) custom-call(bf16[8,8,8,128]{3,2,1,0:T(8,128)(2,1)S(1)} %all_to_all.23.parts_ref, f32[8,32,128]{2,1,0:T(8,128)S(1)} %get-tuple-element.18.probs_ref, f32[128,256]{1,0:T(8,128)S(1)} %copy-done.4, f32[128,256]{1,0:T(8,128)S(1)} %copy-done.5, ...), custom_call_target="tpu_custom_call" | custom-call | tf_op jit(solution)/shard_map/pallas_call | solution.py:30
Async XLA Ops:
  0.6 0.9 %copy-start.3 = (f32[128,256]{1,0:T(8,128)S(1)}, f32[128,256]{1,0:T(8,128)}, u32[]{:S(2)}) copy-start(f32[128,256]{1,0:T(8,128)} %logits_ref.3) | copy-start | bytes 393220
  1.5 0.7 copy-start.7
  43.1 2.0 %copy-start = (bf16[8,4,256,256]{3,2,1,0:T(8,128)(2,1)}, bf16[8,4,256,256]{3,2,1,0:T(8,128)(2,1)S(1)}, u32[]{:S(2)}) copy-start(bf16[8,4,256,256]{3,2,1,0:T(8,128)(2,1)S(1)} %get-tuple-element.15.refs_1_) | copy-start | bytes 12582916
  45.1 5.2 %collective-permute-start = (bf16[128,256]{1,0:T(8,128)(2,1)S(1)}, bf16[128,256]{1,0:T(8,128)(2,1)S(1)}, u32[]{:S(2)}, u32[]{:S(2)}) collective-permute-start(bf16[128,256]{1,0:T(8,128)(2,1)S(1)} %get-tuple-element.17), channel_id=1, source_target_pairs={{0,32},{32,0},{1,33},{33,1},{2,34},{34,2},{3,35},{35,3},{4,36},{36... | collective-permute-start | bytes 196616 | tf_op jit(solution)/shard_map/ppermute | solution.py:310
  46.1 1.6 %copy-start.2 = (f32[16,32768]{1,0:T(8,128)S(1)}, f32[16,32768]{1,0:T(8,128)}, u32[]{:S(2)}) copy-start(f32[16,32768]{1,0:T(8,128)} %refs_2_.1) | copy-start | bytes 6291460
  47.7 38.3 %copy-start.4 = (f32[128,256]{1,0:T(8,128)S(1)}, f32[128,256]{1,0:T(8,128)}, u32[]{:S(2)}) copy-start(f32[128,256]{1,0:T(8,128)} %logits_ref.3) | copy-start | bytes 393220
  47.7 38.3 %copy-start.5 = (f32[128,256]{1,0:T(8,128)S(1)}, f32[128,256]{1,0:T(8,128)}, u32[]{:S(2)}) copy-start(f32[128,256]{1,0:T(8,128)} %first_ref.1) | copy-start | bytes 393220
  47.7 38.3 %copy-start.6 = (f32[128,256]{1,0:T(8,128)S(1)}, f32[128,256]{1,0:T(8,128)}, u32[]{:S(2)}) copy-start(f32[128,256]{1,0:T(8,128)} %second_ref.1) | copy-start | bytes 393220
  50.2 2.2 %copy-start.1 = (bf16[8,4,256,256]{3,2,1,0:T(8,128)(2,1)S(1)}, bf16[8,4,256,256]{3,2,1,0:T(8,128)(2,1)}, u32[]{:S(2)}) copy-start(bf16[8,4,256,256]{3,2,1,0:T(8,128)(2,1)} %copy-done) | copy-start | bytes 12582916

commit v6 on v5

--- a/solution.py
+++ b/solution.py
@@ -21,7 +21,7 @@
 VMEM = pl.BlockSpec(memory_space=pltpu.VMEM)
 SMEM = pl.BlockSpec(memory_space=pltpu.SMEM)
 ANY = pl.BlockSpec(memory_space=pl.ANY)
-LIMIT = 40 * 1024 * 1024
+LIMIT = 20 * 1024 * 1024
 F32 = jnp.float32
 LOW = jnp.bfloat16
 

time: 87.3 us -> 87.3 us (level)
  no operation moved by 1% of the time
where the time goes in v6:
time: 87.3 us; the launch traced here: 87 us
  blocking collectives  68.2 us (78%)
  Pallas kernels  7.6 us (9%)
  local copies, waits for them, and re-layouts  7.32 us (8%)
  waiting for transfers between devices  2.11 us (2%)
  starting transfers between devices  1 us (1%)
    all_to_all x4, blocking collectives, swap(): return lax.all_to_all(value, axes, 0, 0, tiled=True)  68.2 us
    pallas_call x7, Pallas kernels, call(): pl.pallas_call(body, out_shape=out_shape, in_specs=specs, out_specs=jax.t...  7.6 us
    unnamed x16, local copies, waits for them, and re-layouts  7.32 us
    ppermute x1, waiting for transfers between devices, shards(): other = lax.ppermute(send, 'u', [(0, 1), (1, 0)])  2.11 us
  transfers between devices with their start and end apart: 1, of which 1 were waited for; matrix products, arithmetic and copies ran while one was open for 0% of the time, Pallas kernels for 1%

profile of v6, /device:TPU:32, one launch (start us, length us, event | category | flops | bytes accessed | tf_op | source)
XLA Modules:
  0.0 87.0 jit_solution(236153521977673118)
XLA Ops:
  0.6 0.0 copy-start.3
  0.6 0.9 %copy-done.3 = f32[128,256]{1,0:T(8,128)S(1)} copy-done((f32[128,256]{1,0:T(8,128)S(1)}, f32[128,256]{1,0:T(8,128)}, u32[]{:S(2)}) %copy-start.3) | copy-done | bytes 131096
  1.5 0.0 copy-start.7
  1.5 0.7 copy-done.7
  2.2 0.3 shard_map.76
  2.5 21.6 %all_to_all.20 = bf16[8,9,8,128]{3,2,1,0:T(8,128)(2,1)S(1)} all-to-all(bf16[8,9,8,128]{3,2,1,0:T(8,128)(2,1)S(1)} %get-tuple-element.11), channel_id=1, replica_groups=mesh['x'=4,'u'=2,'w'=2,'c'=2,'y'=4,'h'=2] {'y','h'}, dimensions={0} | all-to-all | bytes 294912 | tf_op jit(solution)/shard_map/all_to_all | solution.py:247
  24.2 0.9 shard_map.77
  25.0 16.4 %all_to_all.21.src_ref = bf16[64,3,8,128]{3,2,1,0:T(8,128)(2,1)S(1)} all-to-all(bf16[64,3,8,128]{3,2,1,0:T(8,128)(2,1)S(1)} %get-tuple-element.13), channel_id=1, replica_groups=mesh['x'=4,'u'=2,'w'=2,'c'=2,'y'=4,'h'=2] {'x','w','c','y'}, dimensions={0} | all-to-all | bytes 786432 | tf_op jit(solution)/shard_map/all_to_all | solution.py:247
  41.5 1.6 %shard_map.78 = (f32[128,256]{1,0:T(8,128)S(1)}, bf16[128,256]{1,0:T(8,128)(2,1)S(1)}, bf16[16,3,32,128]{3,2,1,0:T(8,128)(2,1)S(1)}, bf16[8,4,256,256]{3,2,1,0:T(8,128)(2,1)S(1)}) custom-call(bf16[64,3,8,128]{3,2,1,0:T(8,128)(2,1)S(1)} %all_to_all.21.src_ref), custom_call_target="tpu_custom_call" | custom-call | tf_op jit(solution)/shard_map/pallas_call | solution.py:30
  43.1 0.0 copy-start
  43.1 1.9 %copy-done = bf16[8,4,256,256]{3,2,1,0:T(8,128)(2,1)} copy-done((bf16[8,4,256,256]{3,2,1,0:T(8,128)(2,1)}, bf16[8,4,256,256]{3,2,1,0:T(8,128)(2,1)S(1)}, u32[]{:S(2)}) %copy-start) | copy-done | bytes 4194328
  45.1 1.0 %collective-permute-start = (bf16[128,256]{1,0:T(8,128)(2,1)S(1)}, bf16[128,256]{1,0:T(8,128)(2,1)S(1)}, u32[]{:S(2)}, u32[]{:S(2)}) collective-permute-start(bf16[128,256]{1,0:T(8,128)(2,1)S(1)} %get-tuple-element.17), channel_id=1, source_target_pairs={{0,32},{32,0},{1,33},{33,1},{2,34},{34,2},{3,35},{35,3},{4,36},{36... | collective-permute-start | bytes 196616 | tf_op jit(solution)/shard_map/ppermute | solution.py:310
  46.1 0.0 copy-start.2
  46.1 1.6 %copy-done.2 = f32[16,32768]{1,0:T(8,128)S(1)} copy-done((f32[16,32768]{1,0:T(8,128)S(1)}, f32[16,32768]{1,0:T(8,128)}, u32[]{:S(2)}) %copy-start.2) | copy-done | bytes 2097176
  47.7 0.0 copy-start.4
  47.7 0.0 copy-start.5
  47.7 0.0 copy-start.6
  47.7 0.5 shard_map.79.refs_2_
  48.1 2.1 %collective-permute-done.refs_3_ = bf16[128,256]{1,0:T(8,128)(2,1)S(1)} collective-permute-done((bf16[128,256]{1,0:T(8,128)(2,1)S(1)}, bf16[128,256]{1,0:T(8,128)(2,1)S(1)}, u32[]{:S(2)}, u32[]{:S(2)}) %collective-permute-start) | collective-permute-done | bytes 65568 | tf_op jit(solution)/shard_map/ppermute | solution.py:310
  50.2 0.0 copy-start.1
  50.2 2.2 %copy-done.1 = bf16[8,4,256,256]{3,2,1,0:T(8,128)(2,1)S(1)} copy-done((bf16[8,4,256,256]{3,2,1,0:T(8,128)(2,1)S(1)}, bf16[8,4,256,256]{3,2,1,0:T(8,128)(2,1)}, u32[]{:S(2)}) %copy-start.1) | copy-done | bytes 4194328
  52.4 2.3 %shard_map.80 = bf16[64,3,8,128]{3,2,1,0:T(8,128)(2,1)S(1)} custom-call(bf16[16,3,32,128]{3,2,1,0:T(8,128)(2,1)S(1)} %get-tuple-element.14.refs_0_, bf16[8,4,256,256]{3,2,1,0:T(8,128)(2,1)S(1)} %copy-done.1, f32[128,256]{1,0:T(8,128)S(1)} %shard_map.79.refs_2_, bf16[128,256]{1,0:T(8,128)(2,1)S(1)} %collective-permute-done.refs_3_), custom_call_target="tpu_custom_call" | custom-call | tf_op jit(solution)/shard_map/pallas_call | solution.py:30
  54.7 16.0 %all_to_all.22.grads_ref = bf16[64,3,8,128]{3,2,1,0:T(8,128)(2,1)S(1)} all-to-all(bf16[64,3,8,128]{3,2,1,0:T(8,128)(2,1)S(1)} %shard_map.80), channel_id=1, replica_groups=mesh['x'=4,'u'=2,'w'=2,'c'=2,'y'=4,'h'=2] {'x','w','c','y'}, dimensions={0} | all-to-all | bytes 786432 | tf_op jit(solution)/shard_map/all_to_all | solution.py:247
  70.7 1.0 %shard_map.81 = bf16[8,8,8,128]{3,2,1,0:T(8,128)(2,1)S(1)} custom-call(s32[8,128]{1,0:T(8,128)S(1)} %get-tuple-element.12.triples_ref, bf16[64,3,8,128]{3,2,1,0:T(8,128)(2,1)S(1)} %all_to_all.22.grads_ref), custom_call_target="tpu_custom_call" | custom-call | tf_op jit(solution)/shard_map/pallas_call | solution.py:30
  71.8 14.1 %all_to_all.23.parts_ref = bf16[8,8,8,128]{3,2,1,0:T(8,128)(2,1)S(1)} all-to-all(bf16[8,8,8,128]{3,2,1,0:T(8,128)(2,1)S(1)} %shard_map.81), channel_id=1, replica_groups=mesh['x'=4,'u'=2,'w'=2,'c'=2,'y'=4,'h'=2] {'y','h'}, dimensions={0} | all-to-all | bytes 262144 | tf_op jit(solution)/shard_map/all_to_all | solution.py:247
  85.9 0.0 copy-done.4
  85.9 0.0 copy-done.5
  85.9 0.0 copy-done.6
  85.9 1.1 %shard_map.82 = (f32[128,256]{1,0:T(8,128)}, f32[128,256]{1,0:T(8,128)}, f32[128,256]{1,0:T(8,128)}) custom-call(bf16[8,8,8,128]{3,2,1,0:T(8,128)(2,1)S(1)} %all_to_all.23.parts_ref, f32[8,32,128]{2,1,0:T(8,128)S(1)} %get-tuple-element.18.probs_ref, f32[128,256]{1,0:T(8,128)S(1)} %copy-done.4, f32[128,256]{1,0:T(8,128)S(1)} %copy-done.5, ...), custom_call_target="tpu_custom_call" | custom-call | tf_op jit(solution)/shard_map/pallas_call | solution.py:30
Async XLA Ops:
  0.6 0.9 %copy-start.3 = (f32[128,256]{1,0:T(8,128)S(1)}, f32[128,256]{1,0:T(8,128)}, u32[]{:S(2)}) copy-start(f32[128,256]{1,0:T(8,128)} %logits_ref.3) | copy-start | bytes 393220
  1.5 0.7 copy-start.7
  43.1 2.0 %copy-start = (bf16[8,4,256,256]{3,2,1,0:T(8,128)(2,1)}, bf16[8,4,256,256]{3,2,1,0:T(8,128)(2,1)S(1)}, u32[]{:S(2)}) copy-start(bf16[8,4,256,256]{3,2,1,0:T(8,128)(2,1)S(1)} %get-tuple-element.15.refs_1_) | copy-start | bytes 12582916
  45.1 5.2 %collective-permute-start = (bf16[128,256]{1,0:T(8,128)(2,1)S(1)}, bf16[128,256]{1,0:T(8,128)(2,1)S(1)}, u32[]{:S(2)}, u32[]{:S(2)}) collective-permute-start(bf16[128,256]{1,0:T(8,128)(2,1)S(1)} %get-tuple-element.17), channel_id=1, source_target_pairs={{0,32},{32,0},{1,33},{33,1},{2,34},{34,2},{3,35},{35,3},{4,36},{36... | collective-permute-start | bytes 196616 | tf_op jit(solution)/shard_map/ppermute | solution.py:310
  46.1 1.6 %copy-start.2 = (f32[16,32768]{1,0:T(8,128)S(1)}, f32[16,32768]{1,0:T(8,128)}, u32[]{:S(2)}) copy-start(f32[16,32768]{1,0:T(8,128)} %refs_2_.1) | copy-start | bytes 6291460
  47.7 38.3 %copy-start.4 = (f32[128,256]{1,0:T(8,128)S(1)}, f32[128,256]{1,0:T(8,128)}, u32[]{:S(2)}) copy-start(f32[128,256]{1,0:T(8,128)} %logits_ref.3) | copy-start | bytes 393220
  47.7 38.3 %copy-start.5 = (f32[128,256]{1,0:T(8,128)S(1)}, f32[128,256]{1,0:T(8,128)}, u32[]{:S(2)}) copy-start(f32[128,256]{1,0:T(8,128)} %first_ref.1) | copy-start | bytes 393220
  47.7 38.3 %copy-start.6 = (f32[128,256]{1,0:T(8,128)S(1)}, f32[128,256]{1,0:T(8,128)}, u32[]{:S(2)}) copy-start(f32[128,256]{1,0:T(8,128)} %second_ref.1) | copy-start | bytes 393220
  50.2 2.2 %copy-start.1 = (bf16[8,4,256,256]{3,2,1,0:T(8,128)(2,1)S(1)}, bf16[8,4,256,256]{3,2,1,0:T(8,128)(2,1)}, u32[]{:S(2)}) copy-start(bf16[8,4,256,256]{3,2,1,0:T(8,128)(2,1)} %copy-done) | copy-start | bytes 12582916

commit v7 on v6

--- a/solution.py
+++ b/solution.py
@@ -49,7 +49,7 @@
     return blocks
 
 
-def relax_kernel(side_ref, triples_ref, logits_ref, probs_ref, send_ref, tile_ref):
+def relax_kernel(side_ref, place_ref, triples_ref, logits_ref, probs_ref, send_ref, tile_ref):
     flipped = logits_ref[...].T
     attrs = probs_ref.shape[0]
     halves = send_ref.shape[0] // CHUNKS
@@ -294,8 +294,8 @@
     probs, copies = call(
         relax_kernel,
         (shape((attrs, V, rows), F32), shape((groups, attrs + 1, SUB, LANES), LOW)),
-        (side, triples.T, logits),
-        [SMEM, VMEM, VMEM],
+        (side, place, triples.T, logits),
+        [SMEM, SMEM, VMEM, VMEM],
         [pltpu.VMEM((SUB, LANES), F32)],
     )
     full = swap(copies, MARG_AXES)

time: 87.3 us -> 83.3 us (0.954)
  local copies, waits for them, and re-layouts: 7.32 us -> 3.18 us
    unnamed x16 -> x12, local copies, waits for them, and re-layouts: 7.32 us -> 3.18 us
where the time goes in v7:
time: 83.3 us; the launch traced here: 83 us
  blocking collectives  68.2 us (82%)
  Pallas kernels  7.63 us (9%)
  local copies, waits for them, and re-layouts  3.18 us (4%)
  waiting for transfers between devices  2.11 us (3%)
  starting transfers between devices  1.08 us (1%)
    all_to_all x4, blocking collectives, swap(): return lax.all_to_all(value, axes, 0, 0, tiled=True)  68.2 us
    pallas_call x7, Pallas kernels, call(): pl.pallas_call(body, out_shape=out_shape, in_specs=specs, out_specs=jax.t...  7.63 us
    unnamed x12, local copies, waits for them, and re-layouts  3.18 us
    ppermute x1, waiting for transfers between devices, shards(): other = lax.ppermute(send, 'u', [(0, 1), (1, 0)])  2.11 us
  transfers between devices with their start and end apart: 1, of which 1 were waited for; matrix products, arithmetic and copies ran while one was open for 0% of the time, Pallas kernels for 1%

profile of v7, /device:TPU:32, one launch (start us, length us, event | category | flops | bytes accessed | tf_op | source)
XLA Modules:
  0.0 83.0 jit_solution(15715718655581146289)
XLA Ops:
  0.6 0.0 copy-start.1
  0.7 0.9 %copy-done.1 = f32[128,256]{1,0:T(8,128)S(1)} copy-done((f32[128,256]{1,0:T(8,128)S(1)}, f32[128,256]{1,0:T(8,128)}, u32[]{:S(2)}) %copy-start.1) | copy-done | bytes 131096
  1.5 0.0 copy-start.5
  1.5 0.7 copy-done.5
  2.2 0.3 shard_map.76
  2.5 21.6 %all_to_all.20 = bf16[8,9,8,128]{3,2,1,0:T(8,128)(2,1)S(1)} all-to-all(bf16[8,9,8,128]{3,2,1,0:T(8,128)(2,1)S(1)} %get-tuple-element.11), channel_id=1, replica_groups=mesh['x'=4,'u'=2,'w'=2,'c'=2,'y'=4,'h'=2] {'y','h'}, dimensions={0} | all-to-all | bytes 294912 | tf_op jit(solution)/shard_map/all_to_all | solution.py:247
  24.2 0.9 %shard_map.77 = (bf16[64,3,8,128]{3,2,1,0:T(8,128)(2,1)S(1)}, s32[8,128]{1,0:T(8,128)S(1)}) custom-call(bf16[72,8,128]{2,1,0:T(8,128)(2,1)S(1)} %bitcast.4), custom_call_target="tpu_custom_call" | custom-call | tf_op jit(solution)/shard_map/pallas_call | solution.py:30
  25.0 16.4 %all_to_all.21.src_ref = bf16[64,3,8,128]{3,2,1,0:T(8,128)(2,1)S(1)} all-to-all(bf16[64,3,8,128]{3,2,1,0:T(8,128)(2,1)S(1)} %get-tuple-element.13), channel_id=1, replica_groups=mesh['x'=4,'u'=2,'w'=2,'c'=2,'y'=4,'h'=2] {'x','w','c','y'}, dimensions={0} | all-to-all | bytes 786432 | tf_op jit(solution)/shard_map/all_to_all | solution.py:247
  41.5 1.6 %shard_map.78 = (f32[128,256]{1,0:T(8,128)S(1)}, bf16[128,256]{1,0:T(8,128)(2,1)S(1)}, bf16[16,3,32,128]{3,2,1,0:T(8,128)(2,1)S(1)}, bf16[8,4,256,256]{3,2,1,0:T(8,128)(2,1)S(1)}) custom-call(bf16[64,3,8,128]{3,2,1,0:T(8,128)(2,1)S(1)} %all_to_all.21.src_ref), custom_call_target="tpu_custom_call" | custom-call | tf_op jit(solution)/shard_map/pallas_call | solution.py:30
  43.1 1.1 %collective-permute-start = (bf16[128,256]{1,0:T(8,128)(2,1)S(1)}, bf16[128,256]{1,0:T(8,128)(2,1)S(1)}, u32[]{:S(2)}, u32[]{:S(2)}) collective-permute-start(bf16[128,256]{1,0:T(8,128)(2,1)S(1)} %get-tuple-element.17), channel_id=1, source_target_pairs={{0,32},{32,0},{1,33},{33,1},{2,34},{34,2},{3,35},{35,3},{4,36},{36... | collective-permute-start | bytes 196616 | tf_op jit(solution)/shard_map/ppermute | solution.py:310
  44.2 0.0 copy-start
  44.2 1.6 %copy-done = f32[16,32768]{1,0:T(8,128)S(1)} copy-done((f32[16,32768]{1,0:T(8,128)S(1)}, f32[16,32768]{1,0:T(8,128)}, u32[]{:S(2)}) %copy-start) | copy-done | bytes 2097176
  45.8 0.0 copy-start.2
  45.8 0.0 copy-start.3
  45.8 0.0 copy-start.4
  45.8 0.5 shard_map.79.refs_2_
  46.3 2.1 %collective-permute-done.refs_3_ = bf16[128,256]{1,0:T(8,128)(2,1)S(1)} collective-permute-done((bf16[128,256]{1,0:T(8,128)(2,1)S(1)}, bf16[128,256]{1,0:T(8,128)(2,1)S(1)}, u32[]{:S(2)}, u32[]{:S(2)}) %collective-permute-start) | collective-permute-done | bytes 65568 | tf_op jit(solution)/shard_map/ppermute | solution.py:310
  48.4 2.3 %shard_map.80 = bf16[64,3,8,128]{3,2,1,0:T(8,128)(2,1)S(1)} custom-call(bf16[16,3,32,128]{3,2,1,0:T(8,128)(2,1)S(1)} %get-tuple-element.14.refs_0_, bf16[8,4,256,256]{3,2,1,0:T(8,128)(2,1)S(1)} %get-tuple-element.15.refs_1_, f32[128,256]{1,0:T(8,128)S(1)} %shard_map.79.refs_2_, bf16[128,256]{1,0:T(8,128)(2,1)S(1)} %collective-permute-done.refs_3_), custom_call_target="tpu_custom_call" | custom-call | tf_op jit(solution)/shard_map/pallas_call | solution.py:30
  50.7 16.0 %all_to_all.22.grads_ref = bf16[64,3,8,128]{3,2,1,0:T(8,128)(2,1)S(1)} all-to-all(bf16[64,3,8,128]{3,2,1,0:T(8,128)(2,1)S(1)} %shard_map.80), channel_id=1, replica_groups=mesh['x'=4,'u'=2,'w'=2,'c'=2,'y'=4,'h'=2] {'x','w','c','y'}, dimensions={0} | all-to-all | bytes 786432 | tf_op jit(solution)/shard_map/all_to_all | solution.py:247
  66.7 1.0 %shard_map.81 = bf16[8,8,8,128]{3,2,1,0:T(8,128)(2,1)S(1)} custom-call(s32[8,128]{1,0:T(8,128)S(1)} %get-tuple-element.12.triples_ref, bf16[64,3,8,128]{3,2,1,0:T(8,128)(2,1)S(1)} %all_to_all.22.grads_ref), custom_call_target="tpu_custom_call" | custom-call | tf_op jit(solution)/shard_map/pallas_call | solution.py:30
  67.7 14.1 %all_to_all.23.parts_ref = bf16[8,8,8,128]{3,2,1,0:T(8,128)(2,1)S(1)} all-to-all(bf16[8,8,8,128]{3,2,1,0:T(8,128)(2,1)S(1)} %shard_map.81), channel_id=1, replica_groups=mesh['x'=4,'u'=2,'w'=2,'c'=2,'y'=4,'h'=2] {'y','h'}, dimensions={0} | all-to-all | bytes 262144 | tf_op jit(solution)/shard_map/all_to_all | solution.py:247
  81.9 0.0 copy-done.2
  81.9 0.0 copy-done.3
  81.9 0.0 copy-done.4
  81.9 1.1 %shard_map.82 = (f32[128,256]{1,0:T(8,128)}, f32[128,256]{1,0:T(8,128)}, f32[128,256]{1,0:T(8,128)}) custom-call(bf16[8,8,8,128]{3,2,1,0:T(8,128)(2,1)S(1)} %all_to_all.23.parts_ref, f32[8,32,128]{2,1,0:T(8,128)S(1)} %get-tuple-element.18.probs_ref, f32[128,256]{1,0:T(8,128)S(1)} %copy-done.2, f32[128,256]{1,0:T(8,128)S(1)} %copy-done.3, ...), custom_call_target="tpu_custom_call" | custom-call | tf_op jit(solution)/shard_map/pallas_call | solution.py:30
Async XLA Ops:
  0.6 0.9 %copy-start.1 = (f32[128,256]{1,0:T(8,128)S(1)}, f32[128,256]{1,0:T(8,128)}, u32[]{:S(2)}) copy-start(f32[128,256]{1,0:T(8,128)} %logits_ref.3) | copy-start | bytes 393220
  1.5 0.7 copy-start.5
  43.1 5.3 %collective-permute-start = (bf16[128,256]{1,0:T(8,128)(2,1)S(1)}, bf16[128,256]{1,0:T(8,128)(2,1)S(1)}, u32[]{:S(2)}, u32[]{:S(2)}) collective-permute-start(bf16[128,256]{1,0:T(8,128)(2,1)S(1)} %get-tuple-element.17), channel_id=1, source_target_pairs={{0,32},{32,0},{1,33},{33,1},{2,34},{34,2},{3,35},{35,3},{4,36},{36... | collective-permute-start | bytes 196616 | tf_op jit(solution)/shard_map/ppermute | solution.py:310
  44.2 1.6 %copy-start = (f32[16,32768]{1,0:T(8,128)S(1)}, f32[16,32768]{1,0:T(8,128)}, u32[]{:S(2)}) copy-start(f32[16,32768]{1,0:T(8,128)} %refs_2_.1) | copy-start | bytes 6291460
  45.8 36.1 %copy-start.2 = (f32[128,256]{1,0:T(8,128)S(1)}, f32[128,256]{1,0:T(8,128)}, u32[]{:S(2)}) copy-start(f32[128,256]{1,0:T(8,128)} %logits_ref.3) | copy-start | bytes 393220
  45.8 36.1 %copy-start.3 = (f32[128,256]{1,0:T(8,128)S(1)}, f32[128,256]{1,0:T(8,128)}, u32[]{:S(2)}) copy-start(f32[128,256]{1,0:T(8,128)} %first_ref.1) | copy-start | bytes 393220
  45.8 36.1 %copy-start.4 = (f32[128,256]{1,0:T(8,128)S(1)}, f32[128,256]{1,0:T(8,128)}, u32[]{:S(2)}) copy-start(f32[128,256]{1,0:T(8,128)} %second_ref.1) | copy-start | bytes 393220

commit v8 on v7

--- a/solution.py
+++ b/solution.py
@@ -49,7 +49,18 @@
     return blocks
 
 
-def relax_kernel(side_ref, place_ref, triples_ref, logits_ref, probs_ref, send_ref, tile_ref):
+def stay(value):
+    return pltpu.with_memory_space_constraint(value, pltpu.HBM)
+
+
+def relax_kernel(
+    side_ref, place_ref, triples_hbm, logits_hbm, probs_ref, send_ref, tile_ref, triples_ref, logits_ref, sems
+):
+    logits_copy = pltpu.make_async_copy(logits_hbm, logits_ref, sems.at[0])
+    triples_copy = pltpu.make_async_copy(triples_hbm, triples_ref, sems.at[1])
+    logits_copy.start()
+    triples_copy.start()
+    logits_copy.wait()
     flipped = logits_ref[...].T
     attrs = probs_ref.shape[0]
     halves = send_ref.shape[0] // CHUNKS
@@ -64,6 +75,7 @@
             low = chunks[chunk].astype(LOW)
             for half in range(halves):
                 send_ref[chunk * halves + half, attr] = low
+    triples_copy.wait()
     tile_ref[...] = jnp.zeros(tile_ref.shape, F32)
     tile_ref[0:3, 0 : triples_ref.shape[1]] = triples_ref[...].astype(F32)
     for half in range(halves):
@@ -294,9 +306,14 @@
     probs, copies = call(
         relax_kernel,
         (shape((attrs, V, rows), F32), shape((groups, attrs + 1, SUB, LANES), LOW)),
-        (side, place, triples.T, logits),
-        [SMEM, SMEM, VMEM, VMEM],
-        [pltpu.VMEM((SUB, LANES), F32)],
+        (side, place, stay(triples.T), stay(logits)),
+        [SMEM, SMEM, ANY, ANY],
+        [
+            pltpu.VMEM((SUB, LANES), F32),
+            pltpu.VMEM((3, margs), jnp.int32),
+            pltpu.VMEM((rows, cols), F32),
+            pltpu.SemaphoreType.DMA((2,)),
+        ],
     )
     full = swap(copies, MARG_AXES)
     picked, attributes = call(
@@ -311,7 +328,7 @@
     base = call(
         lambda *refs: base_kernel(scale, *refs),
         shape((wide, tall), F32),
-        (place, own, targets),
+        (place, own, stay(targets)),
         [SMEM, VMEM, ANY],
         [pltpu.VMEM((8, cells), F32), pltpu.VMEM((tall, wide), F32), pltpu.SemaphoreType.DMA],
     )

time: 83.3 us -> 82.5 us (level)
  local copies, waits for them, and re-layouts: 3.18 us -> 0.01 us
  Pallas kernels: 7.63 us -> 9.74 us
    unnamed x12 -> x6, local copies, waits for them, and re-layouts: 3.18 us -> 0.01 us
    pallas_call x7, Pallas kernels: 7.63 us -> 9.74 us  [call(): pl.pallas_call(body, out_shape=out_shape, in_specs=specs, out_specs=jax.t...]
  transfers between devices with their start and end apart: 1 -> 1, of which waited for: 1 -> 1; matrix products, arithmetic and copies ran while one was open for 0% -> 0% of each run, Pallas kernels for 1% -> 2%
where the time goes in v8:
time: 82.5 us; the launch traced here: 82.3 us
  blocking collectives  68.2 us (83%)
  Pallas kernels  9.74 us (12%)
  waiting for transfers between devices  2.5 us (3%)
  starting transfers between devices  1.08 us (1%)
    all_to_all x4, blocking collectives, swap(): return lax.all_to_all(value, axes, 0, 0, tiled=True)  68.2 us
    pallas_call x7, Pallas kernels, call(): pl.pallas_call(body, out_shape=out_shape, in_specs=specs, out_specs=jax.t...  9.74 us
    ppermute x1, waiting for transfers between devices, shards(): other = lax.ppermute(send, 'u', [(0, 1), (1, 0)])  2.5 us
  transfers between devices with their start and end apart: 1, of which 1 were waited for; matrix products, arithmetic and copies ran while one was open for 0% of the time, Pallas kernels for 2%

profile of v8, /device:TPU:32, one launch (start us, length us, event | category | flops | bytes accessed | tf_op | source)
XLA Modules:
  0.0 82.3 jit_solution(12058737839521217903)
XLA Ops:
  0.6 1.2 %shard_map.76 = (f32[8,32,128]{2,1,0:T(8,128)S(1)}, bf16[8,9,8,128]{3,2,1,0:T(8,128)(2,1)S(1)}) custom-call(s32[1]{0:T(128)} %bitcast.side_ref, s32[1]{0:T(128)} %bitcast.1.place_ref.refs_0_, s32[3,16]{1,0:T(4,128)} %bitcast.5, f32[128,256]{1,0:T(8,128)} %logits_ref.1), custom_call_target="tpu_custom_call" | custom-call | tf_op jit(solution)/shard_map/pallas_call | solution.py:30
  1.9 21.6 %all_to_all.20 = bf16[8,9,8,128]{3,2,1,0:T(8,128)(2,1)S(1)} all-to-all(bf16[8,9,8,128]{3,2,1,0:T(8,128)(2,1)S(1)} %get-tuple-element.11), channel_id=1, replica_groups=mesh['x'=4,'u'=2,'w'=2,'c'=2,'y'=4,'h'=2] {'y','h'}, dimensions={0} | all-to-all | bytes 294912 | tf_op jit(solution)/shard_map/all_to_all | solution.py:259
  23.5 0.9 %shard_map.77 = (bf16[64,3,8,128]{3,2,1,0:T(8,128)(2,1)S(1)}, s32[8,128]{1,0:T(8,128)S(1)}) custom-call(bf16[72,8,128]{2,1,0:T(8,128)(2,1)S(1)} %bitcast.4), custom_call_target="tpu_custom_call" | custom-call | tf_op jit(solution)/shard_map/pallas_call | solution.py:30
  24.4 16.4 %all_to_all.21.src_ref = bf16[64,3,8,128]{3,2,1,0:T(8,128)(2,1)S(1)} all-to-all(bf16[64,3,8,128]{3,2,1,0:T(8,128)(2,1)S(1)} %get-tuple-element.13), channel_id=1, replica_groups=mesh['x'=4,'u'=2,'w'=2,'c'=2,'y'=4,'h'=2] {'x','w','c','y'}, dimensions={0} | all-to-all | bytes 786432 | tf_op jit(solution)/shard_map/all_to_all | solution.py:259
  40.8 1.6 %shard_map.78 = (f32[128,256]{1,0:T(8,128)S(1)}, bf16[128,256]{1,0:T(8,128)(2,1)S(1)}, bf16[16,3,32,128]{3,2,1,0:T(8,128)(2,1)S(1)}, bf16[8,4,256,256]{3,2,1,0:T(8,128)(2,1)S(1)}) custom-call(bf16[64,3,8,128]{3,2,1,0:T(8,128)(2,1)S(1)} %all_to_all.21.src_ref), custom_call_target="tpu_custom_call" | custom-call | tf_op jit(solution)/shard_map/pallas_call | solution.py:30
  42.5 1.1 %collective-permute-start = (bf16[128,256]{1,0:T(8,128)(2,1)S(1)}, bf16[128,256]{1,0:T(8,128)(2,1)S(1)}, u32[]{:S(2)}, u32[]{:S(2)}) collective-permute-start(bf16[128,256]{1,0:T(8,128)(2,1)S(1)} %get-tuple-element.17), channel_id=1, source_target_pairs={{0,32},{32,0},{1,33},{33,1},{2,34},{34,2},{3,35},{35,3},{4,36},{36... | collective-permute-start | bytes 196616 | tf_op jit(solution)/shard_map/ppermute | solution.py:327
  43.6 0.0 copy-start
  43.6 0.0 copy-start.1
  43.6 0.0 copy-start.2
  43.6 1.7 %shard_map.79.refs_2_ = f32[128,256]{1,0:T(8,128)S(1)} custom-call(s32[1]{0:T(128)} %bitcast.1.place_ref.refs_0_, f32[128,256]{1,0:T(8,128)S(1)} %get-tuple-element.16.refs_1_, f32[16,32768]{1,0:T(8,128)} %refs_2_.1), custom_call_target="tpu_custom_call" | custom-call | tf_op jit(solution)/shard_map/pallas_call | solution.py:30
  45.2 2.5 %collective-permute-done.refs_3_ = bf16[128,256]{1,0:T(8,128)(2,1)S(1)} collective-permute-done((bf16[128,256]{1,0:T(8,128)(2,1)S(1)}, bf16[128,256]{1,0:T(8,128)(2,1)S(1)}, u32[]{:S(2)}, u32[]{:S(2)}) %collective-permute-start) | collective-permute-done | bytes 65568 | tf_op jit(solution)/shard_map/ppermute | solution.py:327
  47.7 2.3 %shard_map.80 = bf16[64,3,8,128]{3,2,1,0:T(8,128)(2,1)S(1)} custom-call(bf16[16,3,32,128]{3,2,1,0:T(8,128)(2,1)S(1)} %get-tuple-element.14.refs_0_, bf16[8,4,256,256]{3,2,1,0:T(8,128)(2,1)S(1)} %get-tuple-element.15.refs_1_, f32[128,256]{1,0:T(8,128)S(1)} %shard_map.79.refs_2_, bf16[128,256]{1,0:T(8,128)(2,1)S(1)} %collective-permute-done.refs_3_), custom_call_target="tpu_custom_call" | custom-call | tf_op jit(solution)/shard_map/pallas_call | solution.py:30
  50.0 16.0 %all_to_all.22.grads_ref = bf16[64,3,8,128]{3,2,1,0:T(8,128)(2,1)S(1)} all-to-all(bf16[64,3,8,128]{3,2,1,0:T(8,128)(2,1)S(1)} %shard_map.80), channel_id=1, replica_groups=mesh['x'=4,'u'=2,'w'=2,'c'=2,'y'=4,'h'=2] {'x','w','c','y'}, dimensions={0} | all-to-all | bytes 786432 | tf_op jit(solution)/shard_map/all_to_all | solution.py:259
  66.0 1.0 %shard_map.81 = bf16[8,8,8,128]{3,2,1,0:T(8,128)(2,1)S(1)} custom-call(s32[8,128]{1,0:T(8,128)S(1)} %get-tuple-element.12.triples_ref, bf16[64,3,8,128]{3,2,1,0:T(8,128)(2,1)S(1)} %all_to_all.22.grads_ref), custom_call_target="tpu_custom_call" | custom-call | tf_op jit(solution)/shard_map/pallas_call | solution.py:30
  67.1 14.1 %all_to_all.23.parts_ref = bf16[8,8,8,128]{3,2,1,0:T(8,128)(2,1)S(1)} all-to-all(bf16[8,8,8,128]{3,2,1,0:T(8,128)(2,1)S(1)} %shard_map.81), channel_id=1, replica_groups=mesh['x'=4,'u'=2,'w'=2,'c'=2,'y'=4,'h'=2] {'y','h'}, dimensions={0} | all-to-all | bytes 262144 | tf_op jit(solution)/shard_map/all_to_all | solution.py:259
  81.2 0.0 copy-done
  81.2 0.0 copy-done.1
  81.2 0.0 copy-done.2
  81.2 1.1 %shard_map.82 = (f32[128,256]{1,0:T(8,128)}, f32[128,256]{1,0:T(8,128)}, f32[128,256]{1,0:T(8,128)}) custom-call(bf16[8,8,8,128]{3,2,1,0:T(8,128)(2,1)S(1)} %all_to_all.23.parts_ref, f32[8,32,128]{2,1,0:T(8,128)S(1)} %get-tuple-element.18.probs_ref, f32[128,256]{1,0:T(8,128)S(1)} %copy-done, f32[128,256]{1,0:T(8,128)S(1)} %copy-done.1, f32[128,256]{1,0:T(8,128)S(1)} %copy-done.2), custom_call_target="tpu_custom_call" | custom-call | tf_op jit(solution)/shard_map/pallas_call | solution.py:30
Async XLA Ops:
  42.5 5.3 %collective-permute-start = (bf16[128,256]{1,0:T(8,128)(2,1)S(1)}, bf16[128,256]{1,0:T(8,128)(2,1)S(1)}, u32[]{:S(2)}, u32[]{:S(2)}) collective-permute-start(bf16[128,256]{1,0:T(8,128)(2,1)S(1)} %get-tuple-element.17), channel_id=1, source_target_pairs={{0,32},{32,0},{1,33},{33,1},{2,34},{34,2},{3,35},{35,3},{4,36},{36... | collective-permute-start | bytes 196616 | tf_op jit(solution)/shard_map/ppermute | solution.py:327
  43.6 37.7 %copy-start = (f32[128,256]{1,0:T(8,128)S(1)}, f32[128,256]{1,0:T(8,128)}, u32[]{:S(2)}) copy-start(f32[128,256]{1,0:T(8,128)} %logits_ref.1) | copy-start | bytes 393220
  43.6 37.7 %copy-start.1 = (f32[128,256]{1,0:T(8,128)S(1)}, f32[128,256]{1,0:T(8,128)}, u32[]{:S(2)}) copy-start(f32[128,256]{1,0:T(8,128)} %first_ref.1) | copy-start | bytes 393220
  43.6 37.7 %copy-start.2 = (f32[128,256]{1,0:T(8,128)S(1)}, f32[128,256]{1,0:T(8,128)}, u32[]{:S(2)}) copy-start(f32[128,256]{1,0:T(8,128)} %second_ref.1) | copy-start | bytes 393220

commit v9 on v8

--- a/solution.py
+++ b/solution.py
@@ -7,17 +7,20 @@
 
 V = 32
 ADAM_STEP = 4
-PARTS = (4, 2, 2, 2, 4, 2)
-NAMES = ("x", "u", "w", "c", "y", "h")
+PARTS = (4, 2, 2, 2, 2, 2, 2)
+NAMES = ("x", "u", "w", "c", "v", "y", "h")
 ROW_AXES = ("x", "u", "w", "c")
-MARG_AXES = ("y", "h")
+MARG_AXES = ("v", "y", "h")
+SIDE_AXES = ("v", "h")
 PLACE_AXES = ("x", "w", "c")
 SHARE_AXES = ("x", "w", "c", "y")
-CHUNKS = 4
-CHUNK = 32
+CHUNKS = 2
+CHUNK = 64
 LANES = CHUNKS * CHUNK
 SUB = V // CHUNKS
+TILE = 8
 MODS = 4
+REST = V // MODS
 VMEM = pl.BlockSpec(memory_space=pltpu.VMEM)
 SMEM = pl.BlockSpec(memory_space=pltpu.SMEM)
 ANY = pl.BlockSpec(memory_space=pl.ANY)
@@ -38,15 +41,16 @@
 
 
 def exchange(blocks):
-    lane = lax.broadcasted_iota(jnp.int32, blocks[0].shape, 1)
-    blocks = list(blocks)
-    for width, pairs in ((2 * CHUNK, ((0, 2), (1, 3))), (CHUNK, ((0, 1), (2, 3)))):
-        low_part = (lane // width) % 2 == 0
-        for a, b in pairs:
-            left, right = blocks[a], blocks[b]
-            blocks[a] = jnp.where(low_part, left, pltpu.roll(right, width, 1))
-            blocks[b] = jnp.where(low_part, pltpu.roll(left, LANES - width, 1), right)
-    return blocks
+    left, right = blocks
+    first = lax.broadcasted_iota(jnp.int32, left.shape, 1) < CHUNK
+    return [
+        jnp.where(first, left, pltpu.roll(right, CHUNK, 1)),
+        jnp.where(first, pltpu.roll(left, CHUNK, 1), right),
+    ]
+
+
+def members(chunk, groups):
+    return [index for index in range(groups) if (index // 2) % CHUNKS == chunk]
 
 
 def stay(value):
@@ -63,44 +67,46 @@
     logits_copy.wait()
     flipped = logits_ref[...].T
     attrs = probs_ref.shape[0]
-    halves = send_ref.shape[0] // CHUNKS
+    groups = send_ref.shape[0]
     for attr in range(attrs):
         block = flipped[attr * V : (attr + 1) * V, :]
         top = jnp.max(block, axis=0, keepdims=True)
         expo = jnp.exp(block - top)
         probs = expo / jnp.sum(expo, axis=0, keepdims=True)
         probs_ref[attr] = probs
-        chunks = exchange([probs[part * SUB : (part + 1) * SUB, :] for part in range(CHUNKS)])
-        for chunk in range(CHUNKS):
-            low = chunks[chunk].astype(LOW)
-            for half in range(halves):
-                send_ref[chunk * halves + half, attr] = low
+        for chunk, packed in enumerate(exchange([probs[part * SUB : (part + 1) * SUB, :] for part in range(CHUNKS)])):
+            low = packed.astype(LOW)
+            for index in members(chunk, groups):
+                send_ref[index, attr] = low
     triples_copy.wait()
     tile_ref[...] = jnp.zeros(tile_ref.shape, F32)
     tile_ref[0:3, 0 : triples_ref.shape[1]] = triples_ref[...].astype(F32)
-    for half in range(halves):
-        tile = (tile_ref[...] * jnp.where(side_ref[0] == half, 1.0, 0.0)).astype(LOW)
+    for side in range(groups // CHUNKS):
+        tile = (tile_ref[...] * jnp.where(side_ref[0] == side, 1.0, 0.0)).astype(LOW)
         for chunk in range(CHUNKS):
-            send_ref[chunk * halves + half, attrs] = tile
+            send_ref[members(chunk, groups)[side], attrs] = tile
 
 
 def select_kernel(full_ref, send_ref, triples_ref, index_ref, scalar_ref, sem):
-    slots = full_ref.shape[0] // (2 * CHUNKS)
+    slots = full_ref.shape[1]
     places = send_ref.shape[0] // CHUNKS
     triples = jnp.zeros(triples_ref.shape, F32)
     for chunk in range(CHUNKS):
-        tile = full_ref[2 * chunk * slots + slots - 1].astype(F32) + full_ref[(2 * chunk + 2) * slots - 1].astype(F32)
-        triples += pltpu.roll(tile, chunk * places, 1) if chunk else tile
+        tile = jnp.zeros((SUB, LANES), F32)
+        for index in members(chunk, full_ref.shape[0]):
+            tile += full_ref[index, slots - 1].astype(F32)
+        triples += pltpu.roll(tile[0:TILE, :], chunk * places, 1) if chunk else tile[0:TILE, :]
     attrs = triples.astype(jnp.int32)
     triples_ref[...] = attrs
     index_ref[...] = attrs + attrs // (slots - 1)
     copy = pltpu.make_async_copy(index_ref, scalar_ref, sem)
     copy.start()
     copy.wait()
+    flat_ref = full_ref.reshape(full_ref.shape[0] * slots, SUB, LANES)
     for place in range(places):
         for chunk in range(CHUNKS):
             for which in range(3):
-                send_ref[place * CHUNKS + chunk, which] = full_ref[scalar_ref[which, chunk * places + place]]
+                send_ref[place * CHUNKS + chunk, which] = flat_ref[scalar_ref[which, chunk * places + place]]
 
 
 def unpack(src_ref, shard):
@@ -148,14 +154,14 @@
 
 def base_kernel(scale, place_ref, own_ref, targets_any, base_ref, block_ref, target_ref, sem):
     place = place_ref[0]
-    start = pl.multiple_of(place // 8 * 8, 8)
-    copy = pltpu.make_async_copy(targets_any.at[pl.ds(start, 8), :], block_ref, sem)
+    start = pl.multiple_of(place // TILE * TILE, TILE)
+    copy = pltpu.make_async_copy(targets_any.at[pl.ds(start, TILE), :], block_ref, sem)
     copy.start()
     copy.wait()
-    mine = lax.broadcasted_iota(jnp.int32, (8, LANES), 0) == lax.rem(place, 8)
-    for rest in range(SUB):
+    mine = lax.broadcasted_iota(jnp.int32, (TILE, LANES), 0) == lax.rem(place, TILE)
+    for rest in range(REST):
         for value in range(V):
-            tile = block_ref[:, pl.ds((value * SUB + rest) * LANES, LANES)]
+            tile = block_ref[:, pl.ds((value * REST + rest) * LANES, LANES)]
             row = jnp.sum(jnp.where(mine, tile, 0.0), axis=0, keepdims=True)
             target_ref[pl.ds(rest * V + value, 1), :] = row
     base_ref[...] = scale * own_ref[...] - target_ref[...].T
@@ -186,7 +192,7 @@
                 low_ref[mod * V : (mod + 1) * V, :], pairs_ref[index, mod], preferred_element_type=F32
             )
             cross = jnp.dot(mask_ref[mod], stacked, preferred_element_type=F32)
-            for rest in range(SUB):
+            for rest in range(REST):
                 value = rest * MODS + mod
                 block = cross[rest * V : (rest + 1) * V, :]
                 first_grad += block * row_ref[pl.ds(value, 1), :]
@@ -232,12 +238,11 @@
     parts_ref, probs_ref, logits_ref, first_ref, second_ref, out_logits_ref, out_first_ref, out_second_ref, grad_ref
 ):
     groups, attrs = parts_ref.shape[0], parts_ref.shape[1]
-    halves = groups // CHUNKS
     chunks = []
     for chunk in range(CHUNKS):
-        total = parts_ref[chunk * halves].astype(F32)
-        for half in range(1, halves):
-            total += parts_ref[chunk * halves + half].astype(F32)
+        total = jnp.zeros((attrs, SUB, LANES), F32)
+        for index in members(chunk, groups):
+            total += parts_ref[index].astype(F32)
         chunks.append(total.reshape(attrs * SUB, LANES))
     parts = exchange(chunks)
     for attr in range(attrs):
@@ -302,7 +307,7 @@
     shape = jax.ShapeDtypeStruct
     tall, wide = V * V // MODS, V * MODS
     place = lax.axis_index(PLACE_AXES).astype(jnp.int32).reshape(1)
-    side = lax.axis_index("h").astype(jnp.int32).reshape(1)
+    side = lax.axis_index(SIDE_AXES).astype(jnp.int32).reshape(1)
     probs, copies = call(
         relax_kernel,
         (shape((attrs, V, rows), F32), shape((groups, attrs + 1, SUB, LANES), LOW)),
@@ -318,10 +323,10 @@
     full = swap(copies, MARG_AXES)
     picked, attributes = call(
         select_kernel,
-        (shape((margs * CHUNKS, 3, SUB, LANES), LOW), shape((SUB, LANES), jnp.int32)),
-        (full.reshape(groups * (attrs + 1), SUB, LANES),),
+        (shape((margs * CHUNKS, 3, SUB, LANES), LOW), shape((TILE, LANES), jnp.int32)),
+        (full,),
         [VMEM],
-        [pltpu.VMEM((SUB, LANES), jnp.int32), pltpu.SMEM((SUB, LANES), jnp.int32), pltpu.SemaphoreType.DMA],
+        [pltpu.VMEM((TILE, LANES), jnp.int32), pltpu.SMEM((TILE, LANES), jnp.int32), pltpu.SemaphoreType.DMA],
     )
     own, send, table, pairs = answers(swap(picked, SHARE_AXES))
     other = lax.ppermute(send, "u", [(0, 1), (1, 0)])
@@ -330,7 +335,7 @@
         shape((wide, tall), F32),
         (place, own, stay(targets)),
         [SMEM, VMEM, ANY],
-        [pltpu.VMEM((8, cells), F32), pltpu.VMEM((tall, wide), F32), pltpu.SemaphoreType.DMA],
+        [pltpu.VMEM((TILE, cells), F32), pltpu.VMEM((tall, wide), F32), pltpu.SemaphoreType.DMA],
     )
     returned = swap(backward(scale, table, pairs, base, other), SHARE_AXES)
     totals = call(

time: 82.5 us -> 84.7 us (1.027)
  blocking collectives: 68.2 us -> 70.6 us
    all_to_all x4, blocking collectives: 68.2 us -> 70.6 us  [swap(): return lax.all_to_all(value, axes, 0, 0, tiled=True)]
where the time goes in v9:
time: 84.7 us; the launch traced here: 84.5 us
  blocking collectives  70.6 us (83%)
  Pallas kernels  9.09 us (11%)
  waiting for transfers between devices  2.99 us (4%)
  starting transfers between devices  1.11 us (1%)
    all_to_all x4, blocking collectives, swap(): return lax.all_to_all(value, axes, 0, 0, tiled=True)  70.6 us
    pallas_call x7, Pallas kernels, call(): pl.pallas_call(body, out_shape=out_shape, in_specs=specs, out_specs=jax.t...  9.09 us
    ppermute x1, waiting for transfers between devices, shards(): other = lax.ppermute(send, 'u', [(0, 1), (1, 0)])  2.99 us
  transfers between devices with their start and end apart: 1, of which 1 were waited for; matrix products, arithmetic and copies ran while one was open for 0% of the time, Pallas kernels for 2%

profile of v9, /device:TPU:32, one launch (start us, length us, event | category | flops | bytes accessed | tf_op | source)
XLA Modules:
  0.0 84.5 jit_solution(16424822896688682911)
XLA Ops:
  0.6 1.2 %shard_map.76 = (f32[8,32,128]{2,1,0:T(8,128)S(1)}, bf16[8,9,16,128]{3,2,1,0:T(8,128)(2,1)S(1)}) custom-call(s32[1]{0:T(128)} %bitcast.side_ref, s32[1]{0:T(128)} %bitcast.1.place_ref.refs_0_, s32[3,16]{1,0:T(4,128)} %bitcast.3, f32[128,256]{1,0:T(8,128)} %logits_ref.1), custom_call_target="tpu_custom_call" | custom-call | tf_op jit(solution)/shard_map/pallas_call | solution.py:33
  1.8 24.9 %all_to_all.20.full_ref = bf16[8,9,16,128]{3,2,1,0:T(8,128)(2,1)S(1)} all-to-all(bf16[8,9,16,128]{3,2,1,0:T(8,128)(2,1)S(1)} %get-tuple-element.11), channel_id=1, replica_groups=mesh['x'=4,'u'=2,'w'=2,'c'=2,'v'=2,'y'=2,'h'=2] {'v','y','h'}, dimensions={0} | all-to-all | bytes 589824 | tf_op jit(solution)/shard_map/all_to_all | solution.py:264
  26.7 0.8 shard_map.77
  27.5 14.0 %all_to_all.21.src_ref = bf16[32,3,16,128]{3,2,1,0:T(8,128)(2,1)S(1)} all-to-all(bf16[32,3,16,128]{3,2,1,0:T(8,128)(2,1)S(1)} %get-tuple-element.13), channel_id=1, replica_groups=mesh['x'=4,'u'=2,'w'=2,'c'=2,'v'=2,'y'=2,'h'=2] {'x','w','c','y'}, dimensions={0} | all-to-all | bytes 786432 | tf_op jit(solution)/shard_map/all_to_all | solution.py:264
  41.5 1.4 %shard_map.78 = (f32[128,256]{1,0:T(8,128)S(1)}, bf16[128,256]{1,0:T(8,128)(2,1)S(1)}, bf16[16,3,32,128]{3,2,1,0:T(8,128)(2,1)S(1)}, bf16[8,4,256,256]{3,2,1,0:T(8,128)(2,1)S(1)}) custom-call(bf16[32,3,16,128]{3,2,1,0:T(8,128)(2,1)S(1)} %all_to_all.21.src_ref), custom_call_target="tpu_custom_call" | custom-call | tf_op jit(solution)/shard_map/pallas_call | solution.py:33
  42.9 1.1 %collective-permute-start = (bf16[128,256]{1,0:T(8,128)(2,1)S(1)}, bf16[128,256]{1,0:T(8,128)(2,1)S(1)}, u32[]{:S(2)}, u32[]{:S(2)}) collective-permute-start(bf16[128,256]{1,0:T(8,128)(2,1)S(1)} %get-tuple-element.17), channel_id=1, source_target_pairs={{0,32},{32,0},{1,33},{33,1},{2,34},{34,2},{3,35},{35,3},{4,36},{36... | collective-permute-start | bytes 196616 | tf_op jit(solution)/shard_map/ppermute | solution.py:332
  44.0 0.0 copy-start
  44.0 0.0 copy-start.1
  44.0 0.0 copy-start.2
  44.0 1.7 %shard_map.79.refs_2_ = f32[128,256]{1,0:T(8,128)S(1)} custom-call(s32[1]{0:T(128)} %bitcast.1.place_ref.refs_0_, f32[128,256]{1,0:T(8,128)S(1)} %get-tuple-element.16.refs_1_, f32[16,32768]{1,0:T(8,128)} %refs_2_.1), custom_call_target="tpu_custom_call" | custom-call | tf_op jit(solution)/shard_map/pallas_call | solution.py:33
  45.7 3.0 %collective-permute-done.refs_3_ = bf16[128,256]{1,0:T(8,128)(2,1)S(1)} collective-permute-done((bf16[128,256]{1,0:T(8,128)(2,1)S(1)}, bf16[128,256]{1,0:T(8,128)(2,1)S(1)}, u32[]{:S(2)}, u32[]{:S(2)}) %collective-permute-start) | collective-permute-done | bytes 65568 | tf_op jit(solution)/shard_map/ppermute | solution.py:332
  48.7 2.1 %shard_map.80 = bf16[32,3,16,128]{3,2,1,0:T(8,128)(2,1)S(1)} custom-call(bf16[16,3,32,128]{3,2,1,0:T(8,128)(2,1)S(1)} %get-tuple-element.14.refs_0_, bf16[8,4,256,256]{3,2,1,0:T(8,128)(2,1)S(1)} %get-tuple-element.15.refs_1_, f32[128,256]{1,0:T(8,128)S(1)} %shard_map.79.refs_2_, bf16[128,256]{1,0:T(8,128)(2,1)S(1)} %collective-permute-done.refs_3_), custom_call_target="tpu_custom_call" | custom-call | tf_op jit(solution)/shard_map/pallas_call | solution.py:33
  50.8 13.7 %all_to_all.22.grads_ref = bf16[32,3,16,128]{3,2,1,0:T(8,128)(2,1)S(1)} all-to-all(bf16[32,3,16,128]{3,2,1,0:T(8,128)(2,1)S(1)} %shard_map.80), channel_id=1, replica_groups=mesh['x'=4,'u'=2,'w'=2,'c'=2,'v'=2,'y'=2,'h'=2] {'x','w','c','y'}, dimensions={0} | all-to-all | bytes 786432 | tf_op jit(solution)/shard_map/all_to_all | solution.py:264
  64.5 1.0 %shard_map.81 = bf16[8,8,16,128]{3,2,1,0:T(8,128)(2,1)S(1)} custom-call(s32[8,128]{1,0:T(8,128)S(1)} %get-tuple-element.12.triples_ref, bf16[32,3,16,128]{3,2,1,0:T(8,128)(2,1)S(1)} %all_to_all.22.grads_ref), custom_call_target="tpu_custom_call" | custom-call | tf_op jit(solution)/shard_map/pallas_call | solution.py:33
  65.5 18.0 %all_to_all.23.parts_ref = bf16[8,8,16,128]{3,2,1,0:T(8,128)(2,1)S(1)} all-to-all(bf16[8,8,16,128]{3,2,1,0:T(8,128)(2,1)S(1)} %shard_map.81), channel_id=1, replica_groups=mesh['x'=4,'u'=2,'w'=2,'c'=2,'v'=2,'y'=2,'h'=2] {'v','y','h'}, dimensions={0} | all-to-all | bytes 524288 | tf_op jit(solution)/shard_map/all_to_all | solution.py:264
  83.5 0.0 copy-done
  83.5 0.0 copy-done.1
  83.5 0.0 copy-done.2
  83.5 1.0 %shard_map.82 = (f32[128,256]{1,0:T(8,128)}, f32[128,256]{1,0:T(8,128)}, f32[128,256]{1,0:T(8,128)}) custom-call(bf16[8,8,16,128]{3,2,1,0:T(8,128)(2,1)S(1)} %all_to_all.23.parts_ref, f32[8,32,128]{2,1,0:T(8,128)S(1)} %get-tuple-element.18.probs_ref, f32[128,256]{1,0:T(8,128)S(1)} %copy-done, f32[128,256]{1,0:T(8,128)S(1)} %copy-done.1, f32[128,256]{1,0:T(8,128)S(1)} %copy-done.2), custom_call_target="tpu_custom_call" | custom-call | tf_op jit(solution)/shard_map/pallas_call | solution.py:33
Async XLA Ops:
  42.9 5.8 %collective-permute-start = (bf16[128,256]{1,0:T(8,128)(2,1)S(1)}, bf16[128,256]{1,0:T(8,128)(2,1)S(1)}, u32[]{:S(2)}, u32[]{:S(2)}) collective-permute-start(bf16[128,256]{1,0:T(8,128)(2,1)S(1)} %get-tuple-element.17), channel_id=1, source_target_pairs={{0,32},{32,0},{1,33},{33,1},{2,34},{34,2},{3,35},{35,3},{4,36},{36... | collective-permute-start | bytes 196616 | tf_op jit(solution)/shard_map/ppermute | solution.py:332
  44.0 39.4 %copy-start = (f32[128,256]{1,0:T(8,128)S(1)}, f32[128,256]{1,0:T(8,128)}, u32[]{:S(2)}) copy-start(f32[128,256]{1,0:T(8,128)} %logits_ref.1) | copy-start | bytes 393220
  44.0 39.4 %copy-start.1 = (f32[128,256]{1,0:T(8,128)S(1)}, f32[128,256]{1,0:T(8,128)}, u32[]{:S(2)}) copy-start(f32[128,256]{1,0:T(8,128)} %first_ref.1) | copy-start | bytes 393220
  44.0 39.4 %copy-start.2 = (f32[128,256]{1,0:T(8,128)S(1)}, f32[128,256]{1,0:T(8,128)}, u32[]{:S(2)}) copy-start(f32[128,256]{1,0:T(8,128)} %second_ref.1) | copy-start | bytes 393220

commit v10 on v8

--- a/solution.py
+++ b/solution.py
@@ -18,6 +18,7 @@
 LANES = CHUNKS * CHUNK
 SUB = V // CHUNKS
 MODS = 4
+MARGS = 16
 VMEM = pl.BlockSpec(memory_space=pltpu.VMEM)
 SMEM = pl.BlockSpec(memory_space=pltpu.SMEM)
 ANY = pl.BlockSpec(memory_space=pl.ANY)
@@ -54,53 +55,85 @@
 
 
 def relax_kernel(
-    side_ref, place_ref, triples_hbm, logits_hbm, probs_ref, send_ref, tile_ref, triples_ref, logits_ref, sems
+    side_ref,
+    place_ref,
+    triples_hbm,
+    logits_hbm,
+    probs_ref,
+    send_ref,
+    tile_ref,
+    triples_ref,
+    logits_ref,
+    flipped_ref,
+    sems,
 ):
     logits_copy = pltpu.make_async_copy(logits_hbm, logits_ref, sems.at[0])
     triples_copy = pltpu.make_async_copy(triples_hbm, triples_ref, sems.at[1])
     logits_copy.start()
     triples_copy.start()
     logits_copy.wait()
-    flipped = logits_ref[...].T
-    attrs = probs_ref.shape[0]
+    flipped_ref[...] = logits_ref[...].T
+    attrs = probs_ref.shape[1]
     halves = send_ref.shape[0] // CHUNKS
-    for attr in range(attrs):
-        block = flipped[attr * V : (attr + 1) * V, :]
-        top = jnp.max(block, axis=0, keepdims=True)
-        expo = jnp.exp(block - top)
-        probs = expo / jnp.sum(expo, axis=0, keepdims=True)
-        probs_ref[attr] = probs
-        chunks = exchange([probs[part * SUB : (part + 1) * SUB, :] for part in range(CHUNKS)])
-        for chunk in range(CHUNKS):
-            low = chunks[chunk].astype(LOW)
+    values = [flipped_ref[pl.ds(value, attrs, stride=V), :] for value in range(V)]
+    top = values[0]
+    for value in values[1:]:
+        top = jnp.maximum(top, value)
+    expos = [jnp.exp(value - top) for value in values]
+    total = expos[0]
+    for expo in expos[1:]:
+        total = total + expo
+    probs = [expo / total for expo in expos]
+    for value in range(V):
+        probs_ref[value] = probs[value]
+    for rest in range(SUB):
+        for chunk, packed in enumerate(exchange([probs[part * SUB + rest] for part in range(CHUNKS)])):
+            low = packed.astype(LOW)
             for half in range(halves):
-                send_ref[chunk * halves + half, attr] = low
+                send_ref[chunk * halves + half, :, rest * LANES : (rest + 1) * LANES] = low
     triples_copy.wait()
     tile_ref[...] = jnp.zeros(tile_ref.shape, F32)
     tile_ref[0:3, 0 : triples_ref.shape[1]] = triples_ref[...].astype(F32)
     for half in range(halves):
         tile = (tile_ref[...] * jnp.where(side_ref[0] == half, 1.0, 0.0)).astype(LOW)
         for chunk in range(CHUNKS):
-            send_ref[chunk * halves + half, attrs] = tile
-
-
-def select_kernel(full_ref, send_ref, triples_ref, index_ref, scalar_ref, sem):
-    slots = full_ref.shape[0] // (2 * CHUNKS)
-    places = send_ref.shape[0] // CHUNKS
+            send_ref[chunk * halves + half, :, SUB * LANES :] = tile
+
+
+def one_hot(triples, which, count):
+    width = CHUNKS * MARGS
+    row = jnp.broadcast_to(triples[which : which + 1, 0:width], (count, width))
+    attr = lax.broadcasted_iota(jnp.int32, (count, width), 0).astype(F32)
+    return jnp.where(row == attr, 1.0, 0.0).astype(LOW)
+
+
+def tile_rows(which, rest):
+    step = 3 * SUB
+    for chunk in range(CHUNKS):
+        for start in range(0, MARGS, SUB):
+            rows = pl.ds((start * CHUNKS + chunk) * step + which * SUB + rest, SUB, stride=CHUNKS * step)
+            yield rows, chunk * MARGS + start
+
+
+def select_kernel(full_ref, send_ref, triples_ref, picked_ref):
+    groups, attrs = full_ref.shape[0], full_ref.shape[1]
+    halves = groups // CHUNKS
+    full = [full_ref[index].astype(F32) for index in range(groups)]
     triples = jnp.zeros(triples_ref.shape, F32)
     for chunk in range(CHUNKS):
-        tile = full_ref[2 * chunk * slots + slots - 1].astype(F32) + full_ref[(2 * chunk + 2) * slots - 1].astype(F32)
-        triples += pltpu.roll(tile, chunk * places, 1) if chunk else tile
-    attrs = triples.astype(jnp.int32)
-    triples_ref[...] = attrs
-    index_ref[...] = attrs + attrs // (slots - 1)
-    copy = pltpu.make_async_copy(index_ref, scalar_ref, sem)
-    copy.start()
-    copy.wait()
-    for place in range(places):
-        for chunk in range(CHUNKS):
-            for which in range(3):
-                send_ref[place * CHUNKS + chunk, which] = full_ref[scalar_ref[which, chunk * places + place]]
+        tile = full[chunk * halves][:, SUB * LANES :]
+        for half in range(1, halves):
+            tile += full[chunk * halves + half][:, SUB * LANES :]
+        triples += pltpu.roll(tile, chunk * MARGS, 1) if chunk else tile
+    triples_ref[...] = triples
+    table = jnp.concatenate([value[:, 0 : SUB * LANES] for value in full], axis=0).astype(LOW)
+    for which in range(3):
+        mine = one_hot(triples, which, groups * attrs)
+        picked = lax.dot_general(mine, table, (((0,), (0,)), ((), ())), preferred_element_type=F32)
+        for rest in range(SUB):
+            for rows, place in tile_rows(which, rest):
+                picked_ref[rows, :] = picked[place : place + SUB, rest * LANES : (rest + 1) * LANES]
+    send_ref[...] = picked_ref[...].reshape(send_ref.shape).astype(LOW)
 
 
 def unpack(src_ref, shard):
@@ -214,18 +247,20 @@
     lax.fori_loop(0, steps, step, 0, unroll=steps)
 
 
-def collect_kernel(triples_ref, grads_ref, send_ref, *total_refs):
+def collect_kernel(triples_ref, grads_ref, send_ref, grad_ref):
     groups, attrs = send_ref.shape[0], send_ref.shape[1]
-    places = grads_ref.shape[0] // CHUNKS
-    for total_ref in total_refs:
-        total_ref[...] = jnp.zeros(total_ref.shape, F32)
-    for place in range(places):
-        for chunk in range(CHUNKS):
-            for which, total_ref in enumerate(total_refs):
-                attr = triples_ref[which, chunk * places + place]
-                total_ref[attr] = total_ref[attr] + grads_ref[place * CHUNKS + chunk, which].astype(F32)
-    total = total_refs[0][...] + total_refs[1][...] + total_refs[2][...]
-    send_ref[...] = total.reshape(groups, attrs, SUB, LANES).astype(LOW)
+    triples = triples_ref[...]
+    grad_ref[...] = grads_ref[...].astype(F32).reshape(grad_ref.shape)
+    total = jnp.zeros((groups * attrs, SUB * LANES), F32)
+    for which in range(3):
+        parts = []
+        for rest in range(SUB):
+            tiles = [grad_ref[rows, :] for rows, unused in tile_rows(which, rest)]
+            parts.append(jnp.concatenate(tiles, axis=0))
+        grads = jnp.concatenate(parts, axis=1).astype(LOW)
+        total += jnp.dot(one_hot(triples, which, groups * attrs), grads, preferred_element_type=F32)
+    for index in range(groups):
+        send_ref[index] = total[index * attrs : (index + 1) * attrs, :].astype(LOW)
 
 
 def adam_kernel(
@@ -238,13 +273,17 @@
         total = parts_ref[chunk * halves].astype(F32)
         for half in range(1, halves):
             total += parts_ref[chunk * halves + half].astype(F32)
-        chunks.append(total.reshape(attrs * SUB, LANES))
-    parts = exchange(chunks)
-    for attr in range(attrs):
-        row_grad = jnp.concatenate([part[attr * SUB : (attr + 1) * SUB, :] for part in parts], axis=0)
-        probs = probs_ref[attr]
-        inner = jnp.sum(probs * row_grad, axis=0, keepdims=True)
-        grad_ref[attr * V : (attr + 1) * V, :] = 512.0 * probs * (row_grad - inner)
+        chunks.append(total)
+    row_grad = [None] * V
+    for rest in range(SUB):
+        blocks = [chunk[:, rest * LANES : (rest + 1) * LANES] for chunk in chunks]
+        for part, block in enumerate(exchange(blocks)):
+            row_grad[part * SUB + rest] = block
+    inner = jnp.zeros((attrs, LANES), F32)
+    for value in range(V):
+        inner += probs_ref[value] * row_grad[value]
+    for value in range(V):
+        grad_ref[pl.ds(value, attrs, stride=V), :] = 512.0 * probs_ref[value] * (row_grad[value] - inner)
     grad = grad_ref[...].T
     new_first = 0.9 * first_ref[...] + 0.1 * grad
     new_second = 0.999 * second_ref[...] + 0.001 * grad * grad
@@ -305,23 +344,24 @@
     side = lax.axis_index("h").astype(jnp.int32).reshape(1)
     probs, copies = call(
         relax_kernel,
-        (shape((attrs, V, rows), F32), shape((groups, attrs + 1, SUB, LANES), LOW)),
+        (shape((V, attrs, rows), F32), shape((groups, attrs, (SUB + 1) * LANES), LOW)),
         (side, place, stay(triples.T), stay(logits)),
         [SMEM, SMEM, ANY, ANY],
         [
             pltpu.VMEM((SUB, LANES), F32),
             pltpu.VMEM((3, margs), jnp.int32),
             pltpu.VMEM((rows, cols), F32),
+            pltpu.VMEM((cols, rows), F32),
             pltpu.SemaphoreType.DMA((2,)),
         ],
     )
     full = swap(copies, MARG_AXES)
     picked, attributes = call(
         select_kernel,
-        (shape((margs * CHUNKS, 3, SUB, LANES), LOW), shape((SUB, LANES), jnp.int32)),
-        (full.reshape(groups * (attrs + 1), SUB, LANES),),
+        (shape((margs * CHUNKS, 3, SUB, LANES), LOW), shape((SUB, LANES), F32)),
+        (full,),
         [VMEM],
-        [pltpu.VMEM((SUB, LANES), jnp.int32), pltpu.SMEM((SUB, LANES), jnp.int32), pltpu.SemaphoreType.DMA],
+        [pltpu.VMEM((margs * CHUNKS * 3 * SUB, LANES), F32)],
     )
     own, send, table, pairs = answers(swap(picked, SHARE_AXES))
     other = lax.ppermute(send, "u", [(0, 1), (1, 0)])
@@ -335,10 +375,10 @@
     returned = swap(backward(scale, table, pairs, base, other), SHARE_AXES)
     totals = call(
         collect_kernel,
-        shape((groups, attrs, SUB, LANES), LOW),
+        shape((groups, attrs, SUB * LANES), LOW),
         (attributes, returned),
-        [SMEM, VMEM],
-        [pltpu.VMEM((groups * attrs, SUB, LANES), F32)] * 3,
+        [VMEM, VMEM],
+        [pltpu.VMEM((margs * CHUNKS * 3 * SUB, LANES), F32)],
     )
     return call(
         adam_kernel,

time: 82.5 us -> 82.3 us (level)
  no operation moved by 1% of the time
where the time goes in v10:
time: 82.3 us; the launch traced here: 82 us
  blocking collectives  68.2 us (83%)
  Pallas kernels  9.45 us (11%)
  waiting for transfers between devices  2.5 us (3%)
  starting transfers between devices  1.08 us (1%)
    all_to_all x4, blocking collectives, swap(): return lax.all_to_all(value, axes, 0, 0, tiled=True)  68.2 us
    pallas_call x7, Pallas kernels, call(): pl.pallas_call(body, out_shape=out_shape, in_specs=specs, out_specs=jax.t...  9.45 us
    ppermute x1, waiting for transfers between devices, shards(): other = lax.ppermute(send, 'u', [(0, 1), (1, 0)])  2.5 us
  transfers between devices with their start and end apart: 1, of which 1 were waited for; matrix products, arithmetic and copies ran while one was open for 0% of the time, Pallas kernels for 2%

profile of v10, /device:TPU:32, one launch (start us, length us, event | category | flops | bytes accessed | tf_op | source)
XLA Modules:
  0.0 82.0 jit_solution(3808006663657022847)
XLA Ops:
  0.6 1.3 %shard_map.76 = (f32[32,8,128]{2,1,0:T(8,128)S(1)}, bf16[8,8,1152]{2,1,0:T(8,128)(2,1)S(1)}) custom-call(s32[1]{0:T(128)} %bitcast.side_ref, s32[1]{0:T(128)} %bitcast.1.place_ref.refs_0_, s32[3,16]{1,0:T(4,128)} %bitcast.3, f32[128,256]{1,0:T(8,128)} %logits_ref.1), custom_call_target="tpu_custom_call" | custom-call | tf_op jit(solution)/shard_map/pallas_call | solution.py:31
  2.0 21.6 %all_to_all.20.full_ref = bf16[8,8,1152]{2,1,0:T(8,128)(2,1)S(1)} all-to-all(bf16[8,8,1152]{2,1,0:T(8,128)(2,1)S(1)} %get-tuple-element.11), channel_id=1, replica_groups=mesh['x'=4,'u'=2,'w'=2,'c'=2,'y'=4,'h'=2] {'y','h'}, dimensions={0} | all-to-all | bytes 294912 | tf_op jit(solution)/shard_map/all_to_all | solution.py:298
  23.6 0.7 shard_map.77
  24.3 16.4 %all_to_all.21.src_ref = bf16[64,3,8,128]{3,2,1,0:T(8,128)(2,1)S(1)} all-to-all(bf16[64,3,8,128]{3,2,1,0:T(8,128)(2,1)S(1)} %get-tuple-element.13), channel_id=1, replica_groups=mesh['x'=4,'u'=2,'w'=2,'c'=2,'y'=4,'h'=2] {'x','w','c','y'}, dimensions={0} | all-to-all | bytes 786432 | tf_op jit(solution)/shard_map/all_to_all | solution.py:298
  40.8 1.6 %shard_map.78 = (f32[128,256]{1,0:T(8,128)S(1)}, bf16[128,256]{1,0:T(8,128)(2,1)S(1)}, bf16[16,3,32,128]{3,2,1,0:T(8,128)(2,1)S(1)}, bf16[8,4,256,256]{3,2,1,0:T(8,128)(2,1)S(1)}) custom-call(bf16[64,3,8,128]{3,2,1,0:T(8,128)(2,1)S(1)} %all_to_all.21.src_ref), custom_call_target="tpu_custom_call" | custom-call | tf_op jit(solution)/shard_map/pallas_call | solution.py:31
  42.4 1.1 %collective-permute-start = (bf16[128,256]{1,0:T(8,128)(2,1)S(1)}, bf16[128,256]{1,0:T(8,128)(2,1)S(1)}, u32[]{:S(2)}, u32[]{:S(2)}) collective-permute-start(bf16[128,256]{1,0:T(8,128)(2,1)S(1)} %get-tuple-element.17), channel_id=1, source_target_pairs={{0,32},{32,0},{1,33},{33,1},{2,34},{34,2},{3,35},{35,3},{4,36},{36... | collective-permute-start | bytes 196616 | tf_op jit(solution)/shard_map/ppermute | solution.py:367
  43.5 0.0 copy-start
  43.5 0.0 copy-start.1
  43.5 0.0 copy-start.2
  43.5 1.7 %shard_map.79.refs_2_ = f32[128,256]{1,0:T(8,128)S(1)} custom-call(s32[1]{0:T(128)} %bitcast.1.place_ref.refs_0_, f32[128,256]{1,0:T(8,128)S(1)} %get-tuple-element.16.refs_1_, f32[16,32768]{1,0:T(8,128)} %refs_2_.1), custom_call_target="tpu_custom_call" | custom-call | tf_op jit(solution)/shard_map/pallas_call | solution.py:31
  45.2 2.5 %collective-permute-done.refs_3_ = bf16[128,256]{1,0:T(8,128)(2,1)S(1)} collective-permute-done((bf16[128,256]{1,0:T(8,128)(2,1)S(1)}, bf16[128,256]{1,0:T(8,128)(2,1)S(1)}, u32[]{:S(2)}, u32[]{:S(2)}) %collective-permute-start) | collective-permute-done | bytes 65568 | tf_op jit(solution)/shard_map/ppermute | solution.py:367
  47.7 2.3 %shard_map.80 = bf16[64,3,8,128]{3,2,1,0:T(8,128)(2,1)S(1)} custom-call(bf16[16,3,32,128]{3,2,1,0:T(8,128)(2,1)S(1)} %get-tuple-element.14.refs_0_, bf16[8,4,256,256]{3,2,1,0:T(8,128)(2,1)S(1)} %get-tuple-element.15.refs_1_, f32[128,256]{1,0:T(8,128)S(1)} %shard_map.79.refs_2_, bf16[128,256]{1,0:T(8,128)(2,1)S(1)} %collective-permute-done.refs_3_), custom_call_target="tpu_custom_call" | custom-call | tf_op jit(solution)/shard_map/pallas_call | solution.py:31
  50.0 16.0 %all_to_all.22.grads_ref = bf16[64,3,8,128]{3,2,1,0:T(8,128)(2,1)S(1)} all-to-all(bf16[64,3,8,128]{3,2,1,0:T(8,128)(2,1)S(1)} %shard_map.80), channel_id=1, replica_groups=mesh['x'=4,'u'=2,'w'=2,'c'=2,'y'=4,'h'=2] {'x','w','c','y'}, dimensions={0} | all-to-all | bytes 786432 | tf_op jit(solution)/shard_map/all_to_all | solution.py:298
  66.0 0.7 shard_map.81
  66.7 14.1 %all_to_all.23.parts_ref = bf16[8,8,1024]{2,1,0:T(8,128)(2,1)S(1)} all-to-all(bf16[8,8,1024]{2,1,0:T(8,128)(2,1)S(1)} %shard_map.81), channel_id=1, replica_groups=mesh['x'=4,'u'=2,'w'=2,'c'=2,'y'=4,'h'=2] {'y','h'}, dimensions={0} | all-to-all | bytes 262144 | tf_op jit(solution)/shard_map/all_to_all | solution.py:298
  80.8 0.0 copy-done
  80.8 0.0 copy-done.1
  80.8 0.0 copy-done.2
  80.8 1.2 %shard_map.82 = (f32[128,256]{1,0:T(8,128)}, f32[128,256]{1,0:T(8,128)}, f32[128,256]{1,0:T(8,128)}) custom-call(bf16[8,8,1024]{2,1,0:T(8,128)(2,1)S(1)} %all_to_all.23.parts_ref, f32[32,8,128]{2,1,0:T(8,128)S(1)} %get-tuple-element.18.probs_ref, f32[128,256]{1,0:T(8,128)S(1)} %copy-done, f32[128,256]{1,0:T(8,128)S(1)} %copy-done.1, f32[128,256]{1,0:T(8,128)S(1)} %copy-done.2), custom_call_target="tpu_custom_call" | custom-call | tf_op jit(solution)/shard_map/pallas_call | solution.py:31
Async XLA Ops:
  42.4 5.3 %collective-permute-start = (bf16[128,256]{1,0:T(8,128)(2,1)S(1)}, bf16[128,256]{1,0:T(8,128)(2,1)S(1)}, u32[]{:S(2)}, u32[]{:S(2)}) collective-permute-start(bf16[128,256]{1,0:T(8,128)(2,1)S(1)} %get-tuple-element.17), channel_id=1, source_target_pairs={{0,32},{32,0},{1,33},{33,1},{2,34},{34,2},{3,35},{35,3},{4,36},{36... | collective-permute-start | bytes 196616 | tf_op jit(solution)/shard_map/ppermute | solution.py:367
  43.5 37.3 %copy-start = (f32[128,256]{1,0:T(8,128)S(1)}, f32[128,256]{1,0:T(8,128)}, u32[]{:S(2)}) copy-start(f32[128,256]{1,0:T(8,128)} %logits_ref.1) | copy-start | bytes 393220
  43.5 37.3 %copy-start.1 = (f32[128,256]{1,0:T(8,128)S(1)}, f32[128,256]{1,0:T(8,128)}, u32[]{:S(2)}) copy-start(f32[128,256]{1,0:T(8,128)} %first_ref.1) | copy-start | bytes 393220
  43.5 37.3 %copy-start.2 = (f32[128,256]{1,0:T(8,128)S(1)}, f32[128,256]{1,0:T(8,128)}, u32[]{:S(2)}) copy-start(f32[128,256]{1,0:T(8,128)} %second_ref.1) | copy-start | bytes 393220

commit v11 on v10

--- a/solution.py
+++ b/solution.py
@@ -229,12 +229,14 @@
                     partial += product[8 * part : 8 * part + 8]
                 for half in range(2):
                     sum_ref[half, value * 8 : value * 8 + 8, :] = partial[:, half * LANES : (half + 1) * LANES]
+        mean = jnp.sum(first * first_grad, axis=0, keepdims=True)
         for half in range(2):
             lanes = slice(half * LANES, (half + 1) * LANES)
             second_grad = jnp.zeros((V, LANES), F32)
             for part in range(8):
                 second_grad += sum_ref[half, pl.ds(part, V, stride=8), :]
-            grads = (first_grad[:, lanes], second_grad, third_grad[:, lanes])
+            centre = jnp.broadcast_to(mean[:, lanes], (V, LANES))
+            grads = [grad - centre for grad in (first_grad[:, lanes], second_grad, third_grad[:, lanes])]
             parts = [
                 jnp.concatenate([grad[part * SUB : (part + 1) * SUB, :] for grad in grads], axis=0)
                 for part in range(CHUNKS)

time: 82.3 us -> 82.3 us (level)
  no operation moved by 1% of the time
where the time goes in v11:
time: 82.3 us; the launch traced here: 82.1 us
  blocking collectives  68.2 us (83%)
  Pallas kernels  9.53 us (12%)
  waiting for transfers between devices  2.5 us (3%)
  starting transfers between devices  1.08 us (1%)
    all_to_all x4, blocking collectives, swap(): return lax.all_to_all(value, axes, 0, 0, tiled=True)  68.2 us
    pallas_call x7, Pallas kernels, call(): pl.pallas_call(body, out_shape=out_shape, in_specs=specs, out_specs=jax.t...  9.53 us
    ppermute x1, waiting for transfers between devices, shards(): other = lax.ppermute(send, 'u', [(0, 1), (1, 0)])  2.5 us
  transfers between devices with their start and end apart: 1, of which 1 were waited for; matrix products, arithmetic and copies ran while one was open for 0% of the time, Pallas kernels for 2%

profile of v11, /device:TPU:32, one launch (start us, length us, event | category | flops | bytes accessed | tf_op | source)
XLA Modules:
  0.0 82.1 jit_solution(14602157704531855635)
XLA Ops:
  0.6 1.3 %shard_map.76 = (f32[32,8,128]{2,1,0:T(8,128)S(1)}, bf16[8,8,1152]{2,1,0:T(8,128)(2,1)S(1)}) custom-call(s32[1]{0:T(128)} %bitcast.side_ref, s32[1]{0:T(128)} %bitcast.1.place_ref.refs_0_, s32[3,16]{1,0:T(4,128)} %bitcast.3, f32[128,256]{1,0:T(8,128)} %logits_ref.1), custom_call_target="tpu_custom_call" | custom-call | tf_op jit(solution)/shard_map/pallas_call | solution.py:31
  2.0 21.6 %all_to_all.20.full_ref = bf16[8,8,1152]{2,1,0:T(8,128)(2,1)S(1)} all-to-all(bf16[8,8,1152]{2,1,0:T(8,128)(2,1)S(1)} %get-tuple-element.11), channel_id=1, replica_groups=mesh['x'=4,'u'=2,'w'=2,'c'=2,'y'=4,'h'=2] {'y','h'}, dimensions={0} | all-to-all | bytes 294912 | tf_op jit(solution)/shard_map/all_to_all | solution.py:300
  23.6 0.7 shard_map.77
  24.3 16.4 %all_to_all.21.src_ref = bf16[64,3,8,128]{3,2,1,0:T(8,128)(2,1)S(1)} all-to-all(bf16[64,3,8,128]{3,2,1,0:T(8,128)(2,1)S(1)} %get-tuple-element.13), channel_id=1, replica_groups=mesh['x'=4,'u'=2,'w'=2,'c'=2,'y'=4,'h'=2] {'x','w','c','y'}, dimensions={0} | all-to-all | bytes 786432 | tf_op jit(solution)/shard_map/all_to_all | solution.py:300
  40.8 1.6 %shard_map.78 = (f32[128,256]{1,0:T(8,128)S(1)}, bf16[128,256]{1,0:T(8,128)(2,1)S(1)}, bf16[16,3,32,128]{3,2,1,0:T(8,128)(2,1)S(1)}, bf16[8,4,256,256]{3,2,1,0:T(8,128)(2,1)S(1)}) custom-call(bf16[64,3,8,128]{3,2,1,0:T(8,128)(2,1)S(1)} %all_to_all.21.src_ref), custom_call_target="tpu_custom_call" | custom-call | tf_op jit(solution)/shard_map/pallas_call | solution.py:31
  42.4 1.1 %collective-permute-start = (bf16[128,256]{1,0:T(8,128)(2,1)S(1)}, bf16[128,256]{1,0:T(8,128)(2,1)S(1)}, u32[]{:S(2)}, u32[]{:S(2)}) collective-permute-start(bf16[128,256]{1,0:T(8,128)(2,1)S(1)} %get-tuple-element.17), channel_id=1, source_target_pairs={{0,32},{32,0},{1,33},{33,1},{2,34},{34,2},{3,35},{35,3},{4,36},{36... | collective-permute-start | bytes 196616 | tf_op jit(solution)/shard_map/ppermute | solution.py:369
  43.5 0.0 copy-start
  43.5 0.0 copy-start.1
  43.5 0.0 copy-start.2
  43.5 1.7 %shard_map.79.refs_2_ = f32[128,256]{1,0:T(8,128)S(1)} custom-call(s32[1]{0:T(128)} %bitcast.1.place_ref.refs_0_, f32[128,256]{1,0:T(8,128)S(1)} %get-tuple-element.16.refs_1_, f32[16,32768]{1,0:T(8,128)} %refs_2_.1), custom_call_target="tpu_custom_call" | custom-call | tf_op jit(solution)/shard_map/pallas_call | solution.py:31
  45.2 2.5 %collective-permute-done.refs_3_ = bf16[128,256]{1,0:T(8,128)(2,1)S(1)} collective-permute-done((bf16[128,256]{1,0:T(8,128)(2,1)S(1)}, bf16[128,256]{1,0:T(8,128)(2,1)S(1)}, u32[]{:S(2)}, u32[]{:S(2)}) %collective-permute-start) | collective-permute-done | bytes 65568 | tf_op jit(solution)/shard_map/ppermute | solution.py:369
  47.7 2.4 %shard_map.80 = bf16[64,3,8,128]{3,2,1,0:T(8,128)(2,1)S(1)} custom-call(bf16[16,3,32,128]{3,2,1,0:T(8,128)(2,1)S(1)} %get-tuple-element.14.refs_0_, bf16[8,4,256,256]{3,2,1,0:T(8,128)(2,1)S(1)} %get-tuple-element.15.refs_1_, f32[128,256]{1,0:T(8,128)S(1)} %shard_map.79.refs_2_, bf16[128,256]{1,0:T(8,128)(2,1)S(1)} %collective-permute-done.refs_3_), custom_call_target="tpu_custom_call" | custom-call | tf_op jit(solution)/shard_map/pallas_call | solution.py:31
  50.1 16.0 %all_to_all.22.grads_ref = bf16[64,3,8,128]{3,2,1,0:T(8,128)(2,1)S(1)} all-to-all(bf16[64,3,8,128]{3,2,1,0:T(8,128)(2,1)S(1)} %shard_map.80), channel_id=1, replica_groups=mesh['x'=4,'u'=2,'w'=2,'c'=2,'y'=4,'h'=2] {'x','w','c','y'}, dimensions={0} | all-to-all | bytes 786432 | tf_op jit(solution)/shard_map/all_to_all | solution.py:300
  66.1 0.7 shard_map.81
  66.7 14.1 %all_to_all.23.parts_ref = bf16[8,8,1024]{2,1,0:T(8,128)(2,1)S(1)} all-to-all(bf16[8,8,1024]{2,1,0:T(8,128)(2,1)S(1)} %shard_map.81), channel_id=1, replica_groups=mesh['x'=4,'u'=2,'w'=2,'c'=2,'y'=4,'h'=2] {'y','h'}, dimensions={0} | all-to-all | bytes 262144 | tf_op jit(solution)/shard_map/all_to_all | solution.py:300
  80.9 0.0 copy-done
  80.9 0.0 copy-done.1
  80.9 0.0 copy-done.2
  80.9 1.2 %shard_map.82 = (f32[128,256]{1,0:T(8,128)}, f32[128,256]{1,0:T(8,128)}, f32[128,256]{1,0:T(8,128)}) custom-call(bf16[8,8,1024]{2,1,0:T(8,128)(2,1)S(1)} %all_to_all.23.parts_ref, f32[32,8,128]{2,1,0:T(8,128)S(1)} %get-tuple-element.18.probs_ref, f32[128,256]{1,0:T(8,128)S(1)} %copy-done, f32[128,256]{1,0:T(8,128)S(1)} %copy-done.1, f32[128,256]{1,0:T(8,128)S(1)} %copy-done.2), custom_call_target="tpu_custom_call" | custom-call | tf_op jit(solution)/shard_map/pallas_call | solution.py:31
Async XLA Ops:
  42.4 5.3 %collective-permute-start = (bf16[128,256]{1,0:T(8,128)(2,1)S(1)}, bf16[128,256]{1,0:T(8,128)(2,1)S(1)}, u32[]{:S(2)}, u32[]{:S(2)}) collective-permute-start(bf16[128,256]{1,0:T(8,128)(2,1)S(1)} %get-tuple-element.17), channel_id=1, source_target_pairs={{0,32},{32,0},{1,33},{33,1},{2,34},{34,2},{3,35},{35,3},{4,36},{36... | collective-permute-start | bytes 196616 | tf_op jit(solution)/shard_map/ppermute | solution.py:369
  43.5 37.4 %copy-start = (f32[128,256]{1,0:T(8,128)S(1)}, f32[128,256]{1,0:T(8,128)}, u32[]{:S(2)}) copy-start(f32[128,256]{1,0:T(8,128)} %logits_ref.1) | copy-start | bytes 393220
  43.5 37.4 %copy-start.1 = (f32[128,256]{1,0:T(8,128)S(1)}, f32[128,256]{1,0:T(8,128)}, u32[]{:S(2)}) copy-start(f32[128,256]{1,0:T(8,128)} %first_ref.1) | copy-start | bytes 393220
  43.5 37.4 %copy-start.2 = (f32[128,256]{1,0:T(8,128)S(1)}, f32[128,256]{1,0:T(8,128)}, u32[]{:S(2)}) copy-start(f32[128,256]{1,0:T(8,128)} %second_ref.1) | copy-start | bytes 393220

commit v12 on v11

--- a/solution.py
+++ b/solution.py
@@ -11,14 +11,15 @@
 NAMES = ("x", "u", "w", "c", "y", "h")
 ROW_AXES = ("x", "u", "w", "c")
 MARG_AXES = ("y", "h")
-PLACE_AXES = ("x", "w", "c")
-SHARE_AXES = ("x", "w", "c", "y")
+PLACE_AXES = ("c", "x", "w")
+SHARE_AXES = ("x", "w", "y")
+CORES = 2
 CHUNKS = 4
 CHUNK = 32
 LANES = CHUNKS * CHUNK
 SUB = V // CHUNKS
 MODS = 4
-MARGS = 16
+MARGS = 8
 VMEM = pl.BlockSpec(memory_space=pltpu.VMEM)
 SMEM = pl.BlockSpec(memory_space=pltpu.SMEM)
 ANY = pl.BlockSpec(memory_space=pl.ANY)
@@ -94,8 +95,12 @@
     triples_copy.wait()
     tile_ref[...] = jnp.zeros(tile_ref.shape, F32)
     tile_ref[0:3, 0 : triples_ref.shape[1]] = triples_ref[...].astype(F32)
+    both = tile_ref[...]
+    first_core = jnp.where(place_ref[0] < MARGS, 1.0, 0.0)
+    kept = both * first_core + pltpu.roll(both, LANES - MARGS, 1) * (1.0 - first_core)
+    kept = jnp.where(lax.broadcasted_iota(jnp.int32, kept.shape, 1) < MARGS, kept, 0.0)
     for half in range(halves):
-        tile = (tile_ref[...] * jnp.where(side_ref[0] == half, 1.0, 0.0)).astype(LOW)
+        tile = (kept * jnp.where(side_ref[0] == half, 1.0, 0.0)).astype(LOW)
         for chunk in range(CHUNKS):
             send_ref[chunk * halves + half, :, SUB * LANES :] = tile
 
@@ -107,37 +112,37 @@
     return jnp.where(row == attr, 1.0, 0.0).astype(LOW)
 
 
-def tile_rows(which, rest):
-    step = 3 * SUB
+def tile_rows(core, which, rest):
+    step = CORES * 3 * SUB
     for chunk in range(CHUNKS):
-        for start in range(0, MARGS, SUB):
-            rows = pl.ds((start * CHUNKS + chunk) * step + which * SUB + rest, SUB, stride=CHUNKS * step)
-            yield rows, chunk * MARGS + start
-
-
-def select_kernel(full_ref, send_ref, triples_ref, picked_ref):
+        rows = pl.ds(chunk * step + (core * 3 + which) * SUB + rest, MARGS, stride=CHUNKS * step)
+        yield rows, chunk * MARGS
+
+
+def select_kernel(full_ref, other_ref, send_ref, triples_ref, picked_ref):
     groups, attrs = full_ref.shape[0], full_ref.shape[1]
     halves = groups // CHUNKS
-    full = [full_ref[index].astype(F32) for index in range(groups)]
     triples = jnp.zeros(triples_ref.shape, F32)
     for chunk in range(CHUNKS):
-        tile = full[chunk * halves][:, SUB * LANES :]
-        for half in range(1, halves):
-            tile += full[chunk * halves + half][:, SUB * LANES :]
+        tile = jnp.zeros(triples_ref.shape, F32)
+        for half in range(halves):
+            tile += full_ref[chunk * halves + half, :, SUB * LANES :].astype(F32)
         triples += pltpu.roll(tile, chunk * MARGS, 1) if chunk else tile
     triples_ref[...] = triples
-    table = jnp.concatenate([value[:, 0 : SUB * LANES] for value in full], axis=0).astype(LOW)
-    for which in range(3):
-        mine = one_hot(triples, which, groups * attrs)
-        picked = lax.dot_general(mine, table, (((0,), (0,)), ((), ())), preferred_element_type=F32)
-        for rest in range(SUB):
-            for rows, place in tile_rows(which, rest):
-                picked_ref[rows, :] = picked[place : place + SUB, rest * LANES : (rest + 1) * LANES]
+    hots = [one_hot(triples, which, groups * attrs) for which in range(3)]
+    for core, table_ref in enumerate((full_ref, other_ref)):
+        parts = [table_ref[index].astype(F32)[:, 0 : SUB * LANES] for index in range(groups)]
+        table = jnp.concatenate(parts, axis=0).astype(LOW)
+        for which in range(3):
+            picked = lax.dot_general(hots[which], table, (((0,), (0,)), ((), ())), preferred_element_type=F32)
+            for rest in range(SUB):
+                for rows, place in tile_rows(core, which, rest):
+                    picked_ref[rows, :] = picked[place : place + MARGS, rest * LANES : (rest + 1) * LANES]
     send_ref[...] = picked_ref[...].reshape(send_ref.shape).astype(LOW)
 
 
-def unpack(src_ref, shard):
-    packed = [src_ref[shard * CHUNKS + chunk].astype(F32).reshape(3 * SUB, LANES) for chunk in range(CHUNKS)]
+def unpack(src_ref, place, core):
+    packed = [src_ref[place * CHUNKS + chunk, core].astype(F32).reshape(3 * SUB, LANES) for chunk in range(CHUNKS)]
     parts = exchange(packed)
     return [
         jnp.concatenate([part[which * SUB : (which + 1) * SUB, :] for part in parts], axis=0) for which in range(3)
@@ -150,7 +155,7 @@
     def fill(step):
         for part in range(2):
             shard = 2 * step + part
-            first, second, third = [value.astype(LOW) for value in unpack(src_ref, shard)]
+            first, second, third = [value.astype(LOW) for value in unpack(src_ref, step, part)]
             table_ref[shard, 0] = first
             table_ref[shard, 1] = second
             table_ref[shard, 2] = third
@@ -242,25 +247,35 @@
                 for part in range(CHUNKS)
             ]
             for chunk, packed in enumerate(exchange(parts)):
-                place = (2 * index + half) * CHUNKS + chunk
-                out_ref[place] = packed.reshape(3, SUB, LANES).astype(LOW)
+                out_ref[index * CHUNKS + chunk, half] = packed.reshape(3, SUB, LANES).astype(LOW)
         return carry
 
     lax.fori_loop(0, steps, step, 0, unroll=steps)
 
 
-def collect_kernel(triples_ref, grads_ref, send_ref, grad_ref):
+def collect_kernel(triples_ref, grads_ref, own_ref, other_ref, grad_ref):
+    attrs = own_ref.shape[0]
+    triples = triples_ref[...]
+    hots = [one_hot(triples, which, attrs) for which in range(3)]
+    grad_ref[...] = grads_ref[...].astype(F32).reshape(grad_ref.shape)
+    for core in range(CORES):
+        total = jnp.zeros(own_ref.shape, F32)
+        for which in range(3):
+            parts = []
+            for rest in range(SUB):
+                tiles = [grad_ref[rows, :] for rows, unused in tile_rows(core, which, rest)]
+                parts.append(jnp.concatenate(tiles, axis=0))
+            grads = jnp.concatenate(parts, axis=1).astype(LOW)
+            total += jnp.dot(hots[which], grads, preferred_element_type=F32)
+        if core == 0:
+            own_ref[...] = total
+        else:
+            other_ref[...] = total.astype(LOW)
+
+
+def join_kernel(own_ref, other_ref, send_ref):
     groups, attrs = send_ref.shape[0], send_ref.shape[1]
-    triples = triples_ref[...]
-    grad_ref[...] = grads_ref[...].astype(F32).reshape(grad_ref.shape)
-    total = jnp.zeros((groups * attrs, SUB * LANES), F32)
-    for which in range(3):
-        parts = []
-        for rest in range(SUB):
-            tiles = [grad_ref[rows, :] for rows, unused in tile_rows(which, rest)]
-            parts.append(jnp.concatenate(tiles, axis=0))
-        grads = jnp.concatenate(parts, axis=1).astype(LOW)
-        total += jnp.dot(one_hot(triples, which, groups * attrs), grads, preferred_element_type=F32)
+    total = own_ref[...] + other_ref[...].astype(F32)
     for index in range(groups):
         send_ref[index] = total[index * attrs : (index + 1) * attrs, :].astype(LOW)
 
@@ -300,9 +315,13 @@
     return lax.all_to_all(value, axes, 0, 0, tiled=True)
 
 
+def cross(value, axis):
+    return lax.ppermute(value, axis, [(0, 1), (1, 0)])
+
+
 def answers(src):
     shape = jax.ShapeDtypeStruct
-    shards = src.shape[0] // CHUNKS
+    shards = src.shape[0] // CHUNKS * CORES
     tall, wide = V * V // MODS, V * MODS
     return call(
         answer_kernel,
@@ -322,7 +341,7 @@
     tall, wide = V * V // MODS, V * MODS
     return call(
         lambda *refs: backward_kernel(scale, *refs),
-        jax.ShapeDtypeStruct((shards * CHUNKS, 3, SUB, LANES), LOW),
+        jax.ShapeDtypeStruct((shards // CORES * CHUNKS, CORES, 3, SUB, LANES), LOW),
         (table, pairs, base, other),
         [VMEM] * 4,
         [
@@ -358,15 +377,17 @@
         ],
     )
     full = swap(copies, MARG_AXES)
+    places = margs // CORES * CHUNKS
+    lines = places * CORES * 3 * SUB
     picked, attributes = call(
         select_kernel,
-        (shape((margs * CHUNKS, 3, SUB, LANES), LOW), shape((SUB, LANES), F32)),
-        (full,),
-        [VMEM],
-        [pltpu.VMEM((margs * CHUNKS * 3 * SUB, LANES), F32)],
+        (shape((places, CORES, 3, SUB, LANES), LOW), shape((SUB, LANES), F32)),
+        (full, cross(full, "c")),
+        [VMEM, VMEM],
+        [pltpu.VMEM((lines, LANES), F32)],
     )
     own, send, table, pairs = answers(swap(picked, SHARE_AXES))
-    other = lax.ppermute(send, "u", [(0, 1), (1, 0)])
+    other = cross(send, "u")
     base = call(
         lambda *refs: base_kernel(scale, *refs),
         shape((wide, tall), F32),
@@ -375,12 +396,15 @@
         [pltpu.VMEM((8, cells), F32), pltpu.VMEM((tall, wide), F32), pltpu.SemaphoreType.DMA],
     )
     returned = swap(backward(scale, table, pairs, base, other), SHARE_AXES)
-    totals = call(
+    kept, given = call(
         collect_kernel,
-        shape((groups, attrs, SUB * LANES), LOW),
+        (shape((groups * attrs, SUB * LANES), F32), shape((groups * attrs, SUB * LANES), LOW)),
         (attributes, returned),
         [VMEM, VMEM],
-        [pltpu.VMEM((margs * CHUNKS * 3 * SUB, LANES), F32)],
+        [pltpu.VMEM((lines, LANES), F32)],
+    )
+    totals = call(
+        join_kernel, shape((groups, attrs, SUB * LANES), LOW), (kept, cross(given, "c")), [VMEM, VMEM]
     )
     return call(
         adam_kernel,

time: 82.3 us -> 82.5 us (level)
  waiting for transfers between devices: 2.5 us -> 5.3 us
  blocking collectives: 68.2 us -> 65.4 us
    all_to_all x4, blocking collectives: 68.2 us -> 65.4 us  [swap(): return lax.all_to_all(value, axes, 0, 0, tiled=True)]
    ppermute x1 -> x3, waiting for transfers between devices: 2.5 us -> 5.3 us  [cross(): return lax.ppermute(value, axis, [(0, 1), (1, 0)])]
    pallas_call x7 -> x8, Pallas kernels: 9.53 us -> 9.73 us  [call(): pl.pallas_call(body, out_shape=out_shape, in_specs=specs, out_specs=jax.t...]
  transfers between devices with their start and end apart: 1 -> 3, of which waited for: 1 -> 3; matrix products, arithmetic and copies ran while one was open for 0% -> 0% of each run, Pallas kernels for 2% -> 2%
where the time goes in v12:
time: 82.5 us; the launch traced here: 82.3 us
  blocking collectives  65.4 us (79%)
  Pallas kernels  9.73 us (12%)
  waiting for transfers between devices  5.3 us (6%)
  starting transfers between devices  1.18 us (1%)
    all_to_all x4, blocking collectives, swap(): return lax.all_to_all(value, axes, 0, 0, tiled=True)  65.4 us
    pallas_call x8, Pallas kernels, call(): pl.pallas_call(body, out_shape=out_shape, in_specs=specs, out_specs=jax.t...  9.73 us
    ppermute x3, waiting for transfers between devices, cross(): return lax.ppermute(value, axis, [(0, 1), (1, 0)])  5.3 us
  transfers between devices with their start and end apart: 3, of which 3 were waited for; matrix products, arithmetic and copies ran while one was open for 0% of the time, Pallas kernels for 2%

profile of v12, /device:TPU:32, one launch (start us, length us, event | category | flops | bytes accessed | tf_op | source)
XLA Modules:
  0.0 82.3 jit_solution(8742367944350694958)
XLA Ops:
  0.6 1.4 %shard_map.76 = (f32[32,8,128]{2,1,0:T(8,128)S(1)}, bf16[8,8,1152]{2,1,0:T(8,128)(2,1)S(1)}) custom-call(s32[1]{0:T(128)} %bitcast.side_ref, s32[1]{0:T(128)} %bitcast.1.place_ref.refs_0_, s32[3,16]{1,0:T(4,128)} %bitcast.3, f32[128,256]{1,0:T(8,128)} %logits_ref.1), custom_call_target="tpu_custom_call" | custom-call | tf_op jit(solution)/shard_map/pallas_call | solution.py:32
  2.0 21.6 %all_to_all.20.full_ref = bf16[8,8,1152]{2,1,0:T(8,128)(2,1)S(1)} all-to-all(bf16[8,8,1152]{2,1,0:T(8,128)(2,1)S(1)} %get-tuple-element.13), channel_id=1, replica_groups=mesh['x'=4,'u'=2,'w'=2,'c'=2,'y'=4,'h'=2] {'y','h'}, dimensions={0} | all-to-all | bytes 294912 | tf_op jit(solution)/shard_map/all_to_all | solution.py:315
  23.7 0.0 collective-permute-start
  23.7 1.4 %collective-permute-done.other_ref = bf16[8,8,1152]{2,1,0:T(8,128)(2,1)S(1)} collective-permute-done((bf16[8,8,1152]{2,1,0:T(8,128)(2,1)S(1)}, bf16[8,8,1152]{2,1,0:T(8,128)(2,1)S(1)}, u32[]{:S(2)}, u32[]{:S(2)}) %collective-permute-start) | collective-permute-done | bytes 147488 | tf_op jit(solution)/shard_map/ppermute | solution.py:319
  25.0 0.7 shard_map.77
  25.8 15.7 %all_to_all.21.src_ref = bf16[32,2,3,8,128]{4,3,2,1,0:T(8,128)(2,1)S(1)} all-to-all(bf16[32,2,3,8,128]{4,3,2,1,0:T(8,128)(2,1)S(1)} %get-tuple-element.15), channel_id=1, replica_groups=mesh['x'=4,'u'=2,'w'=2,'c'=2,'y'=4,'h'=2] {'x','w','y'}, dimensions={0} | all-to-all | bytes 786432 | tf_op jit(solution)/shard_map/all_to_all | solution.py:315
  41.5 1.6 %shard_map.78 = (f32[128,256]{1,0:T(8,128)S(1)}, bf16[128,256]{1,0:T(8,128)(2,1)S(1)}, bf16[16,3,32,128]{3,2,1,0:T(8,128)(2,1)S(1)}, bf16[8,4,256,256]{3,2,1,0:T(8,128)(2,1)S(1)}) custom-call(bf16[32,2,3,8,128]{4,3,2,1,0:T(8,128)(2,1)S(1)} %all_to_all.21.src_ref), custom_call_target="tpu_custom_call" | custom-call | tf_op jit(solution)/shard_map/pallas_call | solution.py:32
  43.2 1.1 %collective-permute-start.1 = (bf16[128,256]{1,0:T(8,128)(2,1)S(1)}, bf16[128,256]{1,0:T(8,128)(2,1)S(1)}, u32[]{:S(2)}, u32[]{:S(2)}) collective-permute-start(bf16[128,256]{1,0:T(8,128)(2,1)S(1)} %get-tuple-element.19), channel_id=1, source_target_pairs={{0,32},{32,0},{1,33},{33,1},{2,34},{34,2},{3,35},{35,3},{4,36},{36... | collective-permute-start | bytes 196616 | tf_op jit(solution)/shard_map/ppermute | solution.py:319
  44.3 0.0 copy-start
  44.3 0.0 copy-start.1
  44.3 0.0 copy-start.2
  44.3 1.7 %shard_map.79.refs_2_ = f32[128,256]{1,0:T(8,128)S(1)} custom-call(s32[1]{0:T(128)} %bitcast.1.place_ref.refs_0_, f32[128,256]{1,0:T(8,128)S(1)} %get-tuple-element.18.refs_1_, f32[16,32768]{1,0:T(8,128)} %refs_2_.1), custom_call_target="tpu_custom_call" | custom-call | tf_op jit(solution)/shard_map/pallas_call | solution.py:32
  45.9 2.6 %collective-permute-done.1.refs_3_ = bf16[128,256]{1,0:T(8,128)(2,1)S(1)} collective-permute-done((bf16[128,256]{1,0:T(8,128)(2,1)S(1)}, bf16[128,256]{1,0:T(8,128)(2,1)S(1)}, u32[]{:S(2)}, u32[]{:S(2)}) %collective-permute-start.1) | collective-permute-done | bytes 65568 | tf_op jit(solution)/shard_map/ppermute | solution.py:319
  48.5 2.4 %shard_map.80 = bf16[32,2,3,8,128]{4,3,2,1,0:T(8,128)(2,1)S(1)} custom-call(bf16[16,3,32,128]{3,2,1,0:T(8,128)(2,1)S(1)} %get-tuple-element.16.refs_0_, bf16[8,4,256,256]{3,2,1,0:T(8,128)(2,1)S(1)} %get-tuple-element.17.refs_1_, f32[128,256]{1,0:T(8,128)S(1)} %shard_map.79.refs_2_, bf16[128,256]{1,0:T(8,128)(2,1)S(1)} %collective-permute-done.1.refs_3_), custom_call_target="tpu_custom_call" | custom-call | tf_op jit(solution)/shard_map/pallas_call | solution.py:32
  51.0 13.6 %all_to_all.22.grads_ref = bf16[32,2,3,8,128]{4,3,2,1,0:T(8,128)(2,1)S(1)} all-to-all(bf16[32,2,3,8,128]{4,3,2,1,0:T(8,128)(2,1)S(1)} %shard_map.80), channel_id=1, replica_groups=mesh['x'=4,'u'=2,'w'=2,'c'=2,'y'=4,'h'=2] {'x','w','y'}, dimensions={0} | all-to-all | bytes 786432 | tf_op jit(solution)/shard_map/all_to_all | solution.py:315
  64.6 0.7 shard_map.81
  65.3 0.1 collective-permute-start.2
  65.4 1.3 %collective-permute-done.2.other_ref = bf16[64,1024]{1,0:T(8,128)(2,1)S(1)} collective-permute-done((bf16[64,1024]{1,0:T(8,128)(2,1)S(1)}, bf16[64,1024]{1,0:T(8,128)(2,1)S(1)}, u32[]{:S(2)}, u32[]{:S(2)}) %collective-permute-start.2) | collective-permute-done | bytes 131104 | tf_op jit(solution)/shard_map/ppermute | solution.py:319
  66.7 14.4 %all_to_all.23.parts_ref = bf16[8,8,1024]{2,1,0:T(8,128)(2,1)S(1)} all-to-all(bf16[8,8,1024]{2,1,0:T(8,128)(2,1)S(1)} %shard_map.82), channel_id=1, replica_groups=mesh['x'=4,'u'=2,'w'=2,'c'=2,'y'=4,'h'=2] {'y','h'}, dimensions={0} | all-to-all | bytes 262144 | tf_op jit(solution)/shard_map/all_to_all | solution.py:315
  81.1 0.0 copy-done
  81.1 0.0 copy-done.1
  81.1 0.0 copy-done.2
  81.1 1.2 %shard_map.83 = (f32[128,256]{1,0:T(8,128)}, f32[128,256]{1,0:T(8,128)}, f32[128,256]{1,0:T(8,128)}) custom-call(bf16[8,8,1024]{2,1,0:T(8,128)(2,1)S(1)} %all_to_all.23.parts_ref, f32[32,8,128]{2,1,0:T(8,128)S(1)} %get-tuple-element.22.probs_ref, f32[128,256]{1,0:T(8,128)S(1)} %copy-done, f32[128,256]{1,0:T(8,128)S(1)} %copy-done.1, f32[128,256]{1,0:T(8,128)S(1)} %copy-done.2), custom_call_target="tpu_custom_call" | custom-call | tf_op jit(solution)/shard_map/pallas_call | solution.py:32
  (1 shorter events, 0.0 us)
Async XLA Ops:
  23.7 1.4 %collective-permute-start = (bf16[8,8,1152]{2,1,0:T(8,128)(2,1)S(1)}, bf16[8,8,1152]{2,1,0:T(8,128)(2,1)S(1)}, u32[]{:S(2)}, u32[]{:S(2)}) collective-permute-start(bf16[8,8,1152]{2,1,0:T(8,128)(2,1)S(1)} %all_to_all.20.full_ref), channel_id=1, source_target_pairs={{0,8},{8,0},{1,9},{9,1},{2,10},{10,2},{3,11},{11,3},{4,12},{12,4},... | collective-permute-start | bytes 442376 | tf_op jit(solution)/shard_map/ppermute | solution.py:319
  43.2 5.4 %collective-permute-start.1 = (bf16[128,256]{1,0:T(8,128)(2,1)S(1)}, bf16[128,256]{1,0:T(8,128)(2,1)S(1)}, u32[]{:S(2)}, u32[]{:S(2)}) collective-permute-start(bf16[128,256]{1,0:T(8,128)(2,1)S(1)} %get-tuple-element.19), channel_id=1, source_target_pairs={{0,32},{32,0},{1,33},{33,1},{2,34},{34,2},{3,35},{35,3},{4,36},{36... | collective-permute-start | bytes 196616 | tf_op jit(solution)/shard_map/ppermute | solution.py:319
  44.3 36.8 %copy-start = (f32[128,256]{1,0:T(8,128)S(1)}, f32[128,256]{1,0:T(8,128)}, u32[]{:S(2)}) copy-start(f32[128,256]{1,0:T(8,128)} %logits_ref.1) | copy-start | bytes 393220
  44.3 36.8 %copy-start.1 = (f32[128,256]{1,0:T(8,128)S(1)}, f32[128,256]{1,0:T(8,128)}, u32[]{:S(2)}) copy-start(f32[128,256]{1,0:T(8,128)} %first_ref.1) | copy-start | bytes 393220
  44.3 36.8 %copy-start.2 = (f32[128,256]{1,0:T(8,128)S(1)}, f32[128,256]{1,0:T(8,128)}, u32[]{:S(2)}) copy-start(f32[128,256]{1,0:T(8,128)} %second_ref.1) | copy-start | bytes 393220
  65.3 1.4 %collective-permute-start.2 = (bf16[64,1024]{1,0:T(8,128)(2,1)S(1)}, bf16[64,1024]{1,0:T(8,128)(2,1)S(1)}, u32[]{:S(2)}, u32[]{:S(2)}) collective-permute-start(bf16[64,1024]{1,0:T(8,128)(2,1)S(1)} %get-tuple-element.21), channel_id=1, source_target_pairs={{0,8},{8,0},{1,9},{9,1},{2,10},{10,2},{3,11},{11,3},{4,12},{12,4},... | collective-permute-start | bytes 393224 | tf_op jit(solution)/shard_map/ppermute | solution.py:319

commit v13 on v12

--- a/solution.py
+++ b/solution.py
@@ -112,16 +112,27 @@
     return jnp.where(row == attr, 1.0, 0.0).astype(LOW)
 
 
-def tile_rows(core, which, rest):
-    step = CORES * 3 * SUB
+def tile_rows(which, rest, gap):
     for chunk in range(CHUNKS):
-        rows = pl.ds(chunk * step + (core * 3 + which) * SUB + rest, MARGS, stride=CHUNKS * step)
+        rows = pl.ds(chunk * gap + which * SUB + rest, MARGS, stride=CHUNKS * gap)
         yield rows, chunk * MARGS
 
 
-def select_kernel(full_ref, other_ref, send_ref, triples_ref, picked_ref):
-    groups, attrs = full_ref.shape[0], full_ref.shape[1]
-    halves = groups // CHUNKS
+def pick(triples, table_ref, picked_ref):
+    groups, attrs = table_ref.shape[0], table_ref.shape[1]
+    parts = [table_ref[index].astype(F32)[:, 0 : SUB * LANES] for index in range(groups)]
+    table = jnp.concatenate(parts, axis=0).astype(LOW)
+    for which in range(3):
+        mine = one_hot(triples, which, groups * attrs)
+        picked = lax.dot_general(mine, table, (((0,), (0,)), ((), ())), preferred_element_type=F32)
+        for rest in range(SUB):
+            for rows, place in tile_rows(which, rest, 3 * SUB):
+                picked_ref[rows, :] = picked[place : place + MARGS, rest * LANES : (rest + 1) * LANES]
+    return picked_ref[...].reshape(CHUNKS * MARGS, 3, SUB, LANES).astype(LOW)
+
+
+def select_kernel(full_ref, mine_ref, triples_ref, picked_ref):
+    halves = full_ref.shape[0] // CHUNKS
     triples = jnp.zeros(triples_ref.shape, F32)
     for chunk in range(CHUNKS):
         tile = jnp.zeros(triples_ref.shape, F32)
@@ -129,16 +140,14 @@
             tile += full_ref[chunk * halves + half, :, SUB * LANES :].astype(F32)
         triples += pltpu.roll(tile, chunk * MARGS, 1) if chunk else tile
     triples_ref[...] = triples
-    hots = [one_hot(triples, which, groups * attrs) for which in range(3)]
-    for core, table_ref in enumerate((full_ref, other_ref)):
-        parts = [table_ref[index].astype(F32)[:, 0 : SUB * LANES] for index in range(groups)]
-        table = jnp.concatenate(parts, axis=0).astype(LOW)
-        for which in range(3):
-            picked = lax.dot_general(hots[which], table, (((0,), (0,)), ((), ())), preferred_element_type=F32)
-            for rest in range(SUB):
-                for rows, place in tile_rows(core, which, rest):
-                    picked_ref[rows, :] = picked[place : place + MARGS, rest * LANES : (rest + 1) * LANES]
-    send_ref[...] = picked_ref[...].reshape(send_ref.shape).astype(LOW)
+    mine_ref[...] = pick(triples, full_ref, picked_ref)
+
+
+def merge_kernel(triples_ref, mine_ref, other_ref, send_ref, picked_ref):
+    theirs = pick(triples_ref[...], other_ref, picked_ref)
+    for place in range(send_ref.shape[0]):
+        send_ref[place, 0] = mine_ref[place]
+        send_ref[place, 1] = theirs[place]
 
 
 def unpack(src_ref, place, core):
@@ -253,24 +262,19 @@
     lax.fori_loop(0, steps, step, 0, unroll=steps)
 
 
-def collect_kernel(triples_ref, grads_ref, own_ref, other_ref, grad_ref):
-    attrs = own_ref.shape[0]
+def collect_kernel(core, triples_ref, grads_ref, total_ref, grad_ref):
+    attrs = total_ref.shape[0]
     triples = triples_ref[...]
-    hots = [one_hot(triples, which, attrs) for which in range(3)]
-    grad_ref[...] = grads_ref[...].astype(F32).reshape(grad_ref.shape)
-    for core in range(CORES):
-        total = jnp.zeros(own_ref.shape, F32)
-        for which in range(3):
-            parts = []
-            for rest in range(SUB):
-                tiles = [grad_ref[rows, :] for rows, unused in tile_rows(core, which, rest)]
-                parts.append(jnp.concatenate(tiles, axis=0))
-            grads = jnp.concatenate(parts, axis=1).astype(LOW)
-            total += jnp.dot(hots[which], grads, preferred_element_type=F32)
-        if core == 0:
-            own_ref[...] = total
-        else:
-            other_ref[...] = total.astype(LOW)
+    grad_ref[...] = grads_ref[:, core].astype(F32).reshape(grad_ref.shape)
+    total = jnp.zeros(total_ref.shape, F32)
+    for which in range(3):
+        parts = []
+        for rest in range(SUB):
+            tiles = [grad_ref[rows, :] for rows, unused in tile_rows(which, rest, 3 * SUB)]
+            parts.append(jnp.concatenate(tiles, axis=0))
+        grads = jnp.concatenate(parts, axis=1).astype(LOW)
+        total += jnp.dot(one_hot(triples, which, attrs), grads, preferred_element_type=F32)
+    total_ref[...] = total.astype(total_ref.dtype)
 
 
 def join_kernel(own_ref, other_ref, send_ref):
@@ -378,13 +382,21 @@
     )
     full = swap(copies, MARG_AXES)
     places = margs // CORES * CHUNKS
-    lines = places * CORES * 3 * SUB
-    picked, attributes = call(
+    lines = [pltpu.VMEM((places * 3 * SUB, LANES), F32)]
+    other_full = cross(full, "c")
+    mine, attributes = call(
         select_kernel,
-        (shape((places, CORES, 3, SUB, LANES), LOW), shape((SUB, LANES), F32)),
-        (full, cross(full, "c")),
-        [VMEM, VMEM],
-        [pltpu.VMEM((lines, LANES), F32)],
+        (shape((places, 3, SUB, LANES), LOW), shape((SUB, LANES), F32)),
+        (full,),
+        [VMEM],
+        lines,
+    )
+    picked = call(
+        merge_kernel,
+        shape((places, CORES, 3, SUB, LANES), LOW),
+        (attributes, mine, other_full),
+        [VMEM] * 3,
+        lines,
     )
     own, send, table, pairs = answers(swap(picked, SHARE_AXES))
     other = cross(send, "u")
@@ -396,13 +408,16 @@
         [pltpu.VMEM((8, cells), F32), pltpu.VMEM((tall, wide), F32), pltpu.SemaphoreType.DMA],
     )
     returned = swap(backward(scale, table, pairs, base, other), SHARE_AXES)
-    kept, given = call(
-        collect_kernel,
-        (shape((groups * attrs, SUB * LANES), F32), shape((groups * attrs, SUB * LANES), LOW)),
-        (attributes, returned),
-        [VMEM, VMEM],
-        [pltpu.VMEM((lines, LANES), F32)],
-    )
+    given, kept = [
+        call(
+            lambda *refs, core=core: collect_kernel(core, *refs),
+            shape((groups * attrs, SUB * LANES), kind),
+            (attributes, returned),
+            [VMEM, VMEM],
+            lines,
+        )
+        for core, kind in ((1, LOW), (0, F32))
+    ]
     totals = call(
         join_kernel, shape((groups, attrs, SUB * LANES), LOW), (kept, cross(given, "c")), [VMEM, VMEM]
     )

time: 82.5 us -> 81.9 us (level)
  waiting for transfers between devices: 5.3 us -> 4.43 us
    ppermute x3, waiting for transfers between devices: 5.3 us -> 4.43 us  [cross(): return lax.ppermute(value, axis, [(0, 1), (1, 0)])]
    pallas_call x8 -> x10, Pallas kernels: 9.73 us -> 9.93 us  [call(): pl.pallas_call(body, out_shape=out_shape, in_specs=specs, out_specs=jax.t...]
  transfers between devices with their start and end apart: 3 -> 3, of which waited for: 3 -> 3; matrix products, arithmetic and copies ran while one was open for 0% -> 0% of each run, Pallas kernels for 2% -> 3%
where the time goes in v13:
time: 81.9 us; the launch traced here: 81.6 us
  blocking collectives  65.3 us (80%)
  Pallas kernels  9.93 us (12%)
  waiting for transfers between devices  4.43 us (5%)
  starting transfers between devices  1.18 us (1%)
    all_to_all x4, blocking collectives, swap(): return lax.all_to_all(value, axes, 0, 0, tiled=True)  65.3 us
    pallas_call x10, Pallas kernels, call(): pl.pallas_call(body, out_shape=out_shape, in_specs=specs, out_specs=jax.t...  9.93 us
    ppermute x3, waiting for transfers between devices, cross(): return lax.ppermute(value, axis, [(0, 1), (1, 0)])  4.43 us
  transfers between devices with their start and end apart: 3, of which 3 were waited for; matrix products, arithmetic and copies ran while one was open for 0% of the time, Pallas kernels for 3%

profile of v13, /device:TPU:32, one launch (start us, length us, event | category | flops | bytes accessed | tf_op | source)
XLA Modules:
  0.0 81.6 jit_solution(6220406464265051273)
XLA Ops:
  0.6 1.4 %shard_map.76 = (f32[32,8,128]{2,1,0:T(8,128)S(1)}, bf16[8,8,1152]{2,1,0:T(8,128)(2,1)S(1)}) custom-call(s32[1]{0:T(128)} %bitcast.side_ref, s32[1]{0:T(128)} %bitcast.1.place_ref.refs_0_, s32[3,16]{1,0:T(4,128)} %bitcast.3, f32[128,256]{1,0:T(8,128)} %logits_ref.1), custom_call_target="tpu_custom_call" | custom-call | tf_op jit(solution)/shard_map/pallas_call | solution.py:32
  2.0 21.6 %all_to_all.20.full_ref = bf16[8,8,1152]{2,1,0:T(8,128)(2,1)S(1)} all-to-all(bf16[8,8,1152]{2,1,0:T(8,128)(2,1)S(1)} %get-tuple-element.11), channel_id=1, replica_groups=mesh['x'=4,'u'=2,'w'=2,'c'=2,'y'=4,'h'=2] {'y','h'}, dimensions={0} | all-to-all | bytes 294912 | tf_op jit(solution)/shard_map/all_to_all | solution.py:319
  23.7 0.0 collective-permute-start
  23.7 0.5 shard_map.77
  24.2 0.9 %collective-permute-done.other_ref = bf16[8,8,1152]{2,1,0:T(8,128)(2,1)S(1)} collective-permute-done((bf16[8,8,1152]{2,1,0:T(8,128)(2,1)S(1)}, bf16[8,8,1152]{2,1,0:T(8,128)(2,1)S(1)}, u32[]{:S(2)}, u32[]{:S(2)}) %collective-permute-start) | collective-permute-done | bytes 147488 | tf_op jit(solution)/shard_map/ppermute | solution.py:323
  25.0 0.4 shard_map.78
  25.5 15.7 %all_to_all.21.src_ref = bf16[32,2,3,8,128]{4,3,2,1,0:T(8,128)(2,1)S(1)} all-to-all(bf16[32,2,3,8,128]{4,3,2,1,0:T(8,128)(2,1)S(1)} %shard_map.78), channel_id=1, replica_groups=mesh['x'=4,'u'=2,'w'=2,'c'=2,'y'=4,'h'=2] {'x','w','y'}, dimensions={0} | all-to-all | bytes 786432 | tf_op jit(solution)/shard_map/all_to_all | solution.py:319
  41.2 1.6 %shard_map.79 = (f32[128,256]{1,0:T(8,128)S(1)}, bf16[128,256]{1,0:T(8,128)(2,1)S(1)}, bf16[16,3,32,128]{3,2,1,0:T(8,128)(2,1)S(1)}, bf16[8,4,256,256]{3,2,1,0:T(8,128)(2,1)S(1)}) custom-call(bf16[32,2,3,8,128]{4,3,2,1,0:T(8,128)(2,1)S(1)} %all_to_all.21.src_ref), custom_call_target="tpu_custom_call" | custom-call | tf_op jit(solution)/shard_map/pallas_call | solution.py:32
  42.8 1.1 %collective-permute-start.1 = (bf16[128,256]{1,0:T(8,128)(2,1)S(1)}, bf16[128,256]{1,0:T(8,128)(2,1)S(1)}, u32[]{:S(2)}, u32[]{:S(2)}) collective-permute-start(bf16[128,256]{1,0:T(8,128)(2,1)S(1)} %get-tuple-element.17), channel_id=1, source_target_pairs={{0,32},{32,0},{1,33},{33,1},{2,34},{34,2},{3,35},{35,3},{4,36},{36... | collective-permute-start | bytes 196616 | tf_op jit(solution)/shard_map/ppermute | solution.py:323
  43.9 1.6 %shard_map.80.refs_2_ = f32[128,256]{1,0:T(8,128)S(1)} custom-call(s32[1]{0:T(128)} %bitcast.1.place_ref.refs_0_, f32[128,256]{1,0:T(8,128)S(1)} %get-tuple-element.16.refs_1_, f32[16,32768]{1,0:T(8,128)} %refs_2_.1), custom_call_target="tpu_custom_call" | custom-call | tf_op jit(solution)/shard_map/pallas_call | solution.py:32
  45.5 0.0 copy-start
  45.6 0.0 copy-start.1
  45.6 0.0 copy-start.2
  45.6 2.6 %collective-permute-done.1.refs_3_ = bf16[128,256]{1,0:T(8,128)(2,1)S(1)} collective-permute-done((bf16[128,256]{1,0:T(8,128)(2,1)S(1)}, bf16[128,256]{1,0:T(8,128)(2,1)S(1)}, u32[]{:S(2)}, u32[]{:S(2)}) %collective-permute-start.1) | collective-permute-done | bytes 65568 | tf_op jit(solution)/shard_map/ppermute | solution.py:323
  48.2 2.4 %shard_map.81 = bf16[32,2,3,8,128]{4,3,2,1,0:T(8,128)(2,1)S(1)} custom-call(bf16[16,3,32,128]{3,2,1,0:T(8,128)(2,1)S(1)} %get-tuple-element.14.refs_0_, bf16[8,4,256,256]{3,2,1,0:T(8,128)(2,1)S(1)} %get-tuple-element.15.refs_1_, f32[128,256]{1,0:T(8,128)S(1)} %shard_map.80.refs_2_, bf16[128,256]{1,0:T(8,128)(2,1)S(1)} %collective-permute-done.1.refs_3_), custom_call_target="tpu_custom_call" | custom-call | tf_op jit(solution)/shard_map/pallas_call | solution.py:32
  50.6 13.6 %all_to_all.22.refs_1_ = bf16[32,2,3,8,128]{4,3,2,1,0:T(8,128)(2,1)S(1)} all-to-all(bf16[32,2,3,8,128]{4,3,2,1,0:T(8,128)(2,1)S(1)} %shard_map.81), channel_id=1, replica_groups=mesh['x'=4,'u'=2,'w'=2,'c'=2,'y'=4,'h'=2] {'x','w','y'}, dimensions={0} | all-to-all | bytes 786432 | tf_op jit(solution)/shard_map/all_to_all | solution.py:319
  64.2 0.4 shard_map.83
  64.6 0.1 collective-permute-start.2
  64.7 0.4 shard_map.82.own_ref
  65.1 0.9 %collective-permute-done.2.other_ref = bf16[64,1024]{1,0:T(8,128)(2,1)S(1)} collective-permute-done((bf16[64,1024]{1,0:T(8,128)(2,1)S(1)}, bf16[64,1024]{1,0:T(8,128)(2,1)S(1)}, u32[]{:S(2)}, u32[]{:S(2)}) %collective-permute-start.2) | collective-permute-done | bytes 131104 | tf_op jit(solution)/shard_map/ppermute | solution.py:323
  66.1 14.4 %all_to_all.23.parts_ref = bf16[8,8,1024]{2,1,0:T(8,128)(2,1)S(1)} all-to-all(bf16[8,8,1024]{2,1,0:T(8,128)(2,1)S(1)} %shard_map.84), channel_id=1, replica_groups=mesh['x'=4,'u'=2,'w'=2,'c'=2,'y'=4,'h'=2] {'y','h'}, dimensions={0} | all-to-all | bytes 262144 | tf_op jit(solution)/shard_map/all_to_all | solution.py:319
  80.5 0.0 copy-done
  80.5 0.0 copy-done.1
  80.5 0.0 copy-done.2
  80.5 1.2 %shard_map.85 = (f32[128,256]{1,0:T(8,128)}, f32[128,256]{1,0:T(8,128)}, f32[128,256]{1,0:T(8,128)}) custom-call(bf16[8,8,1024]{2,1,0:T(8,128)(2,1)S(1)} %all_to_all.23.parts_ref, f32[32,8,128]{2,1,0:T(8,128)S(1)} %get-tuple-element.18.probs_ref, f32[128,256]{1,0:T(8,128)S(1)} %copy-done, f32[128,256]{1,0:T(8,128)S(1)} %copy-done.1, f32[128,256]{1,0:T(8,128)S(1)} %copy-done.2), custom_call_target="tpu_custom_call" | custom-call | tf_op jit(solution)/shard_map/pallas_call | solution.py:32
  (1 shorter events, 0.0 us)
Async XLA Ops:
  23.7 1.4 %collective-permute-start = (bf16[8,8,1152]{2,1,0:T(8,128)(2,1)S(1)}, bf16[8,8,1152]{2,1,0:T(8,128)(2,1)S(1)}, u32[]{:S(2)}, u32[]{:S(2)}) collective-permute-start(bf16[8,8,1152]{2,1,0:T(8,128)(2,1)S(1)} %all_to_all.20.full_ref), channel_id=1, source_target_pairs={{0,8},{8,0},{1,9},{9,1},{2,10},{10,2},{3,11},{11,3},{4,12},{12,4},... | collective-permute-start | bytes 442376 | tf_op jit(solution)/shard_map/ppermute | solution.py:323
  42.8 5.4 %collective-permute-start.1 = (bf16[128,256]{1,0:T(8,128)(2,1)S(1)}, bf16[128,256]{1,0:T(8,128)(2,1)S(1)}, u32[]{:S(2)}, u32[]{:S(2)}) collective-permute-start(bf16[128,256]{1,0:T(8,128)(2,1)S(1)} %get-tuple-element.17), channel_id=1, source_target_pairs={{0,32},{32,0},{1,33},{33,1},{2,34},{34,2},{3,35},{35,3},{4,36},{36... | collective-permute-start | bytes 196616 | tf_op jit(solution)/shard_map/ppermute | solution.py:323
  45.5 34.9 %copy-start = (f32[128,256]{1,0:T(8,128)S(1)}, f32[128,256]{1,0:T(8,128)}, u32[]{:S(2)}) copy-start(f32[128,256]{1,0:T(8,128)} %logits_ref.1) | copy-start | bytes 393220
  45.6 34.9 %copy-start.1 = (f32[128,256]{1,0:T(8,128)S(1)}, f32[128,256]{1,0:T(8,128)}, u32[]{:S(2)}) copy-start(f32[128,256]{1,0:T(8,128)} %first_ref.1) | copy-start | bytes 393220
  45.6 34.9 %copy-start.2 = (f32[128,256]{1,0:T(8,128)S(1)}, f32[128,256]{1,0:T(8,128)}, u32[]{:S(2)}) copy-start(f32[128,256]{1,0:T(8,128)} %second_ref.1) | copy-start | bytes 393220
  64.6 1.4 %collective-permute-start.2 = (bf16[64,1024]{1,0:T(8,128)(2,1)S(1)}, bf16[64,1024]{1,0:T(8,128)(2,1)S(1)}, u32[]{:S(2)}, u32[]{:S(2)}) collective-permute-start(bf16[64,1024]{1,0:T(8,128)(2,1)S(1)} %shard_map.83), channel_id=1, source_target_pairs={{0,8},{8,0},{1,9},{9,1},{2,10},{10,2},{3,11},{11,3},{4,12},{12,4},... | collective-permute-start | bytes 393224 | tf_op jit(solution)/shard_map/ppermute | solution.py:323

commit v14 on v13

--- a/solution.py
+++ b/solution.py
@@ -68,12 +68,19 @@
     flipped_ref,
     sems,
 ):
-    logits_copy = pltpu.make_async_copy(logits_hbm, logits_ref, sems.at[0])
-    triples_copy = pltpu.make_async_copy(triples_hbm, triples_ref, sems.at[1])
-    logits_copy.start()
+    span = logits_ref.shape[0] // 2
+    halves_of = [pl.ds(part * span, span) for part in range(2)]
+    copies = [
+        pltpu.make_async_copy(logits_hbm.at[rows, :], logits_ref.at[rows, :], sems.at[part])
+        for part, rows in enumerate(halves_of)
+    ]
+    triples_copy = pltpu.make_async_copy(triples_hbm, triples_ref, sems.at[2])
+    for copy in copies:
+        copy.start()
     triples_copy.start()
-    logits_copy.wait()
-    flipped_ref[...] = logits_ref[...].T
+    for copy, rows in zip(copies, halves_of):
+        copy.wait()
+        flipped_ref[:, rows] = logits_ref[rows, :].T
     attrs = probs_ref.shape[1]
     halves = send_ref.shape[0] // CHUNKS
     values = [flipped_ref[pl.ds(value, attrs, stride=V), :] for value in range(V)]
@@ -84,7 +91,8 @@
     total = expos[0]
     for expo in expos[1:]:
         total = total + expo
-    probs = [expo / total for expo in expos]
+    scale = 1.0 / total
+    probs = [expo * scale for expo in expos]
     for value in range(V):
         probs_ref[value] = probs[value]
     for rest in range(SUB):
@@ -308,9 +316,9 @@
     grad = grad_ref[...].T
     new_first = 0.9 * first_ref[...] + 0.1 * grad
     new_second = 0.999 * second_ref[...] + 0.001 * grad * grad
-    first_hat = new_first / (1.0 - 0.9**ADAM_STEP)
-    second_hat = new_second / (1.0 - 0.999**ADAM_STEP)
-    out_logits_ref[...] = logits_ref[...] - 0.5 * first_hat / (jnp.sqrt(second_hat) + 1e-08)
+    step = new_first * (0.5 / (1.0 - 0.9**ADAM_STEP))
+    second_hat = new_second * (1.0 / (1.0 - 0.999**ADAM_STEP))
+    out_logits_ref[...] = logits_ref[...] - step / (jnp.sqrt(second_hat) + 1e-08)
     out_first_ref[...] = new_first
     out_second_ref[...] = new_second
 
@@ -377,7 +385,7 @@
             pltpu.VMEM((3, margs), jnp.int32),
             pltpu.VMEM((rows, cols), F32),
             pltpu.VMEM((cols, rows), F32),
-            pltpu.SemaphoreType.DMA((2,)),
+            pltpu.SemaphoreType.DMA((3,)),
         ],
     )
     full = swap(copies, MARG_AXES)

time: 81.9 us -> 82.1 us (level)
  no operation moved by 1% of the time
where the time goes in v14:
time: 82.1 us; the launch traced here: 81.8 us
  blocking collectives  65.3 us (80%)
  Pallas kernels  10 us (12%)
  waiting for transfers between devices  4.43 us (5%)
  starting transfers between devices  1.18 us (1%)
    all_to_all x4, blocking collectives, swap(): return lax.all_to_all(value, axes, 0, 0, tiled=True)  65.3 us
    pallas_call x10, Pallas kernels, call(): pl.pallas_call(body, out_shape=out_shape, in_specs=specs, out_specs=jax.t...  10 us
    ppermute x3, waiting for transfers between devices, cross(): return lax.ppermute(value, axis, [(0, 1), (1, 0)])  4.43 us
  transfers between devices with their start and end apart: 3, of which 3 were waited for; matrix products, arithmetic and copies ran while one was open for 0% of the time, Pallas kernels for 3%

profile of v14, /device:TPU:32, one launch (start us, length us, event | category | flops | bytes accessed | tf_op | source)
XLA Modules:
  0.0 81.8 jit_solution(597478057767863729)
XLA Ops:
  0.6 1.5 %shard_map.76 = (f32[32,8,128]{2,1,0:T(8,128)S(1)}, bf16[8,8,1152]{2,1,0:T(8,128)(2,1)S(1)}) custom-call(s32[1]{0:T(128)} %bitcast.side_ref, s32[1]{0:T(128)} %bitcast.1.place_ref.refs_0_, s32[3,16]{1,0:T(4,128)} %bitcast.3, f32[128,256]{1,0:T(8,128)} %logits_ref.1), custom_call_target="tpu_custom_call" | custom-call | tf_op jit(solution)/shard_map/pallas_call | solution.py:32
  2.2 21.6 %all_to_all.20.full_ref = bf16[8,8,1152]{2,1,0:T(8,128)(2,1)S(1)} all-to-all(bf16[8,8,1152]{2,1,0:T(8,128)(2,1)S(1)} %get-tuple-element.11), channel_id=1, replica_groups=mesh['x'=4,'u'=2,'w'=2,'c'=2,'y'=4,'h'=2] {'y','h'}, dimensions={0} | all-to-all | bytes 294912 | tf_op jit(solution)/shard_map/all_to_all | solution.py:327
  23.8 0.0 collective-permute-start
  23.8 0.5 shard_map.77
  24.3 0.9 %collective-permute-done.other_ref = bf16[8,8,1152]{2,1,0:T(8,128)(2,1)S(1)} collective-permute-done((bf16[8,8,1152]{2,1,0:T(8,128)(2,1)S(1)}, bf16[8,8,1152]{2,1,0:T(8,128)(2,1)S(1)}, u32[]{:S(2)}, u32[]{:S(2)}) %collective-permute-start) | collective-permute-done | bytes 147488 | tf_op jit(solution)/shard_map/ppermute | solution.py:331
  25.2 0.4 shard_map.78
  25.6 15.7 %all_to_all.21.src_ref = bf16[32,2,3,8,128]{4,3,2,1,0:T(8,128)(2,1)S(1)} all-to-all(bf16[32,2,3,8,128]{4,3,2,1,0:T(8,128)(2,1)S(1)} %shard_map.78), channel_id=1, replica_groups=mesh['x'=4,'u'=2,'w'=2,'c'=2,'y'=4,'h'=2] {'x','w','y'}, dimensions={0} | all-to-all | bytes 786432 | tf_op jit(solution)/shard_map/all_to_all | solution.py:327
  41.3 1.6 %shard_map.79 = (f32[128,256]{1,0:T(8,128)S(1)}, bf16[128,256]{1,0:T(8,128)(2,1)S(1)}, bf16[16,3,32,128]{3,2,1,0:T(8,128)(2,1)S(1)}, bf16[8,4,256,256]{3,2,1,0:T(8,128)(2,1)S(1)}) custom-call(bf16[32,2,3,8,128]{4,3,2,1,0:T(8,128)(2,1)S(1)} %all_to_all.21.src_ref), custom_call_target="tpu_custom_call" | custom-call | tf_op jit(solution)/shard_map/pallas_call | solution.py:32
  43.0 1.1 %collective-permute-start.1 = (bf16[128,256]{1,0:T(8,128)(2,1)S(1)}, bf16[128,256]{1,0:T(8,128)(2,1)S(1)}, u32[]{:S(2)}, u32[]{:S(2)}) collective-permute-start(bf16[128,256]{1,0:T(8,128)(2,1)S(1)} %get-tuple-element.17), channel_id=1, source_target_pairs={{0,32},{32,0},{1,33},{33,1},{2,34},{34,2},{3,35},{35,3},{4,36},{36... | collective-permute-start | bytes 196616 | tf_op jit(solution)/shard_map/ppermute | solution.py:331
  44.1 1.6 %shard_map.80.refs_2_ = f32[128,256]{1,0:T(8,128)S(1)} custom-call(s32[1]{0:T(128)} %bitcast.1.place_ref.refs_0_, f32[128,256]{1,0:T(8,128)S(1)} %get-tuple-element.16.refs_1_, f32[16,32768]{1,0:T(8,128)} %refs_2_.1), custom_call_target="tpu_custom_call" | custom-call | tf_op jit(solution)/shard_map/pallas_call | solution.py:32
  45.7 0.0 copy-start
  45.7 0.0 copy-start.1
  45.7 0.0 copy-start.2
  45.7 2.6 %collective-permute-done.1.refs_3_ = bf16[128,256]{1,0:T(8,128)(2,1)S(1)} collective-permute-done((bf16[128,256]{1,0:T(8,128)(2,1)S(1)}, bf16[128,256]{1,0:T(8,128)(2,1)S(1)}, u32[]{:S(2)}, u32[]{:S(2)}) %collective-permute-start.1) | collective-permute-done | bytes 65568 | tf_op jit(solution)/shard_map/ppermute | solution.py:331
  48.3 2.4 %shard_map.81 = bf16[32,2,3,8,128]{4,3,2,1,0:T(8,128)(2,1)S(1)} custom-call(bf16[16,3,32,128]{3,2,1,0:T(8,128)(2,1)S(1)} %get-tuple-element.14.refs_0_, bf16[8,4,256,256]{3,2,1,0:T(8,128)(2,1)S(1)} %get-tuple-element.15.refs_1_, f32[128,256]{1,0:T(8,128)S(1)} %shard_map.80.refs_2_, bf16[128,256]{1,0:T(8,128)(2,1)S(1)} %collective-permute-done.1.refs_3_), custom_call_target="tpu_custom_call" | custom-call | tf_op jit(solution)/shard_map/pallas_call | solution.py:32
  50.7 13.6 %all_to_all.22.refs_1_ = bf16[32,2,3,8,128]{4,3,2,1,0:T(8,128)(2,1)S(1)} all-to-all(bf16[32,2,3,8,128]{4,3,2,1,0:T(8,128)(2,1)S(1)} %shard_map.81), channel_id=1, replica_groups=mesh['x'=4,'u'=2,'w'=2,'c'=2,'y'=4,'h'=2] {'x','w','y'}, dimensions={0} | all-to-all | bytes 786432 | tf_op jit(solution)/shard_map/all_to_all | solution.py:327
  64.4 0.4 shard_map.83
  64.8 0.1 collective-permute-start.2
  64.9 0.4 shard_map.82.own_ref
  65.3 0.9 %collective-permute-done.2.other_ref = bf16[64,1024]{1,0:T(8,128)(2,1)S(1)} collective-permute-done((bf16[64,1024]{1,0:T(8,128)(2,1)S(1)}, bf16[64,1024]{1,0:T(8,128)(2,1)S(1)}, u32[]{:S(2)}, u32[]{:S(2)}) %collective-permute-start.2) | collective-permute-done | bytes 131104 | tf_op jit(solution)/shard_map/ppermute | solution.py:331
  66.2 14.4 %all_to_all.23.parts_ref = bf16[8,8,1024]{2,1,0:T(8,128)(2,1)S(1)} all-to-all(bf16[8,8,1024]{2,1,0:T(8,128)(2,1)S(1)} %shard_map.84), channel_id=1, replica_groups=mesh['x'=4,'u'=2,'w'=2,'c'=2,'y'=4,'h'=2] {'y','h'}, dimensions={0} | all-to-all | bytes 262144 | tf_op jit(solution)/shard_map/all_to_all | solution.py:327
  80.6 0.0 copy-done
  80.6 0.0 copy-done.1
  80.6 0.0 copy-done.2
  80.6 1.2 %shard_map.85 = (f32[128,256]{1,0:T(8,128)}, f32[128,256]{1,0:T(8,128)}, f32[128,256]{1,0:T(8,128)}) custom-call(bf16[8,8,1024]{2,1,0:T(8,128)(2,1)S(1)} %all_to_all.23.parts_ref, f32[32,8,128]{2,1,0:T(8,128)S(1)} %get-tuple-element.18.probs_ref, f32[128,256]{1,0:T(8,128)S(1)} %copy-done, f32[128,256]{1,0:T(8,128)S(1)} %copy-done.1, f32[128,256]{1,0:T(8,128)S(1)} %copy-done.2), custom_call_target="tpu_custom_call" | custom-call | tf_op jit(solution)/shard_map/pallas_call | solution.py:32
  (1 shorter events, 0.0 us)
Async XLA Ops:
  23.8 1.4 %collective-permute-start = (bf16[8,8,1152]{2,1,0:T(8,128)(2,1)S(1)}, bf16[8,8,1152]{2,1,0:T(8,128)(2,1)S(1)}, u32[]{:S(2)}, u32[]{:S(2)}) collective-permute-start(bf16[8,8,1152]{2,1,0:T(8,128)(2,1)S(1)} %all_to_all.20.full_ref), channel_id=1, source_target_pairs={{0,8},{8,0},{1,9},{9,1},{2,10},{10,2},{3,11},{11,3},{4,12},{12,4},... | collective-permute-start | bytes 442376 | tf_op jit(solution)/shard_map/ppermute | solution.py:331
  43.0 5.4 %collective-permute-start.1 = (bf16[128,256]{1,0:T(8,128)(2,1)S(1)}, bf16[128,256]{1,0:T(8,128)(2,1)S(1)}, u32[]{:S(2)}, u32[]{:S(2)}) collective-permute-start(bf16[128,256]{1,0:T(8,128)(2,1)S(1)} %get-tuple-element.17), channel_id=1, source_target_pairs={{0,32},{32,0},{1,33},{33,1},{2,34},{34,2},{3,35},{35,3},{4,36},{36... | collective-permute-start | bytes 196616 | tf_op jit(solution)/shard_map/ppermute | solution.py:331
  45.7 34.9 %copy-start = (f32[128,256]{1,0:T(8,128)S(1)}, f32[128,256]{1,0:T(8,128)}, u32[]{:S(2)}) copy-start(f32[128,256]{1,0:T(8,128)} %logits_ref.1) | copy-start | bytes 393220
  45.7 34.9 %copy-start.1 = (f32[128,256]{1,0:T(8,128)S(1)}, f32[128,256]{1,0:T(8,128)}, u32[]{:S(2)}) copy-start(f32[128,256]{1,0:T(8,128)} %first_ref.1) | copy-start | bytes 393220
  45.7 34.9 %copy-start.2 = (f32[128,256]{1,0:T(8,128)S(1)}, f32[128,256]{1,0:T(8,128)}, u32[]{:S(2)}) copy-start(f32[128,256]{1,0:T(8,128)} %second_ref.1) | copy-start | bytes 393220
  64.8 1.4 %collective-permute-start.2 = (bf16[64,1024]{1,0:T(8,128)(2,1)S(1)}, bf16[64,1024]{1,0:T(8,128)(2,1)S(1)}, u32[]{:S(2)}, u32[]{:S(2)}) collective-permute-start(bf16[64,1024]{1,0:T(8,128)(2,1)S(1)} %shard_map.83), channel_id=1, source_target_pairs={{0,8},{8,0},{1,9},{9,1},{2,10},{10,2},{3,11},{11,3},{4,12},{12,4},... | collective-permute-start | bytes 393224 | tf_op jit(solution)/shard_map/ppermute | solution.py:331

commit v15 on v14

--- a/solution.py
+++ b/solution.py
@@ -68,21 +68,25 @@
     flipped_ref,
     sems,
 ):
-    span = logits_ref.shape[0] // 2
-    halves_of = [pl.ds(part * span, span) for part in range(2)]
-    copies = [
-        pltpu.make_async_copy(logits_hbm.at[rows, :], logits_ref.at[rows, :], sems.at[part])
-        for part, rows in enumerate(halves_of)
-    ]
-    triples_copy = pltpu.make_async_copy(triples_hbm, triples_ref, sems.at[2])
-    for copy in copies:
-        copy.start()
+    logits_copy = pltpu.make_async_copy(logits_hbm, logits_ref, sems.at[0])
+    triples_copy = pltpu.make_async_copy(triples_hbm, triples_ref, sems.at[1])
     triples_copy.start()
-    for copy, rows in zip(copies, halves_of):
-        copy.wait()
-        flipped_ref[:, rows] = logits_ref[rows, :].T
+    logits_copy.start()
     attrs = probs_ref.shape[1]
     halves = send_ref.shape[0] // CHUNKS
+    triples_copy.wait()
+    tile_ref[...] = jnp.zeros(tile_ref.shape, F32)
+    tile_ref[0:3, 0 : triples_ref.shape[1]] = triples_ref[...].astype(F32)
+    both = tile_ref[...]
+    first_core = jnp.where(place_ref[0] < MARGS, 1.0, 0.0)
+    kept = both * first_core + pltpu.roll(both, LANES - MARGS, 1) * (1.0 - first_core)
+    kept = jnp.where(lax.broadcasted_iota(jnp.int32, kept.shape, 1) < MARGS, kept, 0.0)
+    for half in range(halves):
+        tile = (kept * jnp.where(side_ref[0] == half, 1.0, 0.0)).astype(LOW)
+        for chunk in range(CHUNKS):
+            send_ref[chunk * halves + half, :, SUB * LANES :] = tile
+    logits_copy.wait()
+    flipped_ref[...] = logits_ref[...].T
     values = [flipped_ref[pl.ds(value, attrs, stride=V), :] for value in range(V)]
     top = values[0]
     for value in values[1:]:
@@ -100,17 +104,6 @@
             low = packed.astype(LOW)
             for half in range(halves):
                 send_ref[chunk * halves + half, :, rest * LANES : (rest + 1) * LANES] = low
-    triples_copy.wait()
-    tile_ref[...] = jnp.zeros(tile_ref.shape, F32)
-    tile_ref[0:3, 0 : triples_ref.shape[1]] = triples_ref[...].astype(F32)
-    both = tile_ref[...]
-    first_core = jnp.where(place_ref[0] < MARGS, 1.0, 0.0)
-    kept = both * first_core + pltpu.roll(both, LANES - MARGS, 1) * (1.0 - first_core)
-    kept = jnp.where(lax.broadcasted_iota(jnp.int32, kept.shape, 1) < MARGS, kept, 0.0)
-    for half in range(halves):
-        tile = (kept * jnp.where(side_ref[0] == half, 1.0, 0.0)).astype(LOW)
-        for chunk in range(CHUNKS):
-            send_ref[chunk * halves + half, :, SUB * LANES :] = tile
 
 
 def one_hot(triples, which, count):
@@ -385,7 +378,7 @@
             pltpu.VMEM((3, margs), jnp.int32),
             pltpu.VMEM((rows, cols), F32),
             pltpu.VMEM((cols, rows), F32),
-            pltpu.SemaphoreType.DMA((3,)),
+            pltpu.SemaphoreType.DMA((2,)),
         ],
     )
     full = swap(copies, MARG_AXES)

time: 82.1 us -> 81.8 us (level)
  no operation moved by 1% of the time
where the time goes in v15:
time: 81.8 us; the launch traced here: 81.6 us
  blocking collectives  65.3 us (80%)
  Pallas kernels  9.85 us (12%)
  waiting for transfers between devices  4.43 us (5%)
  starting transfers between devices  1.18 us (1%)
    all_to_all x4, blocking collectives, swap(): return lax.all_to_all(value, axes, 0, 0, tiled=True)  65.3 us
    pallas_call x10, Pallas kernels, call(): pl.pallas_call(body, out_shape=out_shape, in_specs=specs, out_specs=jax.t...  9.85 us
    ppermute x3, waiting for transfers between devices, cross(): return lax.ppermute(value, axis, [(0, 1), (1, 0)])  4.43 us
  transfers between devices with their start and end apart: 3, of which 3 were waited for; matrix products, arithmetic and copies ran while one was open for 0% of the time, Pallas kernels for 3%

profile of v15, /device:TPU:32, one launch (start us, length us, event | category | flops | bytes accessed | tf_op | source)
XLA Modules:
  0.0 81.6 jit_solution(6554108907368576217)
XLA Ops:
  0.6 1.3 %shard_map.76 = (f32[32,8,128]{2,1,0:T(8,128)S(1)}, bf16[8,8,1152]{2,1,0:T(8,128)(2,1)S(1)}) custom-call(s32[1]{0:T(128)} %bitcast.side_ref, s32[1]{0:T(128)} %bitcast.1.place_ref.refs_0_, s32[3,16]{1,0:T(4,128)} %bitcast.3, f32[128,256]{1,0:T(8,128)} %logits_ref.1), custom_call_target="tpu_custom_call" | custom-call | tf_op jit(solution)/shard_map/pallas_call | solution.py:32
  2.0 21.6 %all_to_all.20.full_ref = bf16[8,8,1152]{2,1,0:T(8,128)(2,1)S(1)} all-to-all(bf16[8,8,1152]{2,1,0:T(8,128)(2,1)S(1)} %get-tuple-element.11), channel_id=1, replica_groups=mesh['x'=4,'u'=2,'w'=2,'c'=2,'y'=4,'h'=2] {'y','h'}, dimensions={0} | all-to-all | bytes 294912 | tf_op jit(solution)/shard_map/all_to_all | solution.py:320
  23.6 0.0 collective-permute-start
  23.6 0.5 shard_map.77
  24.1 0.9 %collective-permute-done.other_ref = bf16[8,8,1152]{2,1,0:T(8,128)(2,1)S(1)} collective-permute-done((bf16[8,8,1152]{2,1,0:T(8,128)(2,1)S(1)}, bf16[8,8,1152]{2,1,0:T(8,128)(2,1)S(1)}, u32[]{:S(2)}, u32[]{:S(2)}) %collective-permute-start) | collective-permute-done | bytes 147488 | tf_op jit(solution)/shard_map/ppermute | solution.py:324
  25.0 0.4 shard_map.78
  25.4 15.7 %all_to_all.21.src_ref = bf16[32,2,3,8,128]{4,3,2,1,0:T(8,128)(2,1)S(1)} all-to-all(bf16[32,2,3,8,128]{4,3,2,1,0:T(8,128)(2,1)S(1)} %shard_map.78), channel_id=1, replica_groups=mesh['x'=4,'u'=2,'w'=2,'c'=2,'y'=4,'h'=2] {'x','w','y'}, dimensions={0} | all-to-all | bytes 786432 | tf_op jit(solution)/shard_map/all_to_all | solution.py:320
  41.1 1.6 %shard_map.79 = (f32[128,256]{1,0:T(8,128)S(1)}, bf16[128,256]{1,0:T(8,128)(2,1)S(1)}, bf16[16,3,32,128]{3,2,1,0:T(8,128)(2,1)S(1)}, bf16[8,4,256,256]{3,2,1,0:T(8,128)(2,1)S(1)}) custom-call(bf16[32,2,3,8,128]{4,3,2,1,0:T(8,128)(2,1)S(1)} %all_to_all.21.src_ref), custom_call_target="tpu_custom_call" | custom-call | tf_op jit(solution)/shard_map/pallas_call | solution.py:32
  42.8 1.1 %collective-permute-start.1 = (bf16[128,256]{1,0:T(8,128)(2,1)S(1)}, bf16[128,256]{1,0:T(8,128)(2,1)S(1)}, u32[]{:S(2)}, u32[]{:S(2)}) collective-permute-start(bf16[128,256]{1,0:T(8,128)(2,1)S(1)} %get-tuple-element.17), channel_id=1, source_target_pairs={{0,32},{32,0},{1,33},{33,1},{2,34},{34,2},{3,35},{35,3},{4,36},{36... | collective-permute-start | bytes 196616 | tf_op jit(solution)/shard_map/ppermute | solution.py:324
  43.9 1.6 %shard_map.80.refs_2_ = f32[128,256]{1,0:T(8,128)S(1)} custom-call(s32[1]{0:T(128)} %bitcast.1.place_ref.refs_0_, f32[128,256]{1,0:T(8,128)S(1)} %get-tuple-element.16.refs_1_, f32[16,32768]{1,0:T(8,128)} %refs_2_.1), custom_call_target="tpu_custom_call" | custom-call | tf_op jit(solution)/shard_map/pallas_call | solution.py:32
  45.5 0.0 copy-start
  45.5 0.0 copy-start.1
  45.5 0.0 copy-start.2
  45.5 2.6 %collective-permute-done.1.refs_3_ = bf16[128,256]{1,0:T(8,128)(2,1)S(1)} collective-permute-done((bf16[128,256]{1,0:T(8,128)(2,1)S(1)}, bf16[128,256]{1,0:T(8,128)(2,1)S(1)}, u32[]{:S(2)}, u32[]{:S(2)}) %collective-permute-start.1) | collective-permute-done | bytes 65568 | tf_op jit(solution)/shard_map/ppermute | solution.py:324
  48.1 2.4 %shard_map.81 = bf16[32,2,3,8,128]{4,3,2,1,0:T(8,128)(2,1)S(1)} custom-call(bf16[16,3,32,128]{3,2,1,0:T(8,128)(2,1)S(1)} %get-tuple-element.14.refs_0_, bf16[8,4,256,256]{3,2,1,0:T(8,128)(2,1)S(1)} %get-tuple-element.15.refs_1_, f32[128,256]{1,0:T(8,128)S(1)} %shard_map.80.refs_2_, bf16[128,256]{1,0:T(8,128)(2,1)S(1)} %collective-permute-done.1.refs_3_), custom_call_target="tpu_custom_call" | custom-call | tf_op jit(solution)/shard_map/pallas_call | solution.py:32
  50.5 13.6 %all_to_all.22.refs_1_ = bf16[32,2,3,8,128]{4,3,2,1,0:T(8,128)(2,1)S(1)} all-to-all(bf16[32,2,3,8,128]{4,3,2,1,0:T(8,128)(2,1)S(1)} %shard_map.81), channel_id=1, replica_groups=mesh['x'=4,'u'=2,'w'=2,'c'=2,'y'=4,'h'=2] {'x','w','y'}, dimensions={0} | all-to-all | bytes 786432 | tf_op jit(solution)/shard_map/all_to_all | solution.py:320
  64.2 0.4 shard_map.83
  64.6 0.1 collective-permute-start.2
  64.7 0.4 shard_map.82.own_ref
  65.1 0.9 %collective-permute-done.2.other_ref = bf16[64,1024]{1,0:T(8,128)(2,1)S(1)} collective-permute-done((bf16[64,1024]{1,0:T(8,128)(2,1)S(1)}, bf16[64,1024]{1,0:T(8,128)(2,1)S(1)}, u32[]{:S(2)}, u32[]{:S(2)}) %collective-permute-start.2) | collective-permute-done | bytes 131104 | tf_op jit(solution)/shard_map/ppermute | solution.py:324
  66.0 14.4 %all_to_all.23.parts_ref = bf16[8,8,1024]{2,1,0:T(8,128)(2,1)S(1)} all-to-all(bf16[8,8,1024]{2,1,0:T(8,128)(2,1)S(1)} %shard_map.84), channel_id=1, replica_groups=mesh['x'=4,'u'=2,'w'=2,'c'=2,'y'=4,'h'=2] {'y','h'}, dimensions={0} | all-to-all | bytes 262144 | tf_op jit(solution)/shard_map/all_to_all | solution.py:320
  80.4 0.0 copy-done
  80.4 0.0 copy-done.1
  80.4 0.0 copy-done.2
  80.4 1.2 %shard_map.85 = (f32[128,256]{1,0:T(8,128)}, f32[128,256]{1,0:T(8,128)}, f32[128,256]{1,0:T(8,128)}) custom-call(bf16[8,8,1024]{2,1,0:T(8,128)(2,1)S(1)} %all_to_all.23.parts_ref, f32[32,8,128]{2,1,0:T(8,128)S(1)} %get-tuple-element.18.probs_ref, f32[128,256]{1,0:T(8,128)S(1)} %copy-done, f32[128,256]{1,0:T(8,128)S(1)} %copy-done.1, f32[128,256]{1,0:T(8,128)S(1)} %copy-done.2), custom_call_target="tpu_custom_call" | custom-call | tf_op jit(solution)/shard_map/pallas_call | solution.py:32
  (1 shorter events, 0.0 us)
Async XLA Ops:
  23.6 1.4 %collective-permute-start = (bf16[8,8,1152]{2,1,0:T(8,128)(2,1)S(1)}, bf16[8,8,1152]{2,1,0:T(8,128)(2,1)S(1)}, u32[]{:S(2)}, u32[]{:S(2)}) collective-permute-start(bf16[8,8,1152]{2,1,0:T(8,128)(2,1)S(1)} %all_to_all.20.full_ref), channel_id=1, source_target_pairs={{0,8},{8,0},{1,9},{9,1},{2,10},{10,2},{3,11},{11,3},{4,12},{12,4},... | collective-permute-start | bytes 442376 | tf_op jit(solution)/shard_map/ppermute | solution.py:324
  42.8 5.4 %collective-permute-start.1 = (bf16[128,256]{1,0:T(8,128)(2,1)S(1)}, bf16[128,256]{1,0:T(8,128)(2,1)S(1)}, u32[]{:S(2)}, u32[]{:S(2)}) collective-permute-start(bf16[128,256]{1,0:T(8,128)(2,1)S(1)} %get-tuple-element.17), channel_id=1, source_target_pairs={{0,32},{32,0},{1,33},{33,1},{2,34},{34,2},{3,35},{35,3},{4,36},{36... | collective-permute-start | bytes 196616 | tf_op jit(solution)/shard_map/ppermute | solution.py:324
  45.5 34.9 %copy-start = (f32[128,256]{1,0:T(8,128)S(1)}, f32[128,256]{1,0:T(8,128)}, u32[]{:S(2)}) copy-start(f32[128,256]{1,0:T(8,128)} %logits_ref.1) | copy-start | bytes 393220
  45.5 34.9 %copy-start.1 = (f32[128,256]{1,0:T(8,128)S(1)}, f32[128,256]{1,0:T(8,128)}, u32[]{:S(2)}) copy-start(f32[128,256]{1,0:T(8,128)} %first_ref.1) | copy-start | bytes 393220
  45.5 34.9 %copy-start.2 = (f32[128,256]{1,0:T(8,128)S(1)}, f32[128,256]{1,0:T(8,128)}, u32[]{:S(2)}) copy-start(f32[128,256]{1,0:T(8,128)} %second_ref.1) | copy-start | bytes 393220
  64.6 1.4 %collective-permute-start.2 = (bf16[64,1024]{1,0:T(8,128)(2,1)S(1)}, bf16[64,1024]{1,0:T(8,128)(2,1)S(1)}, u32[]{:S(2)}, u32[]{:S(2)}) collective-permute-start(bf16[64,1024]{1,0:T(8,128)(2,1)S(1)} %shard_map.83), channel_id=1, source_target_pairs={{0,8},{8,0},{1,9},{9,1},{2,10},{10,2},{3,11},{11,3},{4,12},{12,4},... | collective-permute-start | bytes 393224 | tf_op jit(solution)/shard_map/ppermute | solution.py:324

commit v16 on v13

--- a/solution.py
+++ b/solution.py
@@ -105,10 +105,11 @@
             send_ref[chunk * halves + half, :, SUB * LANES :] = tile
 
 
-def one_hot(triples, which, count):
+def one_hot(triples, count):
     width = CHUNKS * MARGS
-    row = jnp.broadcast_to(triples[which : which + 1, 0:width], (count, width))
-    attr = lax.broadcasted_iota(jnp.int32, (count, width), 0).astype(F32)
+    row = jnp.concatenate([triples[which : which + 1, 0:width] for which in range(3)], axis=1)
+    row = jnp.broadcast_to(row, (count, 3 * width))
+    attr = lax.broadcasted_iota(jnp.int32, (count, 3 * width), 0).astype(F32)
     return jnp.where(row == attr, 1.0, 0.0).astype(LOW)
 
 
@@ -122,12 +123,13 @@
     groups, attrs = table_ref.shape[0], table_ref.shape[1]
     parts = [table_ref[index].astype(F32)[:, 0 : SUB * LANES] for index in range(groups)]
     table = jnp.concatenate(parts, axis=0).astype(LOW)
+    mine = one_hot(triples, groups * attrs)
+    picked = lax.dot_general(mine, table, (((0,), (0,)), ((), ())), preferred_element_type=F32)
     for which in range(3):
-        mine = one_hot(triples, which, groups * attrs)
-        picked = lax.dot_general(mine, table, (((0,), (0,)), ((), ())), preferred_element_type=F32)
         for rest in range(SUB):
             for rows, place in tile_rows(which, rest, 3 * SUB):
-                picked_ref[rows, :] = picked[place : place + MARGS, rest * LANES : (rest + 1) * LANES]
+                start = which * CHUNKS * MARGS + place
+                picked_ref[rows, :] = picked[start : start + MARGS, rest * LANES : (rest + 1) * LANES]
     return picked_ref[...].reshape(CHUNKS * MARGS, 3, SUB, LANES).astype(LOW)
 
 
@@ -266,14 +268,12 @@
     attrs = total_ref.shape[0]
     triples = triples_ref[...]
     grad_ref[...] = grads_ref[:, core].astype(F32).reshape(grad_ref.shape)
-    total = jnp.zeros(total_ref.shape, F32)
-    for which in range(3):
-        parts = []
-        for rest in range(SUB):
-            tiles = [grad_ref[rows, :] for rows, unused in tile_rows(which, rest, 3 * SUB)]
-            parts.append(jnp.concatenate(tiles, axis=0))
-        grads = jnp.concatenate(parts, axis=1).astype(LOW)
-        total += jnp.dot(one_hot(triples, which, attrs), grads, preferred_element_type=F32)
+    parts = []
+    for rest in range(SUB):
+        tiles = [grad_ref[rows, :] for which in range(3) for rows, unused in tile_rows(which, rest, 3 * SUB)]
+        parts.append(jnp.concatenate(tiles, axis=0))
+    grads = jnp.concatenate(parts, axis=1).astype(LOW)
+    total = jnp.dot(one_hot(triples, attrs), grads, preferred_element_type=F32)
     total_ref[...] = total.astype(total_ref.dtype)
 
 

time: 81.9 us -> 82 us (level)
  no operation moved by 1% of the time
where the time goes in v16:
time: 82 us; the launch traced here: 81.7 us
  blocking collectives  65.3 us (80%)
  Pallas kernels  9.99 us (12%)
  waiting for transfers between devices  4.39 us (5%)
  starting transfers between devices  1.18 us (1%)
    all_to_all x4, blocking collectives, swap(): return lax.all_to_all(value, axes, 0, 0, tiled=True)  65.3 us
    pallas_call x10, Pallas kernels, call(): pl.pallas_call(body, out_shape=out_shape, in_specs=specs, out_specs=jax.t...  9.99 us
    ppermute x3, waiting for transfers between devices, cross(): return lax.ppermute(value, axis, [(0, 1), (1, 0)])  4.39 us
  transfers between devices with their start and end apart: 3, of which 3 were waited for; matrix products, arithmetic and copies ran while one was open for 0% of the time, Pallas kernels for 3%

profile of v16, /device:TPU:32, one launch (start us, length us, event | category | flops | bytes accessed | tf_op | source)
XLA Modules:
  0.0 81.7 jit_solution(2861572729381026287)
XLA Ops:
  0.6 1.4 %shard_map.76 = (f32[32,8,128]{2,1,0:T(8,128)S(1)}, bf16[8,8,1152]{2,1,0:T(8,128)(2,1)S(1)}) custom-call(s32[1]{0:T(128)} %bitcast.side_ref, s32[1]{0:T(128)} %bitcast.1.place_ref.refs_0_, s32[3,16]{1,0:T(4,128)} %bitcast.3, f32[128,256]{1,0:T(8,128)} %logits_ref.1), custom_call_target="tpu_custom_call" | custom-call | tf_op jit(solution)/shard_map/pallas_call | solution.py:32
  2.0 21.6 %all_to_all.20.full_ref = bf16[8,8,1152]{2,1,0:T(8,128)(2,1)S(1)} all-to-all(bf16[8,8,1152]{2,1,0:T(8,128)(2,1)S(1)} %get-tuple-element.11), channel_id=1, replica_groups=mesh['x'=4,'u'=2,'w'=2,'c'=2,'y'=4,'h'=2] {'y','h'}, dimensions={0} | all-to-all | bytes 294912 | tf_op jit(solution)/shard_map/all_to_all | solution.py:319
  23.7 0.0 collective-permute-start
  23.7 0.6 shard_map.77
  24.2 0.8 collective-permute-done.other_ref
  25.0 0.5 shard_map.78
  25.5 15.7 %all_to_all.21.src_ref = bf16[32,2,3,8,128]{4,3,2,1,0:T(8,128)(2,1)S(1)} all-to-all(bf16[32,2,3,8,128]{4,3,2,1,0:T(8,128)(2,1)S(1)} %shard_map.78), channel_id=1, replica_groups=mesh['x'=4,'u'=2,'w'=2,'c'=2,'y'=4,'h'=2] {'x','w','y'}, dimensions={0} | all-to-all | bytes 786432 | tf_op jit(solution)/shard_map/all_to_all | solution.py:319
  41.3 1.6 %shard_map.79 = (f32[128,256]{1,0:T(8,128)S(1)}, bf16[128,256]{1,0:T(8,128)(2,1)S(1)}, bf16[16,3,32,128]{3,2,1,0:T(8,128)(2,1)S(1)}, bf16[8,4,256,256]{3,2,1,0:T(8,128)(2,1)S(1)}) custom-call(bf16[32,2,3,8,128]{4,3,2,1,0:T(8,128)(2,1)S(1)} %all_to_all.21.src_ref), custom_call_target="tpu_custom_call" | custom-call | tf_op jit(solution)/shard_map/pallas_call | solution.py:32
  42.9 1.1 %collective-permute-start.1 = (bf16[128,256]{1,0:T(8,128)(2,1)S(1)}, bf16[128,256]{1,0:T(8,128)(2,1)S(1)}, u32[]{:S(2)}, u32[]{:S(2)}) collective-permute-start(bf16[128,256]{1,0:T(8,128)(2,1)S(1)} %get-tuple-element.17), channel_id=1, source_target_pairs={{0,32},{32,0},{1,33},{33,1},{2,34},{34,2},{3,35},{35,3},{4,36},{36... | collective-permute-start | bytes 196616 | tf_op jit(solution)/shard_map/ppermute | solution.py:323
  44.0 1.6 %shard_map.80.refs_2_ = f32[128,256]{1,0:T(8,128)S(1)} custom-call(s32[1]{0:T(128)} %bitcast.1.place_ref.refs_0_, f32[128,256]{1,0:T(8,128)S(1)} %get-tuple-element.16.refs_1_, f32[16,32768]{1,0:T(8,128)} %refs_2_.1), custom_call_target="tpu_custom_call" | custom-call | tf_op jit(solution)/shard_map/pallas_call | solution.py:32
  45.6 0.0 copy-start
  45.6 0.0 copy-start.1
  45.6 0.0 copy-start.2
  45.7 2.6 %collective-permute-done.1.refs_3_ = bf16[128,256]{1,0:T(8,128)(2,1)S(1)} collective-permute-done((bf16[128,256]{1,0:T(8,128)(2,1)S(1)}, bf16[128,256]{1,0:T(8,128)(2,1)S(1)}, u32[]{:S(2)}, u32[]{:S(2)}) %collective-permute-start.1) | collective-permute-done | bytes 65568 | tf_op jit(solution)/shard_map/ppermute | solution.py:323
  48.3 2.4 %shard_map.81 = bf16[32,2,3,8,128]{4,3,2,1,0:T(8,128)(2,1)S(1)} custom-call(bf16[16,3,32,128]{3,2,1,0:T(8,128)(2,1)S(1)} %get-tuple-element.14.refs_0_, bf16[8,4,256,256]{3,2,1,0:T(8,128)(2,1)S(1)} %get-tuple-element.15.refs_1_, f32[128,256]{1,0:T(8,128)S(1)} %shard_map.80.refs_2_, bf16[128,256]{1,0:T(8,128)(2,1)S(1)} %collective-permute-done.1.refs_3_), custom_call_target="tpu_custom_call" | custom-call | tf_op jit(solution)/shard_map/pallas_call | solution.py:32
  50.7 13.6 %all_to_all.22.refs_1_ = bf16[32,2,3,8,128]{4,3,2,1,0:T(8,128)(2,1)S(1)} all-to-all(bf16[32,2,3,8,128]{4,3,2,1,0:T(8,128)(2,1)S(1)} %shard_map.81), channel_id=1, replica_groups=mesh['x'=4,'u'=2,'w'=2,'c'=2,'y'=4,'h'=2] {'x','w','y'}, dimensions={0} | all-to-all | bytes 786432 | tf_op jit(solution)/shard_map/all_to_all | solution.py:319
  64.3 0.4 shard_map.83
  64.7 0.1 collective-permute-start.2
  64.8 0.4 shard_map.82.own_ref
  65.1 1.0 %collective-permute-done.2.other_ref = bf16[64,1024]{1,0:T(8,128)(2,1)S(1)} collective-permute-done((bf16[64,1024]{1,0:T(8,128)(2,1)S(1)}, bf16[64,1024]{1,0:T(8,128)(2,1)S(1)}, u32[]{:S(2)}, u32[]{:S(2)}) %collective-permute-start.2) | collective-permute-done | bytes 131104 | tf_op jit(solution)/shard_map/ppermute | solution.py:323
  66.1 14.4 %all_to_all.23.parts_ref = bf16[8,8,1024]{2,1,0:T(8,128)(2,1)S(1)} all-to-all(bf16[8,8,1024]{2,1,0:T(8,128)(2,1)S(1)} %shard_map.84), channel_id=1, replica_groups=mesh['x'=4,'u'=2,'w'=2,'c'=2,'y'=4,'h'=2] {'y','h'}, dimensions={0} | all-to-all | bytes 262144 | tf_op jit(solution)/shard_map/all_to_all | solution.py:319
  80.5 0.0 copy-done
  80.5 0.0 copy-done.1
  80.5 0.0 copy-done.2
  80.5 1.2 %shard_map.85 = (f32[128,256]{1,0:T(8,128)}, f32[128,256]{1,0:T(8,128)}, f32[128,256]{1,0:T(8,128)}) custom-call(bf16[8,8,1024]{2,1,0:T(8,128)(2,1)S(1)} %all_to_all.23.parts_ref, f32[32,8,128]{2,1,0:T(8,128)S(1)} %get-tuple-element.18.probs_ref, f32[128,256]{1,0:T(8,128)S(1)} %copy-done, f32[128,256]{1,0:T(8,128)S(1)} %copy-done.1, f32[128,256]{1,0:T(8,128)S(1)} %copy-done.2), custom_call_target="tpu_custom_call" | custom-call | tf_op jit(solution)/shard_map/pallas_call | solution.py:32
  (1 shorter events, 0.0 us)
Async XLA Ops:
  23.7 1.4 %collective-permute-start = (bf16[8,8,1152]{2,1,0:T(8,128)(2,1)S(1)}, bf16[8,8,1152]{2,1,0:T(8,128)(2,1)S(1)}, u32[]{:S(2)}, u32[]{:S(2)}) collective-permute-start(bf16[8,8,1152]{2,1,0:T(8,128)(2,1)S(1)} %all_to_all.20.full_ref), channel_id=1, source_target_pairs={{0,8},{8,0},{1,9},{9,1},{2,10},{10,2},{3,11},{11,3},{4,12},{12,4},... | collective-permute-start | bytes 442376 | tf_op jit(solution)/shard_map/ppermute | solution.py:323
  42.9 5.4 %collective-permute-start.1 = (bf16[128,256]{1,0:T(8,128)(2,1)S(1)}, bf16[128,256]{1,0:T(8,128)(2,1)S(1)}, u32[]{:S(2)}, u32[]{:S(2)}) collective-permute-start(bf16[128,256]{1,0:T(8,128)(2,1)S(1)} %get-tuple-element.17), channel_id=1, source_target_pairs={{0,32},{32,0},{1,33},{33,1},{2,34},{34,2},{3,35},{35,3},{4,36},{36... | collective-permute-start | bytes 196616 | tf_op jit(solution)/shard_map/ppermute | solution.py:323
  45.6 34.9 %copy-start = (f32[128,256]{1,0:T(8,128)S(1)}, f32[128,256]{1,0:T(8,128)}, u32[]{:S(2)}) copy-start(f32[128,256]{1,0:T(8,128)} %logits_ref.1) | copy-start | bytes 393220
  45.6 34.9 %copy-start.1 = (f32[128,256]{1,0:T(8,128)S(1)}, f32[128,256]{1,0:T(8,128)}, u32[]{:S(2)}) copy-start(f32[128,256]{1,0:T(8,128)} %first_ref.1) | copy-start | bytes 393220
  45.6 34.9 %copy-start.2 = (f32[128,256]{1,0:T(8,128)S(1)}, f32[128,256]{1,0:T(8,128)}, u32[]{:S(2)}) copy-start(f32[128,256]{1,0:T(8,128)} %second_ref.1) | copy-start | bytes 393220
  64.7 1.4 %collective-permute-start.2 = (bf16[64,1024]{1,0:T(8,128)(2,1)S(1)}, bf16[64,1024]{1,0:T(8,128)(2,1)S(1)}, u32[]{:S(2)}, u32[]{:S(2)}) collective-permute-start(bf16[64,1024]{1,0:T(8,128)(2,1)S(1)} %shard_map.83), channel_id=1, source_target_pairs={{0,8},{8,0},{1,9},{9,1},{2,10},{10,2},{3,11},{11,3},{4,12},{12,4},... | collective-permute-start | bytes 393224 | tf_op jit(solution)/shard_map/ppermute | solution.py:323
